TPU v7x, 128 devices: a whole 4x4x4 slice. The times are simulated.
128 devices in a mesh: tm: 4 (over x_lo, core), cell: 32 (over z, y, x_hi).
Axes of the slice: x: 4 (x_hi: 2, x_lo: 2; x = x_hi * 2 + x_lo), y: 4, z: 4, core: 2. Of those that a mesh axis runs over, the one named last changes fastest.
Arguments:
- coords: float32 [4, 64, 16384], P('tm', None, 'cell'), may hold values from -8 to 8
- potentials: float32 [4, 16384], P('tm', 'cell'), may hold values from -6 to 202
Outputs:
- beliefs: float32 [4, 16384], P('tm', 'cell')
All inputs are finite; a program needn't handle non-finite values.
Results may differ from a plain program's by a relative error of at most 0.00011.
Values sent between devices are 32-bit elements; how exact they have to be, the bound alone decides.
No kernel may reach another device: no remote copies, remote signals or barrier semaphores. Data moves between devices by JAX's collectives and lax.ppermute only.
A program may use at most 64 MiB of HBM per device.

v0:
```python
import functools
import math

import jax
import jax.numpy as jnp
from jax import lax
from jax.experimental import pallas as pl
from jax.experimental.pallas import tpu as pltpu
from jax.sharding import PartitionSpec as P

LOG2E = math.log2(math.e)
LN2 = math.log(2.0)
LANES = 128
VMEM_LIMIT = 50 * 2**20

F32 = jnp.float32
BF16 = jnp.bfloat16

GROUPS = 4
PLACES = 16
SIDES = 2


def params():
    return pltpu.CompilerParams(vmem_limit_bytes=VMEM_LIMIT)


def halves(x):
    high = x.astype(BF16)
    return high, (x - high.astype(F32)).astype(BF16)


def bias_rows(first, w, n):
    w1 = w.astype(BF16).astype(F32)
    w2 = (w - w1).astype(BF16).astype(F32)
    w3 = w - w1 - w2
    row = lax.broadcasted_iota(jnp.int32, (16, n), 0)
    other = 3 - first
    block = jnp.where(row == first, w1, jnp.where(row == first + 1, w2, jnp.where(row == first + 2, w3, 0.0)))
    block = jnp.where((row >= other) & (row < other + 3), 1.0, block)
    return jnp.concatenate([block.astype(BF16), jnp.zeros((48, n), BF16)], axis=0)


def row_side(x, w):
    high, low = halves(x * (2.0 * LOG2E))
    return jnp.concatenate([high, high, low, bias_rows(3, w, x.shape[1])], axis=0)


def col_side(x, w):
    high, low = halves(x)
    return jnp.concatenate([high, low, high, bias_rows(0, w, x.shape[1])], axis=0)


def square(x):
    return jnp.sum(x * x, axis=0, keepdims=True)


def largest(parts):
    return functools.reduce(jnp.maximum, parts)


def added(parts):
    while len(parts) > 1:
        parts = [functools.reduce(jnp.add, parts[i : i + 2]) for i in range(0, len(parts), 2)]
    return parts[0]


def lse2(parts):
    top = largest(parts)
    return top + jnp.log2(added([jnp.exp2(p - top) for p in parts]))


def times(a, b):
    return lax.dot_general(a, b, (((1,), (0,)), ((), ())), preferred_element_type=F32)


def piped(count, start, finish):
    start(0)
    for k in range(count):
        if k + 1 < count:
            start(k + 1)
        finish(k)


def more(state, parts):
    best = largest(parts)
    if state is None:
        return best, added([jnp.exp2(p - best) for p in parts])
    top, total = state
    new = jnp.maximum(top, best)
    return new, total * jnp.exp2(top - new) + added([jnp.exp2(p - new) for p in parts])


def over_columns(rows_t, col_chunk, chunks, width, bufs, top, total):
    n = rows_t.shape[0]
    step = 32

    def start(k):
        bufs[k % 2][...] = times(rows_t, col_chunk(k))

    def finish(k):
        buf = bufs[k % 2]
        for r in range(0, n, step):
            at = slice(r, r + step)
            state = None if k == 0 else (top[at, :], total[at, :])
            a, b = more(state, [buf[at, i : i + LANES] for i in range(0, width, LANES)])
            top[at, :] = a
            total[at, :] = b

    piped(chunks, start, finish)
    a = jnp.transpose(top[...])
    b = jnp.transpose(total[...])
    best = jnp.max(a, axis=0, keepdims=True)
    return best + jnp.log2(jnp.sum(b * jnp.exp2(a - best), axis=0, keepdims=True))


def over_rows(rows_t, col_chunk, chunks, width, bufs):
    n = rows_t.shape[0]
    step = 8
    lines = []

    def start(k):
        bufs[k % 2][:, 0:width] = times(rows_t, col_chunk(k))

    def finish(k):
        buf = bufs[k % 2]
        for i in range(0, width, LANES):
            state = None
            for r in range(0, n, 32 * step):
                state = more(state, [buf[q : q + step, i : i + LANES] for q in range(r, r + 32 * step, step)])
            a, b = state
            best = jnp.max(a, axis=0, keepdims=True)
            lines.append(best + jnp.log2(jnp.sum(b * jnp.exp2(a - best), axis=0, keepdims=True)))

    piped(chunks, start, finish)
    return lines


def spread_kernel(place, own, own_pot, other, other_pot, out, target):
    core = place[1]
    _, dims, n = own.shape
    half = n // 2
    at = pl.multiple_of(core * half, half)
    x = jnp.where(core == 0, own[0, :, pl.ds(at, half)], other[0, :, pl.ds(at, half)])
    p = jnp.where(core == 0, own_pot[:, pl.ds(at, half)], other_pot[:, pl.ds(at, half)])
    for i in range(out.shape[0]):
        out[i, 0:dims, :] = x
        out[i, dims:, :] = jnp.broadcast_to(p, (8, half))
    target[0:dims, :] = jnp.where(core == 0, other[0], own[0])
    target[dims:, :] = jnp.broadcast_to(jnp.where(core == 0, other_pot[...], own_pot[...]), (8, n))


def order_kernel(place, own, other, out):
    n = own.shape[1]
    first = place[2] == 0
    out[:, 0:n] = jnp.where(first, own[...], other[...])
    out[:, n:] = jnp.where(first, other[...], own[...])


def first_kernel(place, rows, cols, out, one, two, top, total):
    dims = rows.shape[0] - 8

    @pl.when(place[0] == 0)
    def _():
        y = rows[0:dims, :]
        rows_t = jnp.transpose(row_side(y, jnp.zeros((1, y.shape[1]), F32)))

        def chunk(k):
            parts = []
            for i in range(4 * k, 4 * k + 4):
                x = cols[i, 0:dims, :]
                parts.append(col_side(x, (cols[i, dims : dims + 1, :] - square(x)) * LOG2E))
            return jnp.concatenate(parts, axis=1)

        out[...] = over_columns(rows_t, chunk, cols.shape[0] // 4, 4 * cols.shape[2], (one, two), top, total)

    @pl.when(place[0] != 0)
    def _():
        out[...] = jnp.zeros(out.shape, F32)


def second_kernel(offset, place, rows, cols, *rest):
    *came, belief, out, one, two = rest
    dims = rows.shape[0] - 8

    @pl.when(place[0] == 0)
    def _():
        belief[...] = jnp.zeros(belief.shape, F32)
        out[...] = jnp.zeros(out.shape, F32)

    @pl.when(place[0] != 0)
    def _():
        y = rows[0:dims, :]
        y2 = square(y)
        b = lse2([c[...] for c in came]) * LN2 - y2 - offset + rows[dims : dims + 1, :]
        n = b.shape[1] // 2
        belief[...] = jnp.where(place[2] == 0, b[:, 0:n], b[:, n:])
        rows_t = jnp.transpose(row_side(y, (b - y2) * LOG2E))

        def chunk(k):
            parts = []
            for i in (2 * k, 2 * k + 1):
                parts.append(col_side(cols[i, 0:dims, :], jnp.zeros((1, cols.shape[2]), F32)))
            return jnp.concatenate(parts, axis=1)

        lines = over_rows(rows_t, chunk, cols.shape[0] // 2, 2 * cols.shape[2], (one, two))
        out[...] = jnp.broadcast_to(jnp.concatenate(lines, axis=0)[None], out.shape)


def third_kernel(offset, place, rows, cols, came, out, one, two, top, total, belief):
    dims = rows.shape[0] - 8
    n = cols.shape[0]
    wide = rows.shape[1]

    @pl.when(place[0] == 0)
    def _():
        out[...] = jnp.zeros(out.shape, F32)

    @pl.when(place[0] != 0)
    def _():
        belief[...] = lse2([came[i] for i in range(n)]) * LN2
        rows_t = jnp.transpose(row_side(rows[0:dims, :], jnp.zeros((1, wide), F32)))

        def chunk(k):
            parts = []
            for i in range(4 * k, 4 * k + 4):
                x = cols[i, 0:dims, :]
                x2 = square(x)
                b = jnp.concatenate([belief[2 * i : 2 * i + 1, :], belief[2 * i + 1 : 2 * i + 2, :]], axis=1)
                b = b - x2 - offset + cols[i, dims : dims + 1, :]
                belief[2 * i : 2 * i + 1, :] = b[:, 0:LANES]
                belief[2 * i + 1 : 2 * i + 2, :] = b[:, LANES:]
                parts.append(col_side(x, (b - x2) * LOG2E))
            return jnp.concatenate(parts, axis=1)

        out[:, 0:wide] = over_columns(rows_t, chunk, n // 4, 4 * cols.shape[2], (one, two), top, total)
        own = 2 * place[3]
        out[:, wide : wide + LANES] = belief[pl.ds(own, 1), :]
        out[:, wide + LANES :] = belief[pl.ds(own + 1, 1), :]


def last_kernel(offset, place, pot, belief, rows, own, partner, *rest):
    *came, out = rest
    here = 2 * place[0] + place[1]
    dims = rows.shape[0] - 8
    n = pot.shape[1]
    wide = rows.shape[1]
    x = rows[0:dims, :]
    line = lse2([g[:, 0:wide] for g in (own, partner, *came)]) * LN2 - square(x) - offset + rows[dims : dims + 1, :]
    end = jnp.where(place[2] == 0, line[:, 0:n], line[:, n:])
    middle = jnp.concatenate([own[:, wide:], partner[:, wide:]], axis=1)
    out[...] = jnp.where(here == 0, pot[...], jnp.where(here == 1, belief[...], jnp.where(here == 2, middle, end)))


def device(v):
    low, core, where, high = v
    return (low * 2 + core) * (PLACES * SIDES) + where * SIDES + high


def moves(low=0, core=0, high=0, of=(0, 1)):
    return [
        (device((a, b, c, d)), device((a ^ low, b ^ core, c, d ^ high)))
        for a in of
        for b in (0, 1)
        for c in range(PLACES)
        for d in (0, 1)
    ]


def body(coords, potentials):
    _, dims, n = coords.shape
    cells = lax.axis_size("cell")
    offset = math.log(n * cells)
    tall = dims + 8
    half = n // 2
    here = lax.axis_index("tm")
    spot = lax.axis_index("cell")
    place = jnp.stack([here // 2, here % 2, spot % SIDES, spot // SIDES]).astype(jnp.int32)
    smem = pl.BlockSpec(memory_space=pltpu.SMEM)
    vmem = pl.BlockSpec(memory_space=pltpu.VMEM)
    lines = PLACES * half // LANES

    def arr(*shape):
        return jax.ShapeDtypeStruct(shape, F32)

    def sent(x, **where):
        return lax.ppermute(x, ("tm", "cell"), moves(**where))

    def around(x):
        same = [[p * SIDES + d for p in range(PLACES)] for d in range(SIDES)]
        return lax.all_to_all(x, "cell", 0, 0, axis_index_groups=same, tiled=True)

    def call(kernel, name, out, ins, scratch=()):
        return pl.pallas_call(
            kernel,
            out_shape=out,
            in_specs=[smem] + [vmem] * (ins - 1),
            scratch_shapes=list(scratch),
            compiler_params=params(),
            name=name,
        )

    other = sent(coords, core=1)
    other_pot = sent(potentials, core=1)
    copies, target = call(spread_kernel, "spread", [arr(PLACES, tall, half), arr(tall, n)], 5)(
        place, coords, potentials, other, other_pot
    )
    cols = around(copies)
    rows = call(order_kernel, "order", arr(tall, 2 * n), 3)(place, target, sent(target, high=1))
    rows1 = sent(rows, low=1, of=(0,))

    bufs = [pltpu.VMEM((2 * n, 4 * half), F32)] * 2
    pair = [pltpu.VMEM((2 * n, LANES), F32)] * 2
    part = call(first_kernel, "first", arr(1, 2 * n), 3, bufs + pair)(place, rows, cols)
    parts = [sent(part, low=1, core=j, high=k, of=(0,)) for j in (0, 1) for k in (0, 1)]
    belief1, mine = call(
        functools.partial(second_kernel, offset), "second", [arr(1, n), arr(PLACES, lines, LANES)], 7, bufs
    )(place, rows1, cols, *parts)
    seen = around(mine)
    belief1 = sent(belief1, low=1, of=(1,))
    part = call(
        functools.partial(third_kernel, offset),
        "third",
        arr(1, 2 * n + half),
        4,
        bufs + pair + [pltpu.VMEM((lines, LANES), F32)],
    )(place, rows, cols, seen)
    parts = [sent(part, core=j, high=k, of=(1,)) for j, k in ((1, 0), (0, 1), (1, 1))]
    return call(functools.partial(last_kernel, offset), "last", arr(1, n), 8)(
        place, potentials, belief1, rows, part, *parts
    )


def solution(mesh):
    return jax.shard_map(
        body,
        mesh=mesh,
        in_specs=(P("tm", None, "cell"), P("tm", "cell")),
        out_specs=P("tm", "cell"),
        check_vma=False,
    )
```

profile of v0, /device:TPU:1, one launch (start us, length us, event | category | flops | bytes accessed | tf_op | source)
XLA Modules:
  0.0 79.3 jit_solution(2534754245326573279)
XLA Ops:
  0.0 1.4 %collective-permute-start = (f32[1,64,512]{2,1,0:T(8,128)}, f32[1,64,512]{2,1,0:T(8,128)S(1)}, u32[]{:S(2)}, u32[]{:S(2)}) collective-permute-start(f32[1,64,512]{2,1,0:T(8,128)} %own.1), channel_id=1, source_target_pairs={{0,32},{1,33},{2,34},{3,35},{4,36},{5,37},{6,38},{7,39},{8,40},{9,... | collective-permute-start | bytes 393224 | tf_op jit(solution)/shard_map/ppermute | solution.py:287
  1.4 0.0 collective-permute-start.1
  1.4 0.1 pad_add_fusion.place
  1.5 1.3 %collective-permute-done.1.other_pot = f32[1,512]{1,0:T(1,128)S(1)} collective-permute-done((f32[1,512]{1,0:T(1,128)}, f32[1,512]{1,0:T(1,128)S(1)}, u32[]{:S(2)}, u32[]{:S(2)}) %collective-permute-start.1) | collective-permute-done | bytes 2080 | tf_op jit(solution)/shard_map/ppermute | solution.py:287
  2.8 0.0 collective-permute-done.other
  2.8 0.0 copy-start
  2.8 0.9 %copy-done = f32[1,64,512]{2,1,0:T(8,128)S(1)} copy-done((f32[1,64,512]{2,1,0:T(8,128)S(1)}, f32[1,64,512]{2,1,0:T(8,128)}, u32[]{:S(2)}) %copy-start) | copy-done | bytes 131096
  3.7 0.0 copy-start.1
  3.7 0.7 copy-done.1
  4.4 1.7 %spread.1 = (f32[16,72,256]{2,1,0:T(8,128)}, f32[72,512]{1,0:T(8,128)S(1)}) custom-call(s32[4]{0:T(128)S(1)} %pad_add_fusion.place, f32[1,64,512]{2,1,0:T(8,128)S(1)} %copy-done, f32[1,512]{1,0:T(1,128)S(1)} %copy-done.1, f32[1,64,512]{2,1,0:T(8,128)S(1)} %collective-permute-done.other, f32[1,512]{1,0:T(1,128)S(1)} %collective-permute-done.1.other_pot), custom_call_target="tpu_custom_call" | custom-call | tf_op jit(solution)/shard_map/spread/pallas_call | solution.py:305
  6.1 7.9 %all-to-all-start = ((f32[16,72,256]{2,1,0:T(8,128)}), f32[16,72,256]{2,1,0:T(8,128)S(1)}, u32[]{:S(2)}, u32[]{:S(2)}) async-start(f32[16,72,256]{2,1,0:T(8,128)} %get-tuple-element.10), calls=%async_computation | async-start | bytes 2359296 | tf_op jit(solution)/shard_map/all_to_all | solution.py:291
  13.9 2.8 %collective-permute-start.2 = (f32[72,512]{1,0:T(8,128)S(1)}, f32[72,512]{1,0:T(8,128)S(1)}, u32[]{:S(2)}, u32[]{:S(2)}) collective-permute-start(f32[72,512]{1,0:T(8,128)S(1)} %get-tuple-element.9.own), channel_id=1, source_target_pairs={{0,1},{1,0},{2,3},{3,2},{4,5},{5,4},{6,7},{7,6},{8,9},{9,8},{10,11... | collective-permute-start | bytes 442376 | tf_op jit(solution)/shard_map/ppermute | solution.py:287
  16.8 3.7 %collective-permute-done.2.other = f32[72,512]{1,0:T(8,128)S(1)} collective-permute-done((f32[72,512]{1,0:T(8,128)S(1)}, f32[72,512]{1,0:T(8,128)S(1)}, u32[]{:S(2)}, u32[]{:S(2)}) %collective-permute-start.2) | collective-permute-done | bytes 147488 | tf_op jit(solution)/shard_map/ppermute | solution.py:287
  20.5 0.6 order.1.rows
  21.0 3.1 %collective-permute-start.3 = (f32[72,1024]{1,0:T(8,128)S(1)}, f32[72,1024]{1,0:T(8,128)S(1)}, u32[]{:S(2)}, u32[]{:S(2)}) collective-permute-start(f32[72,1024]{1,0:T(8,128)S(1)} %order.1.rows), channel_id=1, source_target_pairs={{0,64},{1,65},{2,66},{3,67},{4,68},{5,69},{6,70},{7,71},{8,72},{9,... | collective-permute-start | bytes 884744 | tf_op jit(solution)/shard_map/ppermute | solution.py:287
  24.2 8.5 %all-to-all-done.cols = f32[16,72,256]{2,1,0:T(8,128)S(1)} async-done(((f32[16,72,256]{2,1,0:T(8,128)}), f32[16,72,256]{2,1,0:T(8,128)S(1)}, u32[]{:S(2)}, u32[]{:S(2)}) %all-to-all-start) | async-done | bytes 1179680 | tf_op jit(solution)/shard_map/all_to_all | solution.py:291
  32.6 4.2 %first.1 = f32[1,1024]{1,0:T(1,128)S(1)} custom-call(s32[4]{0:T(128)S(1)} %pad_add_fusion.place, f32[72,1024]{1,0:T(8,128)S(1)} %order.1.rows, f32[16,72,256]{2,1,0:T(8,128)S(1)} %all-to-all-done.cols), custom_call_target="tpu_custom_call" | custom-call | tf_op jit(solution)/shard_map/first/pallas_call | solution.py:314
  36.8 2.5 %collective-permute-start.7 = (f32[1,1024]{1,0:T(1,128)S(1)}, f32[1,1024]{1,0:T(1,128)S(1)}, u32[]{:S(2)}, u32[]{:S(2)}) collective-permute-start(f32[1,1024]{1,0:T(1,128)S(1)} %first.1), channel_id=1, source_target_pairs={{0,97},{1,96},{2,99},{3,98},{4,101},{5,100},{6,103},{7,102},{8,105... | collective-permute-start | bytes 12296 | tf_op jit(solution)/shard_map/ppermute | solution.py:287
  39.3 1.3 %collective-permute-start.6 = (f32[1,1024]{1,0:T(1,128)S(1)}, f32[1,1024]{1,0:T(1,128)S(1)}, u32[]{:S(2)}, u32[]{:S(2)}) collective-permute-start(f32[1,1024]{1,0:T(1,128)S(1)} %first.1), channel_id=1, source_target_pairs={{0,96},{1,97},{2,98},{3,99},{4,100},{5,101},{6,102},{7,103},{8,104... | collective-permute-start | bytes 12296 | tf_op jit(solution)/shard_map/ppermute | solution.py:287
  40.6 1.3 %collective-permute-start.5 = (f32[1,1024]{1,0:T(1,128)S(1)}, f32[1,1024]{1,0:T(1,128)S(1)}, u32[]{:S(2)}, u32[]{:S(2)}) collective-permute-start(f32[1,1024]{1,0:T(1,128)S(1)} %first.1), channel_id=1, source_target_pairs={{0,65},{1,64},{2,67},{3,66},{4,69},{5,68},{6,71},{7,70},{8,73},{9,... | collective-permute-start | bytes 12296 | tf_op jit(solution)/shard_map/ppermute | solution.py:287
  41.9 1.3 %collective-permute-start.4 = (f32[1,1024]{1,0:T(1,128)S(1)}, f32[1,1024]{1,0:T(1,128)S(1)}, u32[]{:S(2)}, u32[]{:S(2)}) collective-permute-start(f32[1,1024]{1,0:T(1,128)S(1)} %first.1), channel_id=1, source_target_pairs={{0,64},{1,65},{2,66},{3,67},{4,68},{5,69},{6,70},{7,71},{8,72},{9,... | collective-permute-start | bytes 12296 | tf_op jit(solution)/shard_map/ppermute | solution.py:287
  43.2 0.0 collective-permute-done.3.rows
  43.2 0.0 collective-permute-done.7.rest_3_
  43.3 0.0 collective-permute-done.6.rest_2_
  43.3 0.0 collective-permute-done.5.rest_1_
  43.3 0.7 collective-permute-done.4.rest_0_
  44.0 0.6 second.1
  44.5 0.0 copy-start.2
  44.6 10.4 %all_to_all.10.came = f32[16,32,128]{2,1,0:T(8,128)S(1)} all-to-all(f32[16,32,128]{2,1,0:T(8,128)S(1)} %get-tuple-element.12), channel_id=1, replica_groups={{0,2,4,6,8,10,12,14,16,18,20,22,24,26,28,30},{1,3,5,7,9,11,13,15,17,19,..., dimensions={0} | all-to-all | bytes 524288 | tf_op jit(solution)/shard_map/all_to_all | solution.py:291
  55.0 0.7 third.1.own
  55.7 0.7 collective-permute-start.11
  56.4 0.7 collective-permute-start.10
  57.1 0.7 collective-permute-start.9
  57.7 1.3 %collective-permute-start.8 = (f32[1,512]{1,0:T(1,128)S(1)}, f32[1,512]{1,0:T(1,128)S(1)}, u32[]{:S(2)}, u32[]{:S(2)}) collective-permute-start(f32[1,512]{1,0:T(1,128)S(1)} %get-tuple-element.11), channel_id=1, source_target_pairs={{64,0},{65,1},{66,2},{67,3},{68,4},{69,5},{70,6},{71,7},{72,8},{73... | collective-permute-start | bytes 6152 | tf_op jit(solution)/shard_map/ppermute | solution.py:287
  59.0 19.0 %collective-permute-done.8.belief = f32[1,512]{1,0:T(1,128)S(1)} collective-permute-done((f32[1,512]{1,0:T(1,128)S(1)}, f32[1,512]{1,0:T(1,128)S(1)}, u32[]{:S(2)}, u32[]{:S(2)}) %collective-permute-start.8) | collective-permute-done | bytes 2080 | tf_op jit(solution)/shard_map/ppermute | solution.py:287
  78.1 0.0 collective-permute-done.11.rest_1_
  78.1 0.0 collective-permute-done.10.rest_0_
  78.1 0.0 collective-permute-done.9.partner
  78.1 0.0 copy-done.2
  78.1 1.2 %last.1 = f32[1,512]{1,0:T(1,128)} custom-call(s32[4]{0:T(128)S(1)} %pad_add_fusion.place, f32[1,512]{1,0:T(1,128)S(1)} %copy-done.2, f32[1,512]{1,0:T(1,128)S(1)} %collective-permute-done.8.belief, f32[72,1024]{1,0:T(8,128)S(1)} %order.1.rows, f32[1,1280]{1,0:T(1,128)S(1)} %third.1.own, f32[1,1280]{1,0:T(1,128)S(1)} %collective-permute-done.9.partner, ...), custom_call_target="tpu_custom_call" | custom-call | tf_op jit(solution)/shard_map/last/pallas_call | solution.py:329
Async XLA Ops:
  0.0 2.8 %collective-permute-start = (f32[1,64,512]{2,1,0:T(8,128)}, f32[1,64,512]{2,1,0:T(8,128)S(1)}, u32[]{:S(2)}, u32[]{:S(2)}) collective-permute-start(f32[1,64,512]{2,1,0:T(8,128)} %own.1), channel_id=1, source_target_pairs={{0,32},{1,33},{2,34},{3,35},{4,36},{5,37},{6,38},{7,39},{8,40},{9,... | collective-permute-start | bytes 393224 | tf_op jit(solution)/shard_map/ppermute | solution.py:287
  1.4 1.4 %collective-permute-start.1 = (f32[1,512]{1,0:T(1,128)}, f32[1,512]{1,0:T(1,128)S(1)}, u32[]{:S(2)}, u32[]{:S(2)}) collective-permute-start(f32[1,512]{1,0:T(1,128)} %pot.1), channel_id=1, source_target_pairs={{0,32},{1,33},{2,34},{3,35},{4,36},{5,37},{6,38},{7,39},{8,40},{9,... | collective-permute-start | bytes 6152 | tf_op jit(solution)/shard_map/ppermute | solution.py:287
  2.8 0.9 %copy-start = (f32[1,64,512]{2,1,0:T(8,128)S(1)}, f32[1,64,512]{2,1,0:T(8,128)}, u32[]{:S(2)}) copy-start(f32[1,64,512]{2,1,0:T(8,128)} %own.1) | copy-start | bytes 393220
  3.7 0.7 copy-start.1
  6.1 26.6 %all-to-all-start = ((f32[16,72,256]{2,1,0:T(8,128)}), f32[16,72,256]{2,1,0:T(8,128)S(1)}, u32[]{:S(2)}, u32[]{:S(2)}) async-start(f32[16,72,256]{2,1,0:T(8,128)} %get-tuple-element.10), calls=%async_computation | async-start | bytes 2359296 | tf_op jit(solution)/shard_map/all_to_all | solution.py:291
  13.9 6.5 %collective-permute-start.2 = (f32[72,512]{1,0:T(8,128)S(1)}, f32[72,512]{1,0:T(8,128)S(1)}, u32[]{:S(2)}, u32[]{:S(2)}) collective-permute-start(f32[72,512]{1,0:T(8,128)S(1)} %get-tuple-element.9.own), channel_id=1, source_target_pairs={{0,1},{1,0},{2,3},{3,2},{4,5},{5,4},{6,7},{7,6},{8,9},{9,8},{10,11... | collective-permute-start | bytes 442376 | tf_op jit(solution)/shard_map/ppermute | solution.py:287
  21.0 22.2 %collective-permute-start.3 = (f32[72,1024]{1,0:T(8,128)S(1)}, f32[72,1024]{1,0:T(8,128)S(1)}, u32[]{:S(2)}, u32[]{:S(2)}) collective-permute-start(f32[72,1024]{1,0:T(8,128)S(1)} %order.1.rows), channel_id=1, source_target_pairs={{0,64},{1,65},{2,66},{3,67},{4,68},{5,69},{6,70},{7,71},{8,72},{9,... | collective-permute-start | bytes 884744 | tf_op jit(solution)/shard_map/ppermute | solution.py:287
  36.8 6.4 %collective-permute-start.7 = (f32[1,1024]{1,0:T(1,128)S(1)}, f32[1,1024]{1,0:T(1,128)S(1)}, u32[]{:S(2)}, u32[]{:S(2)}) collective-permute-start(f32[1,1024]{1,0:T(1,128)S(1)} %first.1), channel_id=1, source_target_pairs={{0,97},{1,96},{2,99},{3,98},{4,101},{5,100},{6,103},{7,102},{8,105... | collective-permute-start | bytes 12296 | tf_op jit(solution)/shard_map/ppermute | solution.py:287
  39.3 3.9 %collective-permute-start.6 = (f32[1,1024]{1,0:T(1,128)S(1)}, f32[1,1024]{1,0:T(1,128)S(1)}, u32[]{:S(2)}, u32[]{:S(2)}) collective-permute-start(f32[1,1024]{1,0:T(1,128)S(1)} %first.1), channel_id=1, source_target_pairs={{0,96},{1,97},{2,98},{3,99},{4,100},{5,101},{6,102},{7,103},{8,104... | collective-permute-start | bytes 12296 | tf_op jit(solution)/shard_map/ppermute | solution.py:287
  40.6 2.6 %collective-permute-start.5 = (f32[1,1024]{1,0:T(1,128)S(1)}, f32[1,1024]{1,0:T(1,128)S(1)}, u32[]{:S(2)}, u32[]{:S(2)}) collective-permute-start(f32[1,1024]{1,0:T(1,128)S(1)} %first.1), channel_id=1, source_target_pairs={{0,65},{1,64},{2,67},{3,66},{4,69},{5,68},{6,71},{7,70},{8,73},{9,... | collective-permute-start | bytes 12296 | tf_op jit(solution)/shard_map/ppermute | solution.py:287
  41.9 2.0 %collective-permute-start.4 = (f32[1,1024]{1,0:T(1,128)S(1)}, f32[1,1024]{1,0:T(1,128)S(1)}, u32[]{:S(2)}, u32[]{:S(2)}) collective-permute-start(f32[1,1024]{1,0:T(1,128)S(1)} %first.1), channel_id=1, source_target_pairs={{0,64},{1,65},{2,66},{3,67},{4,68},{5,69},{6,70},{7,71},{8,72},{9,... | collective-permute-start | bytes 12296 | tf_op jit(solution)/shard_map/ppermute | solution.py:287
  44.5 33.5 %copy-start.2 = (f32[1,512]{1,0:T(1,128)S(1)}, f32[1,512]{1,0:T(1,128)}, u32[]{:S(2)}) copy-start(f32[1,512]{1,0:T(1,128)} %pot.1) | copy-start | bytes 6148
  55.7 22.4 %collective-permute-start.11 = (f32[1,1280]{1,0:T(1,128)S(1)}, f32[1,1280]{1,0:T(1,128)S(1)}, u32[]{:S(2)}, u32[]{:S(2)}) collective-permute-start(f32[1,1280]{1,0:T(1,128)S(1)} %third.1.own), channel_id=1, source_target_pairs={{64,97},{65,96},{66,99},{67,98},{68,101},{69,100},{70,103},{71,102... | collective-permute-start | bytes 15368 | tf_op jit(solution)/shard_map/ppermute | solution.py:287
  56.4 21.7 %collective-permute-start.10 = (f32[1,1280]{1,0:T(1,128)S(1)}, f32[1,1280]{1,0:T(1,128)S(1)}, u32[]{:S(2)}, u32[]{:S(2)}) collective-permute-start(f32[1,1280]{1,0:T(1,128)S(1)} %third.1.own), channel_id=1, source_target_pairs={{64,65},{65,64},{66,67},{67,66},{68,69},{69,68},{70,71},{71,70},{7... | collective-permute-start | bytes 15368 | tf_op jit(solution)/shard_map/ppermute | solution.py:287
  57.1 21.0 %collective-permute-start.9 = (f32[1,1280]{1,0:T(1,128)S(1)}, f32[1,1280]{1,0:T(1,128)S(1)}, u32[]{:S(2)}, u32[]{:S(2)}) collective-permute-start(f32[1,1280]{1,0:T(1,128)S(1)} %third.1.own), channel_id=1, source_target_pairs={{64,96},{65,97},{66,98},{67,99},{68,100},{69,101},{70,102},{71,103... | collective-permute-start | bytes 15368 | tf_op jit(solution)/shard_map/ppermute | solution.py:287
  57.7 20.3 %collective-permute-start.8 = (f32[1,512]{1,0:T(1,128)S(1)}, f32[1,512]{1,0:T(1,128)S(1)}, u32[]{:S(2)}, u32[]{:S(2)}) collective-permute-start(f32[1,512]{1,0:T(1,128)S(1)} %get-tuple-element.11), channel_id=1, source_target_pairs={{64,0},{65,1},{66,2},{67,3},{68,4},{69,5},{70,6},{71,7},{72,8},{73... | collective-permute-start | bytes 6152 | tf_op jit(solution)/shard_map/ppermute | solution.py:287
where the time goes:
time: 79.7 us; the launch traced here: 79.3 us
  waiting for transfers between devices  33.2 us (42%)
  starting transfers between devices  24.9 us (31%)
  blocking collectives  10.4 us (13%)
  Pallas kernels  8.92 us (11%)
  local copies, waits for them, and re-layouts  1.59 us (2%)
    ppermute x12, waiting for transfers between devices, sent(): return lax.ppermute(x, ('tm', 'cell'), moves(**where))  24.8 us
    ppermute x12, starting transfers between devices, sent(): return lax.ppermute(x, ('tm', 'cell'), moves(**where))  17 us
    all_to_all x1, blocking collectives, around(): return lax.all_to_all(x, 'cell', 0, 0, axis_index_groups=same, tiled=True)  10.4 us
    all_to_all x1, waiting for transfers between devices, around(): return lax.all_to_all(x, 'cell', 0, 0, axis_index_groups=same, tiled=True)  8.45 us
    all_to_all x1, starting transfers between devices, around(): return lax.all_to_all(x, 'cell', 0, 0, axis_index_groups=same, tiled=True)  7.85 us
    pallas_call x1, Pallas kernels, body(): call(first_kernel, 'first', arr(1, 2 * n), 3, bufs + pair)  4.18 us
    pallas_call x1, Pallas kernels, body(): call(spread_kernel, 'spread', [arr(PLACES, tall, half), arr(tall, n)], 5)  1.69 us
  transfers between devices with their start and end apart: 13, of which 5 were waited for; matrix products, arithmetic and copies ran while one was open for 0% of the time, Pallas kernels for 6%

commit v1 on v0

v1 whole, which is shorter than its diff:
```python
import functools
import itertools
import math

import jax
import jax.numpy as jnp
from jax import lax
from jax.experimental import pallas as pl
from jax.experimental.pallas import tpu as pltpu
from jax.sharding import PartitionSpec as P

LOG2E = math.log2(math.e)
LN2 = math.log(2.0)
LANES = 128
VMEM_LIMIT = 50 * 2**20

F32 = jnp.float32
BF16 = jnp.bfloat16

PLACES = 8
CORNERS = 4


def params():
    return pltpu.CompilerParams(vmem_limit_bytes=VMEM_LIMIT)


def halves(x):
    high = x.astype(BF16)
    return high, (x - high.astype(F32)).astype(BF16)


def bias_rows(first, w, n):
    w1 = w.astype(BF16).astype(F32)
    w2 = (w - w1).astype(BF16).astype(F32)
    w3 = w - w1 - w2
    row = lax.broadcasted_iota(jnp.int32, (16, n), 0)
    other = 3 - first
    block = jnp.where(row == first, w1, jnp.where(row == first + 1, w2, jnp.where(row == first + 2, w3, 0.0)))
    block = jnp.where((row >= other) & (row < other + 3), 1.0, block)
    return jnp.concatenate([block.astype(BF16), jnp.zeros((48, n), BF16)], axis=0)


def row_side(x, w):
    high, low = halves(x * (2.0 * LOG2E))
    return jnp.concatenate([high, high, low, bias_rows(3, w, x.shape[1])], axis=0)


def col_side(x, w):
    high, low = halves(x)
    return jnp.concatenate([high, low, high, bias_rows(0, w, x.shape[1])], axis=0)


def square(x):
    return jnp.sum(x * x, axis=0, keepdims=True)


def largest(parts):
    return functools.reduce(jnp.maximum, parts)


def added(parts):
    while len(parts) > 1:
        parts = [functools.reduce(jnp.add, parts[i : i + 2]) for i in range(0, len(parts), 2)]
    return parts[0]


def lse2(parts):
    top = largest(parts)
    return top + jnp.log2(added([jnp.exp2(p - top) for p in parts]))


def times(a, b):
    return lax.dot_general(a, b, (((1,), (0,)), ((), ())), preferred_element_type=F32)


def piped(count, start, finish):
    start(0)
    for k in range(count):
        if k + 1 < count:
            start(k + 1)
        finish(k)


def more(state, parts):
    best = largest(parts)
    if state is None:
        return best, added([jnp.exp2(p - best) for p in parts])
    top, total = state
    new = jnp.maximum(top, best)
    return new, total * jnp.exp2(top - new) + added([jnp.exp2(p - new) for p in parts])


def over_columns(rows_t, col_chunk, chunks, width, bufs, top, total):
    n = rows_t.shape[0]
    step = 32

    def start(k):
        bufs[k % 2][...] = times(rows_t, col_chunk(k))

    def finish(k):
        buf = bufs[k % 2]
        for r in range(0, n, step):
            at = slice(r, r + step)
            state = None if k == 0 else (top[at, :], total[at, :])
            a, b = more(state, [buf[at, i : i + LANES] for i in range(0, width, LANES)])
            top[at, :] = a
            total[at, :] = b

    piped(chunks, start, finish)
    a = jnp.transpose(top[...])
    b = jnp.transpose(total[...])
    best = jnp.max(a, axis=0, keepdims=True)
    return best + jnp.log2(jnp.sum(b * jnp.exp2(a - best), axis=0, keepdims=True))


def over_rows(rows_t, col_chunk, chunks, width, bufs):
    n = rows_t.shape[0]
    step = 8
    lines = []

    def start(k):
        bufs[k % 2][:, 0:width] = times(rows_t, col_chunk(k))

    def finish(k):
        buf = bufs[k % 2]
        for i in range(0, width, LANES):
            state = None
            for r in range(0, n, 32 * step):
                state = more(state, [buf[q : q + step, i : i + LANES] for q in range(r, r + 32 * step, step)])
            a, b = state
            best = jnp.max(a, axis=0, keepdims=True)
            lines.append(best + jnp.log2(jnp.sum(b * jnp.exp2(a - best), axis=0, keepdims=True)))

    piped(chunks, start, finish)
    return lines


def pack_kernel(own, own_pot, out):
    dims = own.shape[1]
    out[0:dims, :] = own[0]
    out[dims:, :] = jnp.broadcast_to(own_pot[...], (8, own.shape[2]))


def spread_kernel(offset, place, own, other, other_pot, out, target, base, half_shard, sems):
    core = place[1]
    dims = other.shape[1]
    n = own.shape[1]
    half = n // 2
    at = pl.multiple_of(core * half, half)
    half_shard[0:dims, :] = jnp.where(core == 0, own[0:dims, pl.ds(at, half)], other[0, :, pl.ds(at, half)])
    half_shard[dims:, :] = jnp.where(
        core == 0, own[dims:, pl.ds(at, half)], jnp.broadcast_to(other_pot[:, pl.ds(at, half)], (8, half))
    )
    copies = [pltpu.make_async_copy(half_shard, out.at[i], sems.at[i]) for i in range(out.shape[0])]
    for c in copies:
        c.start()
    target[0:dims, :] = jnp.where(core == 0, other[0], own[0:dims, :])
    target[dims:, :] = jnp.where(core == 0, jnp.broadcast_to(other_pot[...], (8, n)), own[dims:, :])
    base[...] = own[dims : dims + 1, :] - square(own[0:dims, :]) - offset
    for c in copies:
        c.wait()


def order_kernel(place, own, other, out):
    n = own.shape[1]
    first = place[2] == 0
    out[:, 0:n] = jnp.where(first, own[...], other[...])
    out[:, n:] = jnp.where(first, other[...], own[...])


def first_kernel(place, rows, cols, *rest):
    *so_far, out, one, two, top, total = rest
    dims = rows.shape[0] - 8

    @pl.when(place[0] == 0)
    def _():
        y = rows[0:dims, :]
        rows_t = jnp.transpose(row_side(y, jnp.zeros((1, y.shape[1]), F32)))

        def chunk(k):
            parts = []
            for i in range(4 * k, 4 * k + 4):
                x = cols[i, 0:dims, :]
                parts.append(col_side(x, (cols[i, dims : dims + 1, :] - square(x)) * LOG2E))
            return jnp.concatenate(parts, axis=1)

        line = over_columns(rows_t, chunk, cols.shape[0] // 4, 4 * cols.shape[2], (one, two), top, total)
        out[...] = lse2([line] + [s[...] for s in so_far])

    @pl.when(place[0] != 0)
    def _():
        out[...] = jnp.zeros(out.shape, F32)


def second_kernel(offset, place, rows, near, far, *rest):
    *came, belief, out, one, two = rest
    dims = rows.shape[0] - 8
    blocks = near.shape[0]

    @pl.when(place[0] == 0)
    def _():
        belief[...] = jnp.zeros(belief.shape, F32)
        out[...] = jnp.zeros(out.shape, F32)

    @pl.when(place[0] != 0)
    def _():
        y = rows[0:dims, :]
        y2 = square(y)
        b = lse2([c[...] for c in came]) * LN2 - y2 - offset + rows[dims : dims + 1, :]
        n = b.shape[1] // 2
        belief[...] = jnp.where(place[2] == 0, b[:, 0:n], b[:, n:])
        rows_t = jnp.transpose(row_side(y, (b - y2) * LOG2E))

        def chunk(k):
            cols = near if k < blocks // 2 else far
            parts = []
            for i in (2 * k % blocks, 2 * k % blocks + 1):
                parts.append(col_side(cols[i, 0:dims, :], jnp.zeros((1, cols.shape[2]), F32)))
            return jnp.concatenate(parts, axis=1)

        lines = over_rows(rows_t, chunk, blocks, 2 * near.shape[2], (one, two))
        some = len(lines) // 2
        for k, side in enumerate((place[1], 1 - place[1])):
            block = jnp.concatenate(lines[k * some : (k + 1) * some], axis=0)
            at = pl.multiple_of(side * some, some)
            out[:, pl.ds(at, some), :] = jnp.broadcast_to(block[None], (out.shape[0], some, LANES))


def third_kernel(offset, place, rows, near, far, came, belief, out, one, two, top, total, seen, final):
    dims = rows.shape[0] - 8
    blocks = near.shape[0]
    some = 2 * blocks
    core = place[1]

    @pl.when(place[0] == 0)
    def _():
        out[...] = jnp.zeros(out.shape, F32)
        belief[...] = jnp.zeros(belief.shape, F32)

    @pl.when(place[0] != 0)
    def _():
        seen[...] = lse2([came[i] for i in range(came.shape[0])]) * LN2 - offset
        rows_t = jnp.transpose(row_side(rows[0:dims, :], jnp.zeros((1, rows.shape[1]), F32)))
        sides = [seen[pl.ds(pl.multiple_of(s * some, some), some), :] for s in (core, 1 - core)]

        def chunk(k):
            side = 0 if 4 * k < blocks else 1
            cols = (near, far)[side]
            parts = []
            for i in range(4 * k % blocks, 4 * k % blocks + 4):
                x = cols[i, 0:dims, :]
                x2 = square(x)
                lines = sides[side][2 * i : 2 * i + 2, :]
                b = jnp.concatenate([lines[0:1], lines[1:2]], axis=1) - x2 + cols[i, dims : dims + 1, :]
                final[side, i : i + 1, :] = b
                parts.append(col_side(x, (b - x2) * LOG2E))
            return jnp.concatenate(parts, axis=1)

        out[...] = over_columns(rows_t, chunk, blocks // 2, 4 * near.shape[2], (one, two), top, total)
        half = near.shape[2]
        mine, theirs = (final[side, pl.ds(place[4], 1), :] for side in (0, 1))
        belief[:, 0:half] = jnp.where(core == 0, mine, theirs)
        belief[:, half:] = jnp.where(core == 0, theirs, mine)


def last_kernel(place, pot, base, belief1, belief2, *rest):
    *came, out = rest
    here = 2 * place[0] + place[1]
    n = pot.shape[1]
    line = lse2([c[...] for c in came]) * LN2
    end = jnp.where(place[2] == 0, line[:, 0:n], line[:, n:]) + base[...]
    out[...] = jnp.where(here == 0, pot[...], jnp.where(here == 1, belief1[...], jnp.where(here == 2, belief2[...], end)))


def device(low, core, where, near, high):
    return ((low * 2 + core) * PLACES + where) * CORNERS + near * 2 + high


def moves(to):
    every = itertools.product((0, 1), (0, 1), range(PLACES), (0, 1), (0, 1))
    return [(device(*v), device(*to(*v))) for v in every]


def body(coords, potentials):
    _, dims, n = coords.shape
    cells = lax.axis_size("cell")
    offset = math.log(n * cells)
    tall = dims + 8
    half = n // 2
    here = lax.axis_index("tm")
    spot = lax.axis_index("cell")
    place = jnp.stack([here // 2, here % 2, spot % 2, spot // 2 % 2, spot // CORNERS]).astype(jnp.int32)
    smem = pl.BlockSpec(memory_space=pltpu.SMEM)
    vmem = pl.BlockSpec(memory_space=pltpu.VMEM)
    lines = 2 * PLACES * half // LANES

    def arr(*shape):
        return jax.ShapeDtypeStruct(shape, F32)

    def sent(x, to):
        return lax.ppermute(x, ("tm", "cell"), moves(to))

    def swapped(x):
        return sent(x, lambda l, c, p, y, h: (l, 1 - c, p, y, h))

    def call(kernel, name, out, ins, scratch=(), **kw):
        return pl.pallas_call(
            kernel,
            out_shape=out,
            in_specs=[smem] + [vmem] * (ins - 1),
            scratch_shapes=list(scratch),
            compiler_params=params(),
            name=name,
            **kw,
        )

    other = swapped(coords)
    other_pot = swapped(potentials)
    own = pl.pallas_call(pack_kernel, out_shape=arr(tall, n), compiler_params=params(), name="pack")(coords, potentials)
    copies, target, base = call(
        functools.partial(spread_kernel, offset),
        "spread",
        [arr(PLACES, tall, half), arr(tall, n), arr(1, n)],
        4,
        [pltpu.VMEM((tall, half), F32), pltpu.SemaphoreType.DMA((PLACES,))],
        out_specs=[pl.BlockSpec(memory_space=pl.ANY), vmem, vmem],
    )(place, own, other, other_pot)
    corners = [[p * CORNERS + k for p in range(PLACES)] for k in range(CORNERS)]
    near = lax.all_to_all(copies, "cell", 0, 0, axis_index_groups=corners, tiled=True)
    rows = call(order_kernel, "order", arr(tall, 2 * n), 3)(
        place,
        sent(target, lambda l, c, p, y, h: (l, y, p, c, h)),
        sent(target, lambda l, c, p, y, h: (l, y, p, c, 1 - h)),
    )
    near, rows = lax.optimization_barrier((near, rows))
    rows1 = sent(rows, lambda l, c, p, y, h: (1 - l, c, p, y, h))
    far = swapped(near)

    bufs = [pltpu.VMEM((2 * n, 4 * half), F32)] * 2
    pair = [pltpu.VMEM((2 * n, LANES), F32)] * 2
    part = call(first_kernel, "first", arr(1, 2 * n), 3, bufs + pair)(place, rows, near)
    part = call(first_kernel, "first_far", arr(1, 2 * n), 4, bufs + pair)(place, rows, far, part)
    parts = [
        sent(part, lambda l, c, p, y, h, j=j, k=k: (1 - l, c, p, y ^ j, h ^ k)) for j in (0, 1) for k in (0, 1)
    ]
    belief1, mine = call(
        functools.partial(second_kernel, offset), "second", [arr(1, n), arr(2 * PLACES, lines, LANES)], 8, bufs
    )(place, rows1, near, far, *parts)
    belief1 = sent(belief1, lambda l, c, p, y, h: (1 - l, c ^ y ^ 1, p, y, h))
    sixteen = [
        [device(l, c, p, y, h) for c in (0, 1) for p in range(PLACES)] for l in (0, 1) for y in (0, 1) for h in (0, 1)
    ]
    seen = lax.all_to_all(mine, ("tm", "cell"), 0, 0, axis_index_groups=sixteen, tiled=True)
    seen, belief1 = lax.optimization_barrier((seen, belief1))
    belief2, part = call(
        functools.partial(third_kernel, offset),
        "third",
        [arr(1, n), arr(1, 2 * n)],
        5,
        bufs + pair + [pltpu.VMEM((lines, LANES), F32), pltpu.VMEM((2, PLACES, half), F32)],
    )(place, rows, near, far, seen)
    parts = [
        sent(part, lambda l, c, p, y, h, j=j, k=k: (l, c ^ y ^ j ^ 1, p, y ^ j, h ^ k)) for j in (0, 1) for k in (0, 1)
    ]
    return call(last_kernel, "last", arr(1, n), 9)(place, potentials, base, belief1, belief2, *parts)


def solution(mesh):
    return jax.shard_map(
        body,
        mesh=mesh,
        in_specs=(P("tm", None, "cell"), P("tm", "cell")),
        out_specs=P("tm", "cell"),
        check_vma=False,
    )
```

time: 79.7 us -> 73.6 us (0.923)
  the two profiles are of different devices: /device:TPU:1 before, /device:TPU:2 now
where the time goes in v1:
time: 73.6 us; the launch traced here: 72.6 us
  starting transfers between devices  30.3 us (41%)
  waiting for transfers between devices  27.1 us (37%)
  Pallas kernels  13.5 us (18%)
  local copies, waits for them, and re-layouts  1.67 us (2%)
    ppermute x15, starting transfers between devices, sent(): return lax.ppermute(x, ('tm', 'cell'), moves(to))  18.6 us
    ppermute x15, waiting for transfers between devices, sent(): return lax.ppermute(x, ('tm', 'cell'), moves(to))  13.7 us
    all_to_all x1, starting transfers between devices, body(): lax.all_to_all(copies, 'cell', 0, 0, axis_index_groups=corners, tiled=True)  7.96 us
    all_to_all x1, waiting for transfers between devices, body(): lax.all_to_all(copies, 'cell', 0, 0, axis_index_groups=corners, tiled=True)  6.97 us
    all_to_all x1, waiting for transfers between devices, body(): lax.all_to_all(mine, ('tm', 'cell'), 0, 0, axis_index_groups=sixteen, til...  6.4 us
    pallas_call x1, Pallas kernels, body(): call(functools.partial(second_kernel, offset), 'second', [arr(1, n), arr(...  4.75 us
    pallas_call x1, Pallas kernels, body(): call(functools.partial(third_kernel, offset), 'third', [arr(1, n), arr(1,...  4.41 us
    all_to_all x1, starting transfers between devices, body(): lax.all_to_all(mine, ('tm', 'cell'), 0, 0, axis_index_groups=sixteen, til...  3.75 us
  transfers between devices with their start and end apart: 17, of which 10 were waited for; matrix products, arithmetic and copies ran while one was open for 0% of the time, Pallas kernels for 2%

profile of v1, /device:TPU:2, one launch (start us, length us, event | category | flops | bytes accessed | tf_op | source)
XLA Modules:
  0.0 72.6 jit_solution(15605339638942318820)
XLA Ops:
  0.0 0.0 collective-permute-start
  0.0 0.5 collective-permute-start.1
  0.5 0.0 copy-start.1
  0.5 0.7 copy-done.1
  1.2 0.0 copy-start
  1.2 0.9 %copy-done = f32[1,64,512]{2,1,0:T(8,128)S(1)} copy-done((f32[1,64,512]{2,1,0:T(8,128)S(1)}, f32[1,64,512]{2,1,0:T(8,128)}, u32[]{:S(2)}) %copy-start) | copy-done | bytes 131096
  2.2 0.1 stack.23.place
  2.2 0.0 collective-permute-done.1.other_pot
  2.2 0.0 collective-permute-done.other
  2.3 1.5 %spread.1 = (f32[8,72,256]{2,1,0:T(8,128)}, f32[72,512]{1,0:T(8,128)S(1)}, f32[1,512]{1,0:T(1,128)S(1)}) custom-call(s32[5]{0:T(128)S(1)} %stack.23.place, f32[72,512]{1,0:T(8,128)S(1)} %pack.1.own, f32[1,64,512]{2,1,0:T(8,128)S(1)} %collective-permute-done.other, f32[1,512]{1,0:T(1,128)S(1)} %collective-permute-done.1.other_pot), custom_call_target="tpu_custom_call" | custom-call | tf_op jit(solution)/shard_map/spread/pallas_call | solution.py:321
  3.7 8.0 %all-to-all-start = ((f32[8,72,256]{2,1,0:T(8,128)}), f32[8,72,256]{2,1,0:T(8,128)S(1)}, u32[]{:S(2)}, u32[]{:S(2)}) async-start(f32[8,72,256]{2,1,0:T(8,128)} %get-tuple-element.17), calls=%async_computation | async-start | bytes 1179648 | tf_op jit(solution)/shard_map/all_to_all | solution.py:330
  11.7 2.1 %collective-permute-start.3 = (f32[72,512]{1,0:T(8,128)S(1)}, f32[72,512]{1,0:T(8,128)S(1)}, u32[]{:S(2)}, u32[]{:S(2)}) collective-permute-start(f32[72,512]{1,0:T(8,128)S(1)} %get-tuple-element.18), channel_id=1, source_target_pairs={{0,1},{1,0},{2,33},{3,32},{4,5},{5,4},{6,37},{7,36},{8,9},{9,8},{1... | collective-permute-start | bytes 442376 | tf_op jit(solution)/shard_map/ppermute | solution.py:302
  13.8 0.7 collective-permute-start.2
  14.5 5.0 %collective-permute-done.3.other = f32[72,512]{1,0:T(8,128)S(1)} collective-permute-done((f32[72,512]{1,0:T(8,128)S(1)}, f32[72,512]{1,0:T(8,128)S(1)}, u32[]{:S(2)}, u32[]{:S(2)}) %collective-permute-start.3) | collective-permute-done | bytes 147488 | tf_op jit(solution)/shard_map/ppermute | solution.py:302
  19.4 0.0 collective-permute-done.2.own
  19.4 0.6 order.1.rows
  20.0 7.0 %all-to-all-done.cols.near = f32[8,72,256]{2,1,0:T(8,128)S(1)} async-done(((f32[8,72,256]{2,1,0:T(8,128)}), f32[8,72,256]{2,1,0:T(8,128)S(1)}, u32[]{:S(2)}, u32[]{:S(2)}) %all-to-all-start) | async-done | bytes 589856 | tf_op jit(solution)/shard_map/all_to_all | solution.py:330
  27.0 0.0 collective-permute-start.5
  27.0 0.4 collective-permute-start.4
  27.4 0.6 first.1.rest_0_
  27.9 1.1 %collective-permute-done.5.cols.far = f32[8,72,256]{2,1,0:T(8,128)S(1)} collective-permute-done((f32[8,72,256]{2,1,0:T(8,128)S(1)}, f32[8,72,256]{2,1,0:T(8,128)S(1)}, u32[]{:S(2)}, u32[]{:S(2)}) %collective-permute-start.5) | collective-permute-done | bytes 589856 | tf_op jit(solution)/shard_map/ppermute | solution.py:302
  29.0 0.6 first_far.1
  29.6 4.3 %collective-permute-start.9 = (f32[1,1024]{1,0:T(1,128)S(1)}, f32[1,1024]{1,0:T(1,128)S(1)}, u32[]{:S(2)}, u32[]{:S(2)}) collective-permute-start(f32[1,1024]{1,0:T(1,128)S(1)} %first_far.1), channel_id=1, source_target_pairs={{0,67},{1,66},{2,65},{3,64},{4,71},{5,70},{6,69},{7,68},{8,75},{9,... | collective-permute-start | bytes 12296 | tf_op jit(solution)/shard_map/ppermute | solution.py:302
  33.8 0.0 collective-permute-start.8
  33.9 4.0 %collective-permute-start.7 = (f32[1,1024]{1,0:T(1,128)S(1)}, f32[1,1024]{1,0:T(1,128)S(1)}, u32[]{:S(2)}, u32[]{:S(2)}) collective-permute-start(f32[1,1024]{1,0:T(1,128)S(1)} %first_far.1), channel_id=1, source_target_pairs={{0,65},{1,64},{2,67},{3,66},{4,69},{5,68},{6,71},{7,70},{8,73},{9,... | collective-permute-start | bytes 12296 | tf_op jit(solution)/shard_map/ppermute | solution.py:302
  37.9 0.1 collective-permute-start.6
  37.9 0.0 collective-permute-done.4.rows
  37.9 0.0 collective-permute-done.9.rest_3_
  37.9 0.4 collective-permute-done.8.rest_2_
  38.4 1.1 %collective-permute-done.7.rest_1_ = f32[1,1024]{1,0:T(1,128)S(1)} collective-permute-done((f32[1,1024]{1,0:T(1,128)S(1)}, f32[1,1024]{1,0:T(1,128)S(1)}, u32[]{:S(2)}, u32[]{:S(2)}) %collective-permute-start.7) | collective-permute-done | bytes 4128 | tf_op jit(solution)/shard_map/ppermute | solution.py:302
  39.5 2.0 %collective-permute-done.6.rest_0_ = f32[1,1024]{1,0:T(1,128)S(1)} collective-permute-done((f32[1,1024]{1,0:T(1,128)S(1)}, f32[1,1024]{1,0:T(1,128)S(1)}, u32[]{:S(2)}, u32[]{:S(2)}) %collective-permute-start.6) | collective-permute-done | bytes 4128 | tf_op jit(solution)/shard_map/ppermute | solution.py:302
  41.5 4.8 %second.1 = (f32[1,512]{1,0:T(1,128)S(1)}, f32[16,32,128]{2,1,0:T(8,128)}) custom-call(s32[5]{0:T(128)S(1)} %stack.23.place, f32[72,1024]{1,0:T(8,128)S(1)} %collective-permute-done.4.rows, f32[8,72,256]{2,1,0:T(8,128)S(1)} %all-to-all-done.cols.near, f32[8,72,256]{2,1,0:T(8,128)S(1)} %collective-permute-done.5.cols.far, ...), custom_call_target="tpu_custom_call" | custom-call | tf_op jit(solution)/shard_map/second/pallas_call | solution.py:347
  46.2 3.7 %all-to-all-start.1 = ((f32[16,32,128]{2,1,0:T(8,128)}), f32[16,32,128]{2,1,0:T(8,128)S(1)}, u32[]{:S(2)}, u32[]{:S(2)}) async-start(f32[16,32,128]{2,1,0:T(8,128)} %get-tuple-element.21), calls=%async_computation.1 | async-start | bytes 524288 | tf_op jit(solution)/shard_map/all_to_all | solution.py:354
  50.0 0.1 collective-permute-start.10
  50.1 3.0 %collective-permute-done.10.belief1 = f32[1,512]{1,0:T(1,128)S(1)} collective-permute-done((f32[1,512]{1,0:T(1,128)S(1)}, f32[1,512]{1,0:T(1,128)S(1)}, u32[]{:S(2)}, u32[]{:S(2)}) %collective-permute-start.10) | collective-permute-done | bytes 2080 | tf_op jit(solution)/shard_map/ppermute | solution.py:302
  53.1 6.4 %all-to-all-done.1.came = f32[16,32,128]{2,1,0:T(8,128)S(1)} async-done(((f32[16,32,128]{2,1,0:T(8,128)}), f32[16,32,128]{2,1,0:T(8,128)S(1)}, u32[]{:S(2)}, u32[]{:S(2)}) %all-to-all-start.1) | async-done | bytes 262176 | tf_op jit(solution)/shard_map/all_to_all | solution.py:354
  59.5 4.4 %third.1 = (f32[1,512]{1,0:T(1,128)S(1)}, f32[1,1024]{1,0:T(1,128)S(1)}) custom-call(s32[5]{0:T(128)S(1)} %stack.23.place, f32[72,1024]{1,0:T(8,128)S(1)} %order.1.rows, f32[8,72,256]{2,1,0:T(8,128)S(1)} %all-to-all-done.cols.near, f32[8,72,256]{2,1,0:T(8,128)S(1)} %collective-permute-done.5.cols.far, f32[16,32,128]{2,1,0:T(8,128)S(1)} %all-to-all-done.1.came), custom_call_target="tpu_custom_call" | custom-call | tf_op jit(solution)/shard_map/third/pallas_call | solution.py:356
  63.9 2.0 %collective-permute-start.14 = (f32[1,1024]{1,0:T(1,128)S(1)}, f32[1,1024]{1,0:T(1,128)S(1)}, u32[]{:S(2)}, u32[]{:S(2)}) collective-permute-start(f32[1,1024]{1,0:T(1,128)S(1)} %get-tuple-element.26), channel_id=1, source_target_pairs={{0,3},{1,2},{2,33},{3,32},{4,7},{5,6},{6,37},{7,36},{8,11},{9,10},... | collective-permute-start | bytes 12296 | tf_op jit(solution)/shard_map/ppermute | solution.py:302
  65.9 0.2 collective-permute-start.13
  66.2 2.3 %collective-permute-start.12 = (f32[1,1024]{1,0:T(1,128)S(1)}, f32[1,1024]{1,0:T(1,128)S(1)}, u32[]{:S(2)}, u32[]{:S(2)}) collective-permute-start(f32[1,1024]{1,0:T(1,128)S(1)} %get-tuple-element.26), channel_id=1, source_target_pairs={{0,33},{1,32},{2,3},{3,2},{4,37},{5,36},{6,7},{7,6},{8,41},{9,40},... | collective-permute-start | bytes 12296 | tf_op jit(solution)/shard_map/ppermute | solution.py:302
  68.4 1.9 %collective-permute-start.11 = (f32[1,1024]{1,0:T(1,128)S(1)}, f32[1,1024]{1,0:T(1,128)S(1)}, u32[]{:S(2)}, u32[]{:S(2)}) collective-permute-start(f32[1,1024]{1,0:T(1,128)S(1)} %get-tuple-element.26), channel_id=1, source_target_pairs={{0,32},{1,33},{2,2},{3,3},{4,36},{5,37},{6,6},{7,7},{8,40},{9,41},... | collective-permute-start | bytes 12296 | tf_op jit(solution)/shard_map/ppermute | solution.py:302
  70.3 0.0 collective-permute-done.14.rest_3_
  70.3 0.0 collective-permute-done.13.rest_2_
  70.3 0.3 collective-permute-done.12.rest_1_
  70.7 0.8 %collective-permute-done.11.rest_0_ = f32[1,1024]{1,0:T(1,128)S(1)} collective-permute-done((f32[1,1024]{1,0:T(1,128)S(1)}, f32[1,1024]{1,0:T(1,128)S(1)}, u32[]{:S(2)}, u32[]{:S(2)}) %collective-permute-start.11) | collective-permute-done | bytes 4128 | tf_op jit(solution)/shard_map/ppermute | solution.py:302
  71.5 1.1 %last.1 = f32[1,512]{1,0:T(1,128)} custom-call(s32[5]{0:T(128)S(1)} %stack.23.place, f32[1,512]{1,0:T(1,128)S(1)} %copy-done.1, f32[1,512]{1,0:T(1,128)S(1)} %get-tuple-element.16.base, f32[1,512]{1,0:T(1,128)S(1)} %collective-permute-done.10.belief1, f32[1,512]{1,0:T(1,128)S(1)} %get-tuple-element.25.belief2, ...), custom_call_target="tpu_custom_call" | custom-call | tf_op jit(solution)/shard_map/last/pallas_call | solution.py:366
  (1 shorter events, 0.0 us)
Async XLA Ops:
  0.0 2.3 %collective-permute-start = (f32[1,64,512]{2,1,0:T(8,128)}, f32[1,64,512]{2,1,0:T(8,128)S(1)}, u32[]{:S(2)}, u32[]{:S(2)}) collective-permute-start(f32[1,64,512]{2,1,0:T(8,128)} %own.1), channel_id=1, source_target_pairs={{0,32},{1,33},{2,34},{3,35},{4,36},{5,37},{6,38},{7,39},{8,40},{9,... | collective-permute-start | bytes 393224 | tf_op jit(solution)/shard_map/ppermute | solution.py:302
  0.0 2.2 %collective-permute-start.1 = (f32[1,512]{1,0:T(1,128)}, f32[1,512]{1,0:T(1,128)S(1)}, u32[]{:S(2)}, u32[]{:S(2)}) collective-permute-start(f32[1,512]{1,0:T(1,128)} %pot.1), channel_id=1, source_target_pairs={{0,32},{1,33},{2,34},{3,35},{4,36},{5,37},{6,38},{7,39},{8,40},{9,... | collective-permute-start | bytes 6152 | tf_op jit(solution)/shard_map/ppermute | solution.py:302
  0.5 0.7 copy-start.1
  1.2 0.9 %copy-start = (f32[1,64,512]{2,1,0:T(8,128)S(1)}, f32[1,64,512]{2,1,0:T(8,128)}, u32[]{:S(2)}) copy-start(f32[1,64,512]{2,1,0:T(8,128)} %own.1) | copy-start | bytes 393220
  3.7 23.3 %all-to-all-start = ((f32[8,72,256]{2,1,0:T(8,128)}), f32[8,72,256]{2,1,0:T(8,128)S(1)}, u32[]{:S(2)}, u32[]{:S(2)}) async-start(f32[8,72,256]{2,1,0:T(8,128)} %get-tuple-element.17), calls=%async_computation | async-start | bytes 1179648 | tf_op jit(solution)/shard_map/all_to_all | solution.py:330
  11.7 7.8 %collective-permute-start.3 = (f32[72,512]{1,0:T(8,128)S(1)}, f32[72,512]{1,0:T(8,128)S(1)}, u32[]{:S(2)}, u32[]{:S(2)}) collective-permute-start(f32[72,512]{1,0:T(8,128)S(1)} %get-tuple-element.18), channel_id=1, source_target_pairs={{0,1},{1,0},{2,33},{3,32},{4,5},{5,4},{6,37},{7,36},{8,9},{9,8},{1... | collective-permute-start | bytes 442376 | tf_op jit(solution)/shard_map/ppermute | solution.py:302
  13.8 5.6 %collective-permute-start.2 = (f32[72,512]{1,0:T(8,128)S(1)}, f32[72,512]{1,0:T(8,128)S(1)}, u32[]{:S(2)}, u32[]{:S(2)}) collective-permute-start(f32[72,512]{1,0:T(8,128)S(1)} %get-tuple-element.18), channel_id=1, source_target_pairs={{0,0},{1,1},{2,32},{3,33},{4,4},{5,5},{6,36},{7,37},{8,8},{9,9},{1... | collective-permute-start | bytes 442376 | tf_op jit(solution)/shard_map/ppermute | solution.py:302
  27.0 2.0 %collective-permute-start.5 = (f32[8,72,256]{2,1,0:T(8,128)S(1)}, f32[8,72,256]{2,1,0:T(8,128)S(1)}, u32[]{:S(2)}, u32[]{:S(2)}) collective-permute-start(f32[8,72,256]{2,1,0:T(8,128)S(1)} %all-to-all-done.cols.near), channel_id=1, source_target_pairs={{0,32},{1,33},{2,34},{3,35},{4,36},{5,37},{6,38},{7,39},{8,40},{9,... | collective-permute-start | bytes 1769480 | tf_op jit(solution)/shard_map/ppermute | solution.py:302
  27.0 10.9 %collective-permute-start.4 = (f32[72,1024]{1,0:T(8,128)S(1)}, f32[72,1024]{1,0:T(8,128)S(1)}, u32[]{:S(2)}, u32[]{:S(2)}) collective-permute-start(f32[72,1024]{1,0:T(8,128)S(1)} %order.1.rows), channel_id=1, source_target_pairs={{0,64},{1,65},{2,66},{3,67},{4,68},{5,69},{6,70},{7,71},{8,72},{9,... | collective-permute-start | bytes 884744 | tf_op jit(solution)/shard_map/ppermute | solution.py:302
  29.6 8.4 %collective-permute-start.9 = (f32[1,1024]{1,0:T(1,128)S(1)}, f32[1,1024]{1,0:T(1,128)S(1)}, u32[]{:S(2)}, u32[]{:S(2)}) collective-permute-start(f32[1,1024]{1,0:T(1,128)S(1)} %first_far.1), channel_id=1, source_target_pairs={{0,67},{1,66},{2,65},{3,64},{4,71},{5,70},{6,69},{7,68},{8,75},{9,... | collective-permute-start | bytes 12296 | tf_op jit(solution)/shard_map/ppermute | solution.py:302
  33.8 4.5 %collective-permute-start.8 = (f32[1,1024]{1,0:T(1,128)S(1)}, f32[1,1024]{1,0:T(1,128)S(1)}, u32[]{:S(2)}, u32[]{:S(2)}) collective-permute-start(f32[1,1024]{1,0:T(1,128)S(1)} %first_far.1), channel_id=1, source_target_pairs={{0,66},{1,67},{2,64},{3,65},{4,70},{5,71},{6,68},{7,69},{8,74},{9,... | collective-permute-start | bytes 12296 | tf_op jit(solution)/shard_map/ppermute | solution.py:302
  33.9 5.6 %collective-permute-start.7 = (f32[1,1024]{1,0:T(1,128)S(1)}, f32[1,1024]{1,0:T(1,128)S(1)}, u32[]{:S(2)}, u32[]{:S(2)}) collective-permute-start(f32[1,1024]{1,0:T(1,128)S(1)} %first_far.1), channel_id=1, source_target_pairs={{0,65},{1,64},{2,67},{3,66},{4,69},{5,68},{6,71},{7,70},{8,73},{9,... | collective-permute-start | bytes 12296 | tf_op jit(solution)/shard_map/ppermute | solution.py:302
  37.9 3.6 %collective-permute-start.6 = (f32[1,1024]{1,0:T(1,128)S(1)}, f32[1,1024]{1,0:T(1,128)S(1)}, u32[]{:S(2)}, u32[]{:S(2)}) collective-permute-start(f32[1,1024]{1,0:T(1,128)S(1)} %first_far.1), channel_id=1, source_target_pairs={{0,64},{1,65},{2,66},{3,67},{4,68},{5,69},{6,70},{7,71},{8,72},{9,... | collective-permute-start | bytes 12296 | tf_op jit(solution)/shard_map/ppermute | solution.py:302
  46.2 13.3 %all-to-all-start.1 = ((f32[16,32,128]{2,1,0:T(8,128)}), f32[16,32,128]{2,1,0:T(8,128)S(1)}, u32[]{:S(2)}, u32[]{:S(2)}) async-start(f32[16,32,128]{2,1,0:T(8,128)} %get-tuple-element.21), calls=%async_computation.1 | async-start | bytes 524288 | tf_op jit(solution)/shard_map/all_to_all | solution.py:354
  50.0 3.1 %collective-permute-start.10 = (f32[1,512]{1,0:T(1,128)S(1)}, f32[1,512]{1,0:T(1,128)S(1)}, u32[]{:S(2)}, u32[]{:S(2)}) collective-permute-start(f32[1,512]{1,0:T(1,128)S(1)} %get-tuple-element.22), channel_id=1, source_target_pairs={{0,96},{1,97},{2,66},{3,67},{4,100},{5,101},{6,70},{7,71},{8,104},... | collective-permute-start | bytes 6152 | tf_op jit(solution)/shard_map/ppermute | solution.py:302
  63.9 6.4 %collective-permute-start.14 = (f32[1,1024]{1,0:T(1,128)S(1)}, f32[1,1024]{1,0:T(1,128)S(1)}, u32[]{:S(2)}, u32[]{:S(2)}) collective-permute-start(f32[1,1024]{1,0:T(1,128)S(1)} %get-tuple-element.26), channel_id=1, source_target_pairs={{0,3},{1,2},{2,33},{3,32},{4,7},{5,6},{6,37},{7,36},{8,11},{9,10},... | collective-permute-start | bytes 12296 | tf_op jit(solution)/shard_map/ppermute | solution.py:302
  65.9 4.4 %collective-permute-start.13 = (f32[1,1024]{1,0:T(1,128)S(1)}, f32[1,1024]{1,0:T(1,128)S(1)}, u32[]{:S(2)}, u32[]{:S(2)}) collective-permute-start(f32[1,1024]{1,0:T(1,128)S(1)} %get-tuple-element.26), channel_id=1, source_target_pairs={{0,2},{1,3},{2,32},{3,33},{4,6},{5,7},{6,36},{7,37},{8,10},{9,11},... | collective-permute-start | bytes 12296 | tf_op jit(solution)/shard_map/ppermute | solution.py:302
  66.2 4.5 %collective-permute-start.12 = (f32[1,1024]{1,0:T(1,128)S(1)}, f32[1,1024]{1,0:T(1,128)S(1)}, u32[]{:S(2)}, u32[]{:S(2)}) collective-permute-start(f32[1,1024]{1,0:T(1,128)S(1)} %get-tuple-element.26), channel_id=1, source_target_pairs={{0,33},{1,32},{2,3},{3,2},{4,37},{5,36},{6,7},{7,6},{8,41},{9,40},... | collective-permute-start | bytes 12296 | tf_op jit(solution)/shard_map/ppermute | solution.py:302
  68.4 3.0 %collective-permute-start.11 = (f32[1,1024]{1,0:T(1,128)S(1)}, f32[1,1024]{1,0:T(1,128)S(1)}, u32[]{:S(2)}, u32[]{:S(2)}) collective-permute-start(f32[1,1024]{1,0:T(1,128)S(1)} %get-tuple-element.26), channel_id=1, source_target_pairs={{0,32},{1,33},{2,2},{3,3},{4,36},{5,37},{6,6},{7,7},{8,40},{9,41},... | collective-permute-start | bytes 12296 | tf_op jit(solution)/shard_map/ppermute | solution.py:302

commit v2 on v1

--- a/solution.py
+++ b/solution.py
@@ -136,17 +136,23 @@
     return lines
 
 
-def pack_kernel(own, own_pot, out):
-    dims = own.shape[1]
-    out[0:dims, :] = own[0]
-    out[dims:, :] = jnp.broadcast_to(own_pot[...], (8, own.shape[2]))
-
-
-def spread_kernel(offset, place, own, other, other_pot, out, target, base, half_shard, sems):
+def pack_kernel(own, own_pot, out, line, sems):
+    dims, n = own.shape[1:]
+    copies = [
+        pltpu.make_async_copy(own.at[0], out.at[pl.ds(0, dims)], sems.at[0]),
+        pltpu.make_async_copy(own_pot, line, sems.at[1]),
+    ]
+    for c in copies:
+        c.start()
+    for c in copies:
+        c.wait()
+    out[dims:, :] = jnp.broadcast_to(line[...], (8, n))
+
+
+def spread_kernel(place, own, other, other_pot, out, half_shard, sems):
     core = place[1]
     dims = other.shape[1]
-    n = own.shape[1]
-    half = n // 2
+    half = own.shape[1] // 2
     at = pl.multiple_of(core * half, half)
     half_shard[0:dims, :] = jnp.where(core == 0, own[0:dims, pl.ds(at, half)], other[0, :, pl.ds(at, half)])
     half_shard[dims:, :] = jnp.where(
@@ -155,28 +161,37 @@
     copies = [pltpu.make_async_copy(half_shard, out.at[i], sems.at[i]) for i in range(out.shape[0])]
     for c in copies:
         c.start()
-    target[0:dims, :] = jnp.where(core == 0, other[0], own[0:dims, :])
-    target[dims:, :] = jnp.where(core == 0, jnp.broadcast_to(other_pot[...], (8, n)), own[dims:, :])
-    base[...] = own[dims : dims + 1, :] - square(own[0:dims, :]) - offset
     for c in copies:
         c.wait()
 
 
-def order_kernel(place, own, other, out):
+def order_kernel(offset, place, own, across, along, both, keep, give, base):
+    dims = across.shape[1]
     n = own.shape[1]
-    first = place[2] == 0
-    out[:, 0:n] = jnp.where(first, own[...], other[...])
-    out[:, n:] = jnp.where(first, other[...], own[...])
+    x = own[0:dims, :]
+    base[...] = own[dims : dims + 1, :] - square(x) - offset
+    for y_lo, out in ((1, keep), (0, give)):
+        here = place[3] == y_lo
+        mine = jnp.where(here, x, along[0])
+        theirs = jnp.where(here, across[0], both[0])
+        out[:, 0:n] = jnp.where(place[2] == 0, mine, theirs)
+        out[:, n:] = jnp.where(place[2] == 0, theirs, mine)
+
+
+def rows_kernel(place, keep, got, rows, operand):
+    x = jnp.where(place[1] == 1, keep[...], got[...])
+    rows[...] = x
+    operand[...] = jnp.transpose(row_side(x, jnp.zeros((1, x.shape[1]), F32)))
 
 
 def first_kernel(place, rows, cols, *rest):
     *so_far, out, one, two, top, total = rest
-    dims = rows.shape[0] - 8
+    dims = cols.shape[1] - 8
+    n = rows.shape[0]
 
     @pl.when(place[0] == 0)
     def _():
-        y = rows[0:dims, :]
-        rows_t = jnp.transpose(row_side(y, jnp.zeros((1, y.shape[1]), F32)))
+        rows_t = rows[...]
 
         def chunk(k):
             parts = []
@@ -186,7 +201,11 @@
             return jnp.concatenate(parts, axis=1)
 
         line = over_columns(rows_t, chunk, cols.shape[0] // 4, 4 * cols.shape[2], (one, two), top, total)
-        out[...] = lse2([line] + [s[...] for s in so_far])
+        if so_far:
+            before, own_pot, other_pot = so_far
+            line = lse2([line, before[...]])
+            out[:, n:] = jnp.where(place[1] == 1, own_pot[...], other_pot[...])
+        out[:, 0:n] = line
 
     @pl.when(place[0] != 0)
     def _():
@@ -195,7 +214,7 @@
 
 def second_kernel(offset, place, rows, near, far, *rest):
     *came, belief, out, one, two = rest
-    dims = rows.shape[0] - 8
+    dims, wide = rows.shape
     blocks = near.shape[0]
 
     @pl.when(place[0] == 0)
@@ -205,11 +224,15 @@
 
     @pl.when(place[0] != 0)
     def _():
-        y = rows[0:dims, :]
+        y = rows[...]
         y2 = square(y)
-        b = lse2([c[...] for c in came]) * LN2 - y2 - offset + rows[dims : dims + 1, :]
-        n = b.shape[1] // 2
-        belief[...] = jnp.where(place[2] == 0, b[:, 0:n], b[:, n:])
+        level = place[1] == place[3]
+        pots = [jnp.where(level, came[k][:, wide:], came[2 + k][:, wide:]) for k in (0, 1)]
+        first = place[2] == 0
+        pot = jnp.concatenate([jnp.where(first, *pots), jnp.where(first, *pots[::-1])], axis=1)
+        b = lse2([c[:, 0:wide] for c in came]) * LN2 - y2 - offset + pot
+        n = wide // 2
+        belief[...] = jnp.where(first, b[:, 0:n], b[:, n:])
         rows_t = jnp.transpose(row_side(y, (b - y2) * LOG2E))
 
         def chunk(k):
@@ -228,7 +251,7 @@
 
 
 def third_kernel(offset, place, rows, near, far, came, belief, out, one, two, top, total, seen, final):
-    dims = rows.shape[0] - 8
+    dims = near.shape[1] - 8
     blocks = near.shape[0]
     some = 2 * blocks
     core = place[1]
@@ -241,7 +264,7 @@
     @pl.when(place[0] != 0)
     def _():
         seen[...] = lse2([came[i] for i in range(came.shape[0])]) * LN2 - offset
-        rows_t = jnp.transpose(row_side(rows[0:dims, :], jnp.zeros((1, rows.shape[1]), F32)))
+        rows_t = rows[...]
         sides = [seen[pl.ds(pl.multiple_of(s * some, some), some), :] for s in (core, 1 - core)]
 
         def chunk(k):
@@ -315,32 +338,47 @@
             **kw,
         )
 
+    anywhere = pl.BlockSpec(memory_space=pl.ANY)
     other = swapped(coords)
     other_pot = swapped(potentials)
-    own = pl.pallas_call(pack_kernel, out_shape=arr(tall, n), compiler_params=params(), name="pack")(coords, potentials)
-    copies, target, base = call(
-        functools.partial(spread_kernel, offset),
+    corner = [
+        sent(coords, lambda l, c, p, y, h, j=j, k=k: (l, c, p, y ^ j, h ^ k)) for j, k in ((0, 1), (1, 0), (1, 1))
+    ]
+    own = pl.pallas_call(
+        pack_kernel,
+        out_shape=arr(tall, n),
+        in_specs=[anywhere, anywhere],
+        scratch_shapes=[pltpu.VMEM((1, n), F32), pltpu.SemaphoreType.DMA((2,))],
+        compiler_params=params(),
+        name="pack",
+    )(coords, potentials)
+    copies = call(
+        spread_kernel,
         "spread",
-        [arr(PLACES, tall, half), arr(tall, n), arr(1, n)],
+        arr(PLACES, tall, half),
         4,
         [pltpu.VMEM((tall, half), F32), pltpu.SemaphoreType.DMA((PLACES,))],
-        out_specs=[pl.BlockSpec(memory_space=pl.ANY), vmem, vmem],
+        out_specs=anywhere,
     )(place, own, other, other_pot)
+    copies, *corner = lax.optimization_barrier((copies, *corner))
     corners = [[p * CORNERS + k for p in range(PLACES)] for k in range(CORNERS)]
     near = lax.all_to_all(copies, "cell", 0, 0, axis_index_groups=corners, tiled=True)
-    rows = call(order_kernel, "order", arr(tall, 2 * n), 3)(
-        place,
-        sent(target, lambda l, c, p, y, h: (l, y, p, c, h)),
-        sent(target, lambda l, c, p, y, h: (l, y, p, c, 1 - h)),
-    )
-    near, rows = lax.optimization_barrier((near, rows))
+    keep, give, base = call(
+        functools.partial(order_kernel, offset), "order", [arr(dims, 2 * n), arr(dims, 2 * n), arr(1, n)], 5
+    )(place, own, *corner)
+    rows, operand = call(
+        rows_kernel, "rows", [arr(dims, 2 * n), jax.ShapeDtypeStruct((2 * n, 4 * dims), BF16)], 3
+    )(place, keep, swapped(give))
+    near, rows, operand = lax.optimization_barrier((near, rows, operand))
     rows1 = sent(rows, lambda l, c, p, y, h: (1 - l, c, p, y, h))
     far = swapped(near)
 
     bufs = [pltpu.VMEM((2 * n, 4 * half), F32)] * 2
     pair = [pltpu.VMEM((2 * n, LANES), F32)] * 2
-    part = call(first_kernel, "first", arr(1, 2 * n), 3, bufs + pair)(place, rows, near)
-    part = call(first_kernel, "first_far", arr(1, 2 * n), 4, bufs + pair)(place, rows, far, part)
+    part = call(first_kernel, "first", arr(1, 2 * n), 3, bufs + pair)(place, operand, near)
+    part = call(first_kernel, "first_far", arr(1, 3 * n), 6, bufs + pair)(
+        place, operand, far, part, potentials, other_pot
+    )
     parts = [
         sent(part, lambda l, c, p, y, h, j=j, k=k: (1 - l, c, p, y ^ j, h ^ k)) for j in (0, 1) for k in (0, 1)
     ]
@@ -359,7 +397,7 @@
         [arr(1, n), arr(1, 2 * n)],
         5,
         bufs + pair + [pltpu.VMEM((lines, LANES), F32), pltpu.VMEM((2, PLACES, half), F32)],
-    )(place, rows, near, far, seen)
+    )(place, operand, near, far, seen)
     parts = [
         sent(part, lambda l, c, p, y, h, j=j, k=k: (l, c ^ y ^ j ^ 1, p, y ^ j, h ^ k)) for j in (0, 1) for k in (0, 1)
     ]

time: 73.6 us -> 78.3 us (1.064)
  waiting for transfers between devices: 27.1 us -> 29.4 us
  starting transfers between devices: 30.3 us -> 31.8 us
  Pallas kernels: 13.5 us -> 14.3 us
    ppermute x15 -> x17, starting transfers between devices: 18.6 us -> 20.6 us  [sent(): return lax.ppermute(x, ('tm', 'cell'), moves(to))]
    all_to_all x1, waiting for transfers between devices: 6.97 us -> 8.57 us  [body(): lax.all_to_all(copies, 'cell', 0, 0, axis_index_groups=corners, tiled=True)]
    pallas_call x4 -> x5, Pallas kernels: 2.59 us -> 3.57 us  [the longest x1 1.48 us: body(): call(spread_kernel, 'spread', arr(PLACES, tall, half), 4, [pltpu.VMEM((ta...]
    ppermute x15 -> x17, waiting for transfers between devices: 13.7 us -> 14.7 us  [sent(): return lax.ppermute(x, ('tm', 'cell'), moves(to))]
  transfers between devices with their start and end apart: 17 -> 19, of which waited for: 10 -> 12; matrix products, arithmetic and copies ran while one was open for 0% -> 0% of each run, Pallas kernels for 2% -> 5%
where the time goes in v2:
time: 78.3 us; the launch traced here: 77.3 us
  starting transfers between devices  31.8 us (41%)
  waiting for transfers between devices  29.4 us (38%)
  Pallas kernels  14.3 us (18%)
  local copies, waits for them, and re-layouts  1.67 us (2%)
    ppermute x17, starting transfers between devices, sent(): return lax.ppermute(x, ('tm', 'cell'), moves(to))  20.6 us
    ppermute x17, waiting for transfers between devices, sent(): return lax.ppermute(x, ('tm', 'cell'), moves(to))  14.7 us
    all_to_all x1, waiting for transfers between devices, body(): lax.all_to_all(copies, 'cell', 0, 0, axis_index_groups=corners, tiled=True)  8.57 us
    all_to_all x1, starting transfers between devices, body(): lax.all_to_all(copies, 'cell', 0, 0, axis_index_groups=corners, tiled=True)  7.65 us
    all_to_all x1, waiting for transfers between devices, body(): lax.all_to_all(mine, ('tm', 'cell'), 0, 0, axis_index_groups=sixteen, til...  6.15 us
    pallas_call x1, Pallas kernels, body(): call(functools.partial(second_kernel, offset), 'second', [arr(1, n), arr(...  4.76 us
    pallas_call x1, Pallas kernels, body(): call(functools.partial(third_kernel, offset), 'third', [arr(1, n), arr(1,...  4.23 us
    all_to_all x1, starting transfers between devices, body(): lax.all_to_all(mine, ('tm', 'cell'), 0, 0, axis_index_groups=sixteen, til...  3.53 us
  transfers between devices with their start and end apart: 19, of which 12 were waited for; matrix products, arithmetic and copies ran while one was open for 0% of the time, Pallas kernels for 5%

profile of v2, /device:TPU:2, one launch (start us, length us, event | category | flops | bytes accessed | tf_op | source)
XLA Modules:
  0.0 77.3 jit_solution(5594007028580582521)
XLA Ops:
  0.0 0.0 collective-permute-start
  0.0 2.1 %collective-permute-start.2 = (f32[1,64,512]{2,1,0:T(8,128)}, f32[1,64,512]{2,1,0:T(8,128)S(1)}, u32[]{:S(2)}, u32[]{:S(2)}) collective-permute-start(f32[1,64,512]{2,1,0:T(8,128)} %own.1), channel_id=1, source_target_pairs={{0,1},{1,0},{2,3},{3,2},{4,5},{5,4},{6,7},{7,6},{8,9},{9,8},{10,11... | collective-permute-start | bytes 393224 | tf_op jit(solution)/shard_map/ppermute | solution.py:325
  2.1 2.4 %collective-permute-start.4 = (f32[1,64,512]{2,1,0:T(8,128)}, f32[1,64,512]{2,1,0:T(8,128)S(1)}, u32[]{:S(2)}, u32[]{:S(2)}) collective-permute-start(f32[1,64,512]{2,1,0:T(8,128)} %own.1), channel_id=1, source_target_pairs={{0,3},{1,2},{2,1},{3,0},{4,7},{5,6},{6,5},{7,4},{8,11},{9,10},{10,... | collective-permute-start | bytes 393224 | tf_op jit(solution)/shard_map/ppermute | solution.py:325
  4.5 0.4 collective-permute-start.3
  5.0 0.0 collective-permute-start.1
  5.0 0.0 copy-start.1
  5.0 0.7 copy-done.1
  5.7 0.0 copy-start
  5.7 0.9 %copy-done = f32[1,64,512]{2,1,0:T(8,128)S(1)} copy-done((f32[1,64,512]{2,1,0:T(8,128)S(1)}, f32[1,64,512]{2,1,0:T(8,128)}, u32[]{:S(2)}) %copy-start) | copy-done | bytes 131096
  6.6 0.2 pack.1.own
  6.8 0.1 stack.23.place
  6.9 0.0 collective-permute-done.1.other_pot.rest_2_
  6.9 0.0 collective-permute-done.other
  6.9 1.5 %spread.1 = f32[8,72,256]{2,1,0:T(8,128)} custom-call(s32[5]{0:T(128)S(1)} %stack.23.place, f32[72,512]{1,0:T(8,128)S(1)} %pack.1.own, f32[1,64,512]{2,1,0:T(8,128)S(1)} %collective-permute-done.other, f32[1,512]{1,0:T(1,128)S(1)} %collective-permute-done.1.other_pot.rest_2_), custom_call_target="tpu_custom_call" | custom-call | tf_op jit(solution)/shard_map/spread/pallas_call | solution.py:355
  8.4 0.0 collective-permute-done.2.across
  8.4 3.2 %collective-permute-done.4.both = f32[1,64,512]{2,1,0:T(8,128)S(1)} collective-permute-done((f32[1,64,512]{2,1,0:T(8,128)}, f32[1,64,512]{2,1,0:T(8,128)S(1)}, u32[]{:S(2)}, u32[]{:S(2)}) %collective-permute-start.4) | collective-permute-done | bytes 131104 | tf_op jit(solution)/shard_map/ppermute | solution.py:325
  11.6 1.4 %collective-permute-done.3.along = f32[1,64,512]{2,1,0:T(8,128)S(1)} collective-permute-done((f32[1,64,512]{2,1,0:T(8,128)}, f32[1,64,512]{2,1,0:T(8,128)S(1)}, u32[]{:S(2)}, u32[]{:S(2)}) %collective-permute-start.3) | collective-permute-done | bytes 131104 | tf_op jit(solution)/shard_map/ppermute | solution.py:325
  12.9 7.7 %all-to-all-start = ((f32[8,72,256]{2,1,0:T(8,128)}), f32[8,72,256]{2,1,0:T(8,128)S(1)}, u32[]{:S(2)}, u32[]{:S(2)}) async-start(f32[8,72,256]{2,1,0:T(8,128)} %spread.1), calls=%async_computation | async-start | bytes 1179648 | tf_op jit(solution)/shard_map/all_to_all | solution.py:365
  20.6 0.6 order.1
  21.2 0.1 collective-permute-start.5
  21.3 1.5 %collective-permute-done.5.got = f32[64,1024]{1,0:T(8,128)S(1)} collective-permute-done((f32[64,1024]{1,0:T(8,128)S(1)}, f32[64,1024]{1,0:T(8,128)S(1)}, u32[]{:S(2)}, u32[]{:S(2)}) %collective-permute-start.5) | collective-permute-done | bytes 262176 | tf_op jit(solution)/shard_map/ppermute | solution.py:325
  22.8 0.8 rows.1
  23.6 8.6 %all-to-all-done.cols.near = f32[8,72,256]{2,1,0:T(8,128)S(1)} async-done(((f32[8,72,256]{2,1,0:T(8,128)}), f32[8,72,256]{2,1,0:T(8,128)S(1)}, u32[]{:S(2)}, u32[]{:S(2)}) %all-to-all-start) | async-done | bytes 589856 | tf_op jit(solution)/shard_map/all_to_all | solution.py:365
  32.1 0.0 collective-permute-start.7
  32.1 0.5 collective-permute-start.6
  32.6 0.6 first.1.rest_0_
  33.2 0.9 %collective-permute-done.7.cols.far = f32[8,72,256]{2,1,0:T(8,128)S(1)} collective-permute-done((f32[8,72,256]{2,1,0:T(8,128)S(1)}, f32[8,72,256]{2,1,0:T(8,128)S(1)}, u32[]{:S(2)}, u32[]{:S(2)}) %collective-permute-start.7) | collective-permute-done | bytes 589856 | tf_op jit(solution)/shard_map/ppermute | solution.py:325
  34.1 0.6 first_far.1
  34.7 5.0 %collective-permute-start.11 = (f32[1,1536]{1,0:T(1,128)S(1)}, f32[1,1536]{1,0:T(1,128)S(1)}, u32[]{:S(2)}, u32[]{:S(2)}) collective-permute-start(f32[1,1536]{1,0:T(1,128)S(1)} %first_far.1), channel_id=1, source_target_pairs={{0,67},{1,66},{2,65},{3,64},{4,71},{5,70},{6,69},{7,68},{8,75},{9,... | collective-permute-start | bytes 18440 | tf_op jit(solution)/shard_map/ppermute | solution.py:325
  39.7 0.0 collective-permute-start.10
  39.7 3.3 %collective-permute-start.9 = (f32[1,1536]{1,0:T(1,128)S(1)}, f32[1,1536]{1,0:T(1,128)S(1)}, u32[]{:S(2)}, u32[]{:S(2)}) collective-permute-start(f32[1,1536]{1,0:T(1,128)S(1)} %first_far.1), channel_id=1, source_target_pairs={{0,65},{1,64},{2,67},{3,66},{4,69},{5,68},{6,71},{7,70},{8,73},{9,... | collective-permute-start | bytes 18440 | tf_op jit(solution)/shard_map/ppermute | solution.py:325
  43.0 0.1 collective-permute-start.8
  43.0 0.0 collective-permute-done.6.rows
  43.1 0.0 collective-permute-done.11.rest_3_
  43.1 1.2 %collective-permute-done.10.rest_2_ = f32[1,1536]{1,0:T(1,128)S(1)} collective-permute-done((f32[1,1536]{1,0:T(1,128)S(1)}, f32[1,1536]{1,0:T(1,128)S(1)}, u32[]{:S(2)}, u32[]{:S(2)}) %collective-permute-start.10) | collective-permute-done | bytes 6176 | tf_op jit(solution)/shard_map/ppermute | solution.py:325
  44.3 0.3 collective-permute-done.9.rest_1_
  44.6 2.0 %collective-permute-done.8.rest_0_ = f32[1,1536]{1,0:T(1,128)S(1)} collective-permute-done((f32[1,1536]{1,0:T(1,128)S(1)}, f32[1,1536]{1,0:T(1,128)S(1)}, u32[]{:S(2)}, u32[]{:S(2)}) %collective-permute-start.8) | collective-permute-done | bytes 6176 | tf_op jit(solution)/shard_map/ppermute | solution.py:325
  46.6 4.8 %second.1 = (f32[1,512]{1,0:T(1,128)S(1)}, f32[16,32,128]{2,1,0:T(8,128)}) custom-call(s32[5]{0:T(128)S(1)} %stack.23.place, f32[64,1024]{1,0:T(8,128)S(1)} %collective-permute-done.6.rows, f32[8,72,256]{2,1,0:T(8,128)S(1)} %all-to-all-done.cols.near, f32[8,72,256]{2,1,0:T(8,128)S(1)} %collective-permute-done.7.cols.far, ...), custom_call_target="tpu_custom_call" | custom-call | tf_op jit(solution)/shard_map/second/pallas_call | solution.py:385
  51.4 3.5 %all-to-all-start.1 = ((f32[16,32,128]{2,1,0:T(8,128)}), f32[16,32,128]{2,1,0:T(8,128)S(1)}, u32[]{:S(2)}, u32[]{:S(2)}) async-start(f32[16,32,128]{2,1,0:T(8,128)} %get-tuple-element.35), calls=%async_computation.1 | async-start | bytes 524288 | tf_op jit(solution)/shard_map/all_to_all | solution.py:392
  54.9 0.3 collective-permute-start.12
  55.2 3.0 %collective-permute-done.12.belief1 = f32[1,512]{1,0:T(1,128)S(1)} collective-permute-done((f32[1,512]{1,0:T(1,128)S(1)}, f32[1,512]{1,0:T(1,128)S(1)}, u32[]{:S(2)}, u32[]{:S(2)}) %collective-permute-start.12) | collective-permute-done | bytes 2080 | tf_op jit(solution)/shard_map/ppermute | solution.py:325
  58.2 6.2 %all-to-all-done.1.came = f32[16,32,128]{2,1,0:T(8,128)S(1)} async-done(((f32[16,32,128]{2,1,0:T(8,128)}), f32[16,32,128]{2,1,0:T(8,128)S(1)}, u32[]{:S(2)}, u32[]{:S(2)}) %all-to-all-start.1) | async-done | bytes 262176 | tf_op jit(solution)/shard_map/all_to_all | solution.py:392
  64.3 4.2 %third.1 = (f32[1,512]{1,0:T(1,128)S(1)}, f32[1,1024]{1,0:T(1,128)S(1)}) custom-call(s32[5]{0:T(128)S(1)} %stack.23.place, bf16[1024,256]{1,0:T(8,128)(2,1)S(1)} %get-tuple-element.34.rows, f32[8,72,256]{2,1,0:T(8,128)S(1)} %all-to-all-done.cols.near, f32[8,72,256]{2,1,0:T(8,128)S(1)} %collective-permute-done.7.cols.far, f32[16,32,128]{2,1,0:T(8,128)S(1)} %all-to-all-done.1.came), custom_call_target="tpu_custom_call" | custom-call | tf_op jit(solution)/shard_map/third/pallas_call | solution.py:394
  68.6 1.8 %collective-permute-start.16 = (f32[1,1024]{1,0:T(1,128)S(1)}, f32[1,1024]{1,0:T(1,128)S(1)}, u32[]{:S(2)}, u32[]{:S(2)}) collective-permute-start(f32[1,1024]{1,0:T(1,128)S(1)} %get-tuple-element.40), channel_id=1, source_target_pairs={{0,3},{1,2},{2,33},{3,32},{4,7},{5,6},{6,37},{7,36},{8,11},{9,10},... | collective-permute-start | bytes 12296 | tf_op jit(solution)/shard_map/ppermute | solution.py:325
  70.4 0.5 collective-permute-start.15
  70.8 2.2 %collective-permute-start.14 = (f32[1,1024]{1,0:T(1,128)S(1)}, f32[1,1024]{1,0:T(1,128)S(1)}, u32[]{:S(2)}, u32[]{:S(2)}) collective-permute-start(f32[1,1024]{1,0:T(1,128)S(1)} %get-tuple-element.40), channel_id=1, source_target_pairs={{0,33},{1,32},{2,3},{3,2},{4,37},{5,36},{6,7},{7,6},{8,41},{9,40},... | collective-permute-start | bytes 12296 | tf_op jit(solution)/shard_map/ppermute | solution.py:325
  73.1 1.9 %collective-permute-start.13 = (f32[1,1024]{1,0:T(1,128)S(1)}, f32[1,1024]{1,0:T(1,128)S(1)}, u32[]{:S(2)}, u32[]{:S(2)}) collective-permute-start(f32[1,1024]{1,0:T(1,128)S(1)} %get-tuple-element.40), channel_id=1, source_target_pairs={{0,32},{1,33},{2,2},{3,3},{4,36},{5,37},{6,6},{7,7},{8,40},{9,41},... | collective-permute-start | bytes 12296 | tf_op jit(solution)/shard_map/ppermute | solution.py:325
  75.0 0.0 collective-permute-done.16.rest_3_
  75.0 0.0 collective-permute-done.15.rest_2_
  75.0 0.4 collective-permute-done.14.rest_1_
  75.4 0.7 collective-permute-done.13.rest_0_
  76.1 1.1 %last.1 = f32[1,512]{1,0:T(1,128)} custom-call(s32[5]{0:T(128)S(1)} %stack.23.place, f32[1,512]{1,0:T(1,128)S(1)} %copy-done.1, f32[1,512]{1,0:T(1,128)S(1)} %get-tuple-element.26.base, f32[1,512]{1,0:T(1,128)S(1)} %collective-permute-done.12.belief1, f32[1,512]{1,0:T(1,128)S(1)} %get-tuple-element.39.belief2, ...), custom_call_target="tpu_custom_call" | custom-call | tf_op jit(solution)/shard_map/last/pallas_call | solution.py:404
Async XLA Ops:
  0.0 6.9 %collective-permute-start = (f32[1,64,512]{2,1,0:T(8,128)}, f32[1,64,512]{2,1,0:T(8,128)S(1)}, u32[]{:S(2)}, u32[]{:S(2)}) collective-permute-start(f32[1,64,512]{2,1,0:T(8,128)} %own.1), channel_id=1, source_target_pairs={{0,32},{1,33},{2,34},{3,35},{4,36},{5,37},{6,38},{7,39},{8,40},{9,... | collective-permute-start | bytes 393224 | tf_op jit(solution)/shard_map/ppermute | solution.py:325
  0.0 8.4 %collective-permute-start.2 = (f32[1,64,512]{2,1,0:T(8,128)}, f32[1,64,512]{2,1,0:T(8,128)S(1)}, u32[]{:S(2)}, u32[]{:S(2)}) collective-permute-start(f32[1,64,512]{2,1,0:T(8,128)} %own.1), channel_id=1, source_target_pairs={{0,1},{1,0},{2,3},{3,2},{4,5},{5,4},{6,7},{7,6},{8,9},{9,8},{10,11... | collective-permute-start | bytes 393224 | tf_op jit(solution)/shard_map/ppermute | solution.py:325
  2.1 9.4 %collective-permute-start.4 = (f32[1,64,512]{2,1,0:T(8,128)}, f32[1,64,512]{2,1,0:T(8,128)S(1)}, u32[]{:S(2)}, u32[]{:S(2)}) collective-permute-start(f32[1,64,512]{2,1,0:T(8,128)} %own.1), channel_id=1, source_target_pairs={{0,3},{1,2},{2,1},{3,0},{4,7},{5,6},{6,5},{7,4},{8,11},{9,10},{10,... | collective-permute-start | bytes 393224 | tf_op jit(solution)/shard_map/ppermute | solution.py:325
  4.5 8.4 %collective-permute-start.3 = (f32[1,64,512]{2,1,0:T(8,128)}, f32[1,64,512]{2,1,0:T(8,128)S(1)}, u32[]{:S(2)}, u32[]{:S(2)}) collective-permute-start(f32[1,64,512]{2,1,0:T(8,128)} %own.1), channel_id=1, source_target_pairs={{0,2},{1,3},{2,0},{3,1},{4,6},{5,7},{6,4},{7,5},{8,10},{9,11},{10,... | collective-permute-start | bytes 393224 | tf_op jit(solution)/shard_map/ppermute | solution.py:325
  5.0 1.9 %collective-permute-start.1 = (f32[1,512]{1,0:T(1,128)}, f32[1,512]{1,0:T(1,128)S(1)}, u32[]{:S(2)}, u32[]{:S(2)}) collective-permute-start(f32[1,512]{1,0:T(1,128)} %pot.1), channel_id=1, source_target_pairs={{0,32},{1,33},{2,34},{3,35},{4,36},{5,37},{6,38},{7,39},{8,40},{9,... | collective-permute-start | bytes 6152 | tf_op jit(solution)/shard_map/ppermute | solution.py:325
  5.0 0.7 copy-start.1
  5.7 0.9 %copy-start = (f32[1,64,512]{2,1,0:T(8,128)S(1)}, f32[1,64,512]{2,1,0:T(8,128)}, u32[]{:S(2)}) copy-start(f32[1,64,512]{2,1,0:T(8,128)} %own.1) | copy-start | bytes 393220
  12.9 19.2 %all-to-all-start = ((f32[8,72,256]{2,1,0:T(8,128)}), f32[8,72,256]{2,1,0:T(8,128)S(1)}, u32[]{:S(2)}, u32[]{:S(2)}) async-start(f32[8,72,256]{2,1,0:T(8,128)} %spread.1), calls=%async_computation | async-start | bytes 1179648 | tf_op jit(solution)/shard_map/all_to_all | solution.py:365
  21.2 1.6 %collective-permute-start.5 = (f32[64,1024]{1,0:T(8,128)S(1)}, f32[64,1024]{1,0:T(8,128)S(1)}, u32[]{:S(2)}, u32[]{:S(2)}) collective-permute-start(f32[64,1024]{1,0:T(8,128)S(1)} %get-tuple-element.29), channel_id=1, source_target_pairs={{0,32},{1,33},{2,34},{3,35},{4,36},{5,37},{6,38},{7,39},{8,40},{9,... | collective-permute-start | bytes 786440 | tf_op jit(solution)/shard_map/ppermute | solution.py:325
  32.1 2.0 %collective-permute-start.7 = (f32[8,72,256]{2,1,0:T(8,128)S(1)}, f32[8,72,256]{2,1,0:T(8,128)S(1)}, u32[]{:S(2)}, u32[]{:S(2)}) collective-permute-start(f32[8,72,256]{2,1,0:T(8,128)S(1)} %all-to-all-done.cols.near), channel_id=1, source_target_pairs={{0,32},{1,33},{2,34},{3,35},{4,36},{5,37},{6,38},{7,39},{8,40},{9,... | collective-permute-start | bytes 1769480 | tf_op jit(solution)/shard_map/ppermute | solution.py:325
  32.1 10.9 %collective-permute-start.6 = (f32[64,1024]{1,0:T(8,128)S(1)}, f32[64,1024]{1,0:T(8,128)S(1)}, u32[]{:S(2)}, u32[]{:S(2)}) collective-permute-start(f32[64,1024]{1,0:T(8,128)S(1)} %get-tuple-element.32), channel_id=1, source_target_pairs={{0,64},{1,65},{2,66},{3,67},{4,68},{5,69},{6,70},{7,71},{8,72},{9,... | collective-permute-start | bytes 786440 | tf_op jit(solution)/shard_map/ppermute | solution.py:325
  34.7 8.3 %collective-permute-start.11 = (f32[1,1536]{1,0:T(1,128)S(1)}, f32[1,1536]{1,0:T(1,128)S(1)}, u32[]{:S(2)}, u32[]{:S(2)}) collective-permute-start(f32[1,1536]{1,0:T(1,128)S(1)} %first_far.1), channel_id=1, source_target_pairs={{0,67},{1,66},{2,65},{3,64},{4,71},{5,70},{6,69},{7,68},{8,75},{9,... | collective-permute-start | bytes 18440 | tf_op jit(solution)/shard_map/ppermute | solution.py:325
  39.7 4.5 %collective-permute-start.10 = (f32[1,1536]{1,0:T(1,128)S(1)}, f32[1,1536]{1,0:T(1,128)S(1)}, u32[]{:S(2)}, u32[]{:S(2)}) collective-permute-start(f32[1,1536]{1,0:T(1,128)S(1)} %first_far.1), channel_id=1, source_target_pairs={{0,66},{1,67},{2,64},{3,65},{4,70},{5,71},{6,68},{7,69},{8,74},{9,... | collective-permute-start | bytes 18440 | tf_op jit(solution)/shard_map/ppermute | solution.py:325
  39.7 4.9 %collective-permute-start.9 = (f32[1,1536]{1,0:T(1,128)S(1)}, f32[1,1536]{1,0:T(1,128)S(1)}, u32[]{:S(2)}, u32[]{:S(2)}) collective-permute-start(f32[1,1536]{1,0:T(1,128)S(1)} %first_far.1), channel_id=1, source_target_pairs={{0,65},{1,64},{2,67},{3,66},{4,69},{5,68},{6,71},{7,70},{8,73},{9,... | collective-permute-start | bytes 18440 | tf_op jit(solution)/shard_map/ppermute | solution.py:325
  43.0 3.6 %collective-permute-start.8 = (f32[1,1536]{1,0:T(1,128)S(1)}, f32[1,1536]{1,0:T(1,128)S(1)}, u32[]{:S(2)}, u32[]{:S(2)}) collective-permute-start(f32[1,1536]{1,0:T(1,128)S(1)} %first_far.1), channel_id=1, source_target_pairs={{0,64},{1,65},{2,66},{3,67},{4,68},{5,69},{6,70},{7,71},{8,72},{9,... | collective-permute-start | bytes 18440 | tf_op jit(solution)/shard_map/ppermute | solution.py:325
  51.4 13.0 %all-to-all-start.1 = ((f32[16,32,128]{2,1,0:T(8,128)}), f32[16,32,128]{2,1,0:T(8,128)S(1)}, u32[]{:S(2)}, u32[]{:S(2)}) async-start(f32[16,32,128]{2,1,0:T(8,128)} %get-tuple-element.35), calls=%async_computation.1 | async-start | bytes 524288 | tf_op jit(solution)/shard_map/all_to_all | solution.py:392
  54.9 3.3 %collective-permute-start.12 = (f32[1,512]{1,0:T(1,128)S(1)}, f32[1,512]{1,0:T(1,128)S(1)}, u32[]{:S(2)}, u32[]{:S(2)}) collective-permute-start(f32[1,512]{1,0:T(1,128)S(1)} %get-tuple-element.36), channel_id=1, source_target_pairs={{0,96},{1,97},{2,66},{3,67},{4,100},{5,101},{6,70},{7,71},{8,104},... | collective-permute-start | bytes 6152 | tf_op jit(solution)/shard_map/ppermute | solution.py:325
  68.6 6.4 %collective-permute-start.16 = (f32[1,1024]{1,0:T(1,128)S(1)}, f32[1,1024]{1,0:T(1,128)S(1)}, u32[]{:S(2)}, u32[]{:S(2)}) collective-permute-start(f32[1,1024]{1,0:T(1,128)S(1)} %get-tuple-element.40), channel_id=1, source_target_pairs={{0,3},{1,2},{2,33},{3,32},{4,7},{5,6},{6,37},{7,36},{8,11},{9,10},... | collective-permute-start | bytes 12296 | tf_op jit(solution)/shard_map/ppermute | solution.py:325
  70.4 4.6 %collective-permute-start.15 = (f32[1,1024]{1,0:T(1,128)S(1)}, f32[1,1024]{1,0:T(1,128)S(1)}, u32[]{:S(2)}, u32[]{:S(2)}) collective-permute-start(f32[1,1024]{1,0:T(1,128)S(1)} %get-tuple-element.40), channel_id=1, source_target_pairs={{0,2},{1,3},{2,32},{3,33},{4,6},{5,7},{6,36},{7,37},{8,10},{9,11},... | collective-permute-start | bytes 12296 | tf_op jit(solution)/shard_map/ppermute | solution.py:325
  70.8 4.5 %collective-permute-start.14 = (f32[1,1024]{1,0:T(1,128)S(1)}, f32[1,1024]{1,0:T(1,128)S(1)}, u32[]{:S(2)}, u32[]{:S(2)}) collective-permute-start(f32[1,1024]{1,0:T(1,128)S(1)} %get-tuple-element.40), channel_id=1, source_target_pairs={{0,33},{1,32},{2,3},{3,2},{4,37},{5,36},{6,7},{7,6},{8,41},{9,40},... | collective-permute-start | bytes 12296 | tf_op jit(solution)/shard_map/ppermute | solution.py:325
  73.1 3.0 %collective-permute-start.13 = (f32[1,1024]{1,0:T(1,128)S(1)}, f32[1,1024]{1,0:T(1,128)S(1)}, u32[]{:S(2)}, u32[]{:S(2)}) collective-permute-start(f32[1,1024]{1,0:T(1,128)S(1)} %get-tuple-element.40), channel_id=1, source_target_pairs={{0,32},{1,33},{2,2},{3,3},{4,36},{5,37},{6,6},{7,7},{8,40},{9,41},... | collective-permute-start | bytes 12296 | tf_op jit(solution)/shard_map/ppermute | solution.py:325

commit v3 on v1

v3 whole, which is shorter than its diff:
```python
import functools
import itertools
import math

import jax
import jax.numpy as jnp
from jax import lax
from jax.experimental import pallas as pl
from jax.experimental.pallas import tpu as pltpu
from jax.sharding import PartitionSpec as P

LOG2E = math.log2(math.e)
LN2 = math.log(2.0)
LANES = 128
VMEM_LIMIT = 50 * 2**20

F32 = jnp.float32
BF16 = jnp.bfloat16

DEPTHS = 4
PLACES = 2 * DEPTHS


def params():
    return pltpu.CompilerParams(vmem_limit_bytes=VMEM_LIMIT)


def halves(x):
    high = x.astype(BF16)
    return high, (x - high.astype(F32)).astype(BF16)


def bias_rows(first, w, n):
    w1 = w.astype(BF16).astype(F32)
    w2 = (w - w1).astype(BF16).astype(F32)
    w3 = w - w1 - w2
    row = lax.broadcasted_iota(jnp.int32, (16, n), 0)
    other = 3 - first
    block = jnp.where(row == first, w1, jnp.where(row == first + 1, w2, jnp.where(row == first + 2, w3, 0.0)))
    block = jnp.where((row >= other) & (row < other + 3), 1.0, block)
    return jnp.concatenate([block.astype(BF16), jnp.zeros((48, n), BF16)], axis=0)


def row_side(x, w):
    high, low = halves(x * (2.0 * LOG2E))
    return jnp.concatenate([high, high, low, bias_rows(3, w, x.shape[1])], axis=0)


def col_side(x, w):
    high, low = halves(x)
    return jnp.concatenate([high, low, high, bias_rows(0, w, x.shape[1])], axis=0)


def square(x):
    return jnp.sum(x * x, axis=0, keepdims=True)


def largest(parts):
    return functools.reduce(jnp.maximum, parts)


def added(parts):
    while len(parts) > 1:
        parts = [functools.reduce(jnp.add, parts[i : i + 2]) for i in range(0, len(parts), 2)]
    return parts[0]


def lse2(parts):
    top = largest(parts)
    return top + jnp.log2(added([jnp.exp2(p - top) for p in parts]))


def times(a, b):
    return lax.dot_general(a, b, (((1,), (0,)), ((), ())), preferred_element_type=F32)


def piped(count, start, finish):
    start(0)
    for k in range(count):
        if k + 1 < count:
            start(k + 1)
        finish(k)


def more(state, parts):
    best = largest(parts)
    if state is None:
        return best, added([jnp.exp2(p - best) for p in parts])
    top, total = state
    new = jnp.maximum(top, best)
    return new, total * jnp.exp2(top - new) + added([jnp.exp2(p - new) for p in parts])


def over_columns(rows_t, col_chunk, chunks, width, bufs, top, total):
    n = rows_t.shape[0]
    step = 32

    def start(k):
        bufs[k % 2][...] = times(rows_t, col_chunk(k))

    def finish(k):
        buf = bufs[k % 2]
        for r in range(0, n, step):
            at = slice(r, r + step)
            state = None if k == 0 else (top[at, :], total[at, :])
            a, b = more(state, [buf[at, i : i + LANES] for i in range(0, width, LANES)])
            top[at, :] = a
            total[at, :] = b

    piped(chunks, start, finish)
    a = jnp.transpose(top[...])
    b = jnp.transpose(total[...])
    best = jnp.max(a, axis=0, keepdims=True)
    return best + jnp.log2(jnp.sum(b * jnp.exp2(a - best), axis=0, keepdims=True))


def over_rows(rows_t, col_chunk, chunks, width, bufs):
    n = rows_t.shape[0]
    step = 8
    lines = []

    def start(k):
        bufs[k % 2][:, 0:width] = times(rows_t, col_chunk(k))

    def finish(k):
        buf = bufs[k % 2]
        for i in range(0, width, LANES):
            state = None
            for r in range(0, n, 32 * step):
                state = more(state, [buf[q : q + step, i : i + LANES] for q in range(r, r + 32 * step, step)])
            a, b = state
            best = jnp.max(a, axis=0, keepdims=True)
            lines.append(best + jnp.log2(jnp.sum(b * jnp.exp2(a - best), axis=0, keepdims=True)))

    piped(chunks, start, finish)
    return lines


def pack_kernel(offset, own, own_pot, out, base):
    dims = own.shape[1]
    out[0:dims, :] = own[0]
    out[dims:, :] = jnp.broadcast_to(own_pot[...], (8, own.shape[2]))
    base[...] = own_pot[...] - square(own[0]) - offset


def pick_kernel(place, own, other, other_pot, source, target):
    first = place[1] == 0
    dims, n = other.shape[1:]
    theirs = jnp.concatenate([other[0], jnp.broadcast_to(other_pot[...], (8, n))], axis=0)
    source[...] = jnp.where(first, own[...], theirs)
    target[...] = jnp.where(first, theirs, own[...])


def order_kernel(place, own, other, out, operand):
    dims = own.shape[0] - 8
    n = own.shape[1]
    first = place[2] == 0
    out[:, 0:n] = jnp.where(first, own[...], other[...])
    out[:, n:] = jnp.where(first, other[...], own[...])
    operand[...] = jnp.transpose(row_side(out[0:dims, :], jnp.zeros((1, 2 * n), F32)))


def first_kernel(place, rows, *rest):
    *ins, out, one, two, top, total = rest
    cols, so_far = ins[:DEPTHS], ins[DEPTHS:]
    dims = cols[0].shape[0] - 8

    @pl.when(place[0] == 0)
    def _():
        def chunk(k):
            parts = []
            for c in cols[2 * k : 2 * k + 2]:
                x = c[0:dims, :]
                parts.append(col_side(x, (c[dims : dims + 1, :] - square(x)) * LOG2E))
            return jnp.concatenate(parts, axis=1)

        line = over_columns(rows[...], chunk, DEPTHS // 2, 2 * cols[0].shape[1], (one, two), top, total)
        out[...] = lse2([line] + [s[...] for s in so_far])

    @pl.when(place[0] != 0)
    def _():
        out[...] = jnp.zeros(out.shape, F32)


def split_kernel(place, *refs):
    *cols, out, extra = refs
    dims = cols[0].shape[0] - 8

    @pl.when(place[0] != 0)
    def _():
        for k, c in enumerate(cols):
            depth = lax.rem(place[4] + DEPTHS - k % DEPTHS, DEPTHS)
            high_y = lax.rem(place[5] + place[1] + k // DEPTHS, 2)
            at = 2 * depth + high_y
            x = c[0:dims, :]
            high, low = halves(x)
            out[at, :, :] = jnp.concatenate([high, low, high], axis=0)
            extra[at, 0:1, :] = square(x)
            extra[at, 1:2, :] = c[dims : dims + 1, :]


def second_kernel(offset, place, rows, cols, *rest):
    *came, belief, out, one, two = rest
    dims = rows.shape[0] - 8
    blocks, _, width = cols.shape

    @pl.when(place[0] == 0)
    def _():
        belief[...] = jnp.zeros(belief.shape, F32)
        out[...] = jnp.zeros(out.shape, F32)

    @pl.when(place[0] != 0)
    def _():
        y = rows[0:dims, :]
        y2 = square(y)
        b = lse2([c[...] for c in came]) * LN2 - y2 - offset + rows[dims : dims + 1, :]
        n = b.shape[1] // 2
        belief[...] = jnp.where(place[2] == 0, b[:, 0:n], b[:, n:])
        rows_t = jnp.transpose(row_side(y, (b - y2) * LOG2E))
        no_bias = bias_rows(0, jnp.zeros((1, width), F32), width)

        def chunk(k):
            return jnp.concatenate([cols[k], no_bias], axis=0)

        lines = over_rows(rows_t, chunk, blocks, width, (one, two))
        out[...] = jnp.broadcast_to(jnp.concatenate(lines, axis=0)[None], out.shape)


def third_kernel(offset, place, rows, cols, extra, came, belief, out, one, two, top, total, seen, final):
    blocks, _, width = cols.shape
    some = width // LANES

    @pl.when(place[0] == 0)
    def _():
        out[...] = jnp.zeros(out.shape, F32)
        belief[...] = jnp.zeros(belief.shape, F32)

    @pl.when(place[0] != 0)
    def _():
        seen[...] = lse2([came[i] for i in range(came.shape[0])]) * LN2 - offset

        def chunk(k):
            parts = []
            for i in (2 * k, 2 * k + 1):
                line = jnp.concatenate([seen[some * i + q : some * i + q + 1, :] for q in range(some)], axis=1)
                x2 = extra[i, 0:1, :]
                b = line - x2 + extra[i, 1:2, :]
                final[i : i + 1, :] = b
                parts.append(jnp.concatenate([cols[i], bias_rows(0, (b - x2) * LOG2E, width)], axis=0))
            return jnp.concatenate(parts, axis=1)

        out[...] = over_columns(rows[...], chunk, blocks // 2, 2 * width, (one, two), top, total)
        belief[...] = final[pl.ds(2 * place[4] + place[5], 1), :]


def last_kernel(place, pot, base, belief1, belief2, *rest):
    *came, out = rest
    here = 2 * place[0] + place[1]
    n = pot.shape[1]
    line = lse2([c[...] for c in came]) * LN2
    end = jnp.where(place[2] == 0, line[:, 0:n], line[:, n:]) + base[...]
    out[...] = jnp.where(here == 0, pot[...], jnp.where(here == 1, belief1[...], jnp.where(here == 2, belief2[...], end)))


def device(low, core, depth, far, near, high):
    return ((((low * 2 + core) * DEPTHS + depth) * 2 + far) * 2 + near) * 2 + high


def moves(to):
    every = itertools.product((0, 1), (0, 1), range(DEPTHS), (0, 1), (0, 1), (0, 1))
    return [(device(*v), device(*to(*v))) for v in every]


def body(coords, potentials):
    _, dims, n = coords.shape
    cells = lax.axis_size("cell")
    offset = math.log(n * cells)
    tall = dims + 8
    here = lax.axis_index("tm")
    spot = lax.axis_index("cell")
    place = jnp.stack([here // 2, here % 2, spot % 2, spot // 2 % 2, spot // 8, spot // 4 % 2]).astype(jnp.int32)
    smem = pl.BlockSpec(memory_space=pltpu.SMEM)
    vmem = pl.BlockSpec(memory_space=pltpu.VMEM)
    lines = PLACES * n // LANES

    def arr(*shape, dtype=F32):
        return jax.ShapeDtypeStruct(shape, dtype)

    def sent(x, to):
        return lax.ppermute(x, ("tm", "cell"), moves(to))

    def swapped(x):
        return sent(x, lambda l, c, z, f, y, h: (l, 1 - c, z, f, y, h))

    def call(kernel, name, out, ins, scratch=()):
        return pl.pallas_call(
            kernel,
            out_shape=out,
            in_specs=[smem] + [vmem] * (ins - 1),
            scratch_shapes=list(scratch),
            compiler_params=params(),
            name=name,
        )

    own, base = pl.pallas_call(
        functools.partial(pack_kernel, offset),
        out_shape=[arr(tall, n), arr(1, n)],
        compiler_params=params(),
        name="pack",
    )(coords, potentials)
    source, target = call(pick_kernel, "pick", [arr(tall, n)] * 2, 4)(
        place, own, swapped(coords), swapped(potentials)
    )
    sides = [
        sent(target, lambda l, c, z, f, y, h: (l, y, z, f, c, h)),
        sent(target, lambda l, c, z, f, y, h: (l, y, z, f, c, 1 - h)),
    ]
    near = [
        sent(source, lambda l, c, z, f, y, h, d=d: (l, c, (z + d) % DEPTHS, f ^ c, y, h)) for d in range(DEPTHS)
    ]
    rows, operand = call(order_kernel, "order", [arr(tall, 2 * n), arr(2 * n, 4 * dims, dtype=BF16)], 3)(place, *sides)
    rows1 = sent(rows, lambda l, c, z, f, y, h: (1 - l, c, z, f, y, h))
    far = [swapped(x) for x in near]

    bufs = [pltpu.VMEM((2 * n, 2 * n), F32)] * 2
    pair = [pltpu.VMEM((2 * n, LANES), F32)] * 2
    part = call(first_kernel, "first", arr(1, 2 * n), 6, bufs + pair)(place, operand, *near)
    part = call(first_kernel, "first_far", arr(1, 2 * n), 7, bufs + pair)(place, operand, *far, part)
    parts = [
        sent(part, lambda l, c, z, f, y, h, j=j, k=k: (1 - l, c, z, f, y ^ j, h ^ k)) for j in (0, 1) for k in (0, 1)
    ]
    cols, extra = call(
        split_kernel, "split", [arr(PLACES, 3 * dims, n, dtype=BF16), arr(PLACES, 8, n)], 1 + PLACES
    )(place, *near, *far)
    belief1, mine = call(
        functools.partial(second_kernel, offset), "second", [arr(1, n), arr(2 * PLACES, lines, LANES)], 7, bufs
    )(place, rows1, cols, *parts)
    belief1 = sent(belief1, lambda l, c, z, f, y, h: (1 - l, c ^ y ^ 1, z, f, y, h))
    sixteen = [
        [device(l, c, z, f, y, h) for c in (0, 1) for z in range(DEPTHS) for f in (0, 1)]
        for l in (0, 1)
        for y in (0, 1)
        for h in (0, 1)
    ]
    seen = lax.all_to_all(mine, ("tm", "cell"), 0, 0, axis_index_groups=sixteen, tiled=True)
    seen, belief1 = lax.optimization_barrier((seen, belief1))
    belief2, part = call(
        functools.partial(third_kernel, offset),
        "third",
        [arr(1, n), arr(1, 2 * n)],
        5,
        bufs + pair + [pltpu.VMEM((lines, LANES), F32), pltpu.VMEM((PLACES, n), F32)],
    )(place, operand, cols, extra, seen)
    parts = [
        sent(part, lambda l, c, z, f, y, h, j=j, k=k: (l, c ^ y ^ j ^ 1, z, f, y ^ j, h ^ k))
        for j in (0, 1)
        for k in (0, 1)
    ]
    return call(last_kernel, "last", arr(1, n), 9)(place, potentials, base, belief1, belief2, *parts)


def solution(mesh):
    return jax.shard_map(
        body,
        mesh=mesh,
        in_specs=(P("tm", None, "cell"), P("tm", "cell")),
        out_specs=P("tm", "cell"),
        check_vma=False,
    )
```

time: 73.6 us -> 74.3 us (level)
  starting transfers between devices: 30.3 us -> 43.9 us
  waiting for transfers between devices: 27.1 us -> 15 us
    ppermute x15 -> x22, starting transfers between devices: 18.6 us -> 39.3 us  [sent(): return lax.ppermute(x, ('tm', 'cell'), moves(to))]
    all_to_all x1 -> x0, starting transfers between devices: 7.96 us -> none  [body(): lax.all_to_all(copies, 'cell', 0, 0, axis_index_groups=corners, tiled=True)]
    all_to_all x1 -> x0, waiting for transfers between devices: 6.97 us -> none  [body(): lax.all_to_all(copies, 'cell', 0, 0, axis_index_groups=corners, tiled=True)]
    ppermute x15 -> x22, waiting for transfers between devices: 13.7 us -> 8.55 us  [sent(): return lax.ppermute(x, ('tm', 'cell'), moves(to))]
    all_to_all x1, starting transfers between devices: 3.75 us -> 4.56 us  [body(): lax.all_to_all(mine, ('tm', 'cell'), 0, 0, axis_index_groups=sixteen, til...]
    pallas_call x5 -> x6, Pallas kernels: 3.15 us -> 3.24 us  [the longest x1 0.78 us: body(): call(split_kernel, 'split', [arr(PLACES, 3 * dims, n, dtype=BF16), arr(PL...]
    unnamed x4 -> x6, local copies, waits for them, and re-layouts: 1.58 us -> 1.59 us
  transfers between devices with their start and end apart: 17 -> 23, of which waited for: 10 -> 7; matrix products, arithmetic and copies ran while one was open for 0% -> 0% of each run, Pallas kernels for 2% -> 4%
where the time goes in v3:
time: 74.3 us; the launch traced here: 74 us
  starting transfers between devices  43.9 us (59%)
  waiting for transfers between devices  15 us (20%)
  Pallas kernels  13.3 us (18%)
  local copies, waits for them, and re-layouts  1.67 us (2%)
    ppermute x22, starting transfers between devices, sent(): return lax.ppermute(x, ('tm', 'cell'), moves(to))  39.3 us
    ppermute x22, waiting for transfers between devices, sent(): return lax.ppermute(x, ('tm', 'cell'), moves(to))  8.55 us
    all_to_all x1, waiting for transfers between devices, body(): lax.all_to_all(mine, ('tm', 'cell'), 0, 0, axis_index_groups=sixteen, til...  6.4 us
    pallas_call x1, Pallas kernels, body(): call(functools.partial(second_kernel, offset), 'second', [arr(1, n), arr(...  4.84 us
    all_to_all x1, starting transfers between devices, body(): lax.all_to_all(mine, ('tm', 'cell'), 0, 0, axis_index_groups=sixteen, til...  4.56 us
    pallas_call x1, Pallas kernels, body(): call(functools.partial(third_kernel, offset), 'third', [arr(1, n), arr(1,...  4.13 us
    unnamed x6, local copies, waits for them, and re-layouts  1.59 us
  transfers between devices with their start and end apart: 23, of which 7 were waited for; matrix products, arithmetic and copies ran while one was open for 0% of the time, Pallas kernels for 4%

profile of v3, /device:TPU:2, one launch (start us, length us, event | category | flops | bytes accessed | tf_op | source)
XLA Modules:
  0.0 74.0 jit_solution(5320177798392311111)
XLA Ops:
  0.0 0.0 collective-permute-start
  0.0 0.5 collective-permute-start.1
  0.5 0.0 copy-start
  0.5 0.9 %copy-done = f32[1,64,512]{2,1,0:T(8,128)S(1)} copy-done((f32[1,64,512]{2,1,0:T(8,128)S(1)}, f32[1,64,512]{2,1,0:T(8,128)}, u32[]{:S(2)}) %copy-start) | copy-done | bytes 131096
  1.4 0.0 copy-start.1
  1.4 0.7 copy-done.1
  2.2 0.1 stack.27.place
  2.3 0.0 collective-permute-done.1.other_pot
  2.3 0.0 collective-permute-done.other
  2.3 0.6 pick.1
  2.9 0.7 collective-permute-start.2
  3.5 2.2 %collective-permute-start.3 = (f32[72,512]{1,0:T(8,128)S(1)}, f32[72,512]{1,0:T(8,128)S(1)}, u32[]{:S(2)}, u32[]{:S(2)}) collective-permute-start(f32[72,512]{1,0:T(8,128)S(1)} %get-tuple-element.21), channel_id=1, source_target_pairs={{0,1},{1,0},{2,33},{3,32},{4,5},{5,4},{6,37},{7,36},{8,9},{9,8},{1... | collective-permute-start | bytes 442376 | tf_op jit(solution)/shard_map/ppermute | solution.py:290
  5.7 0.7 collective-permute-start.5
  6.4 2.0 %collective-permute-start.6 = (f32[72,512]{1,0:T(8,128)S(1)}, f32[72,512]{1,0:T(8,128)S(1)}, u32[]{:S(2)}, u32[]{:S(2)}) collective-permute-start(f32[72,512]{1,0:T(8,128)S(1)} %get-tuple-element.23), channel_id=1, source_target_pairs={{0,8},{1,9},{2,10},{3,11},{4,12},{5,13},{6,14},{7,15},{8,16},{9,17... | collective-permute-start | bytes 442376 | tf_op jit(solution)/shard_map/ppermute | solution.py:290
  8.4 3.6 %collective-permute-start.7 = (f32[72,512]{1,0:T(8,128)S(1)}, f32[72,512]{1,0:T(8,128)S(1)}, u32[]{:S(2)}, u32[]{:S(2)}) collective-permute-start(f32[72,512]{1,0:T(8,128)S(1)} %get-tuple-element.23), channel_id=1, source_target_pairs={{0,16},{1,17},{2,18},{3,19},{4,20},{5,21},{6,22},{7,23},{8,24},{9,... | collective-permute-start | bytes 442376 | tf_op jit(solution)/shard_map/ppermute | solution.py:290
  12.0 0.0 collective-permute-done.2.own
  12.0 1.0 %collective-permute-start.8 = (f32[72,512]{1,0:T(8,128)S(1)}, f32[72,512]{1,0:T(8,128)S(1)}, u32[]{:S(2)}, u32[]{:S(2)}) collective-permute-start(f32[72,512]{1,0:T(8,128)S(1)} %get-tuple-element.23), channel_id=1, source_target_pairs={{0,24},{1,25},{2,26},{3,27},{4,28},{5,29},{6,30},{7,31},{8,0},{9,1... | collective-permute-start | bytes 442376 | tf_op jit(solution)/shard_map/ppermute | solution.py:290
  13.0 0.0 collective-permute-done.3.other
  13.0 0.7 %order.1 = (f32[72,1024]{1,0:T(8,128)S(1)}, bf16[1024,256]{1,0:T(8,128)(2,1)S(1)}) custom-call(s32[6]{0:T(128)S(1)} %stack.27.place, f32[72,512]{1,0:T(8,128)S(1)} %collective-permute-done.2.own, f32[72,512]{1,0:T(8,128)S(1)} %collective-permute-done.3.other), custom_call_target="tpu_custom_call" | custom-call | tf_op jit(solution)/shard_map/order/pallas_call | solution.py:321
  13.7 1.5 %collective-permute-start.4 = (f32[72,1024]{1,0:T(8,128)S(1)}, f32[72,1024]{1,0:T(8,128)S(1)}, u32[]{:S(2)}, u32[]{:S(2)}) collective-permute-start(f32[72,1024]{1,0:T(8,128)S(1)} %get-tuple-element.22), channel_id=1, source_target_pairs={{0,64},{1,65},{2,66},{3,67},{4,68},{5,69},{6,70},{7,71},{8,72},{9,... | collective-permute-start | bytes 884744 | tf_op jit(solution)/shard_map/ppermute | solution.py:290
  15.3 0.0 collective-permute-done.5.refs_0_.rest_0_
  15.3 7.6 %collective-permute-start.9 = (f32[72,512]{1,0:T(8,128)S(1)}, f32[72,512]{1,0:T(8,128)S(1)}, u32[]{:S(2)}, u32[]{:S(2)}) collective-permute-start(f32[72,512]{1,0:T(8,128)S(1)} %collective-permute-done.5.refs_0_.rest_0_), channel_id=1, source_target_pairs={{0,32},{1,33},{2,34},{3,35},{4,36},{5,37},{6,38},{7,39},{8,40},{9,... | collective-permute-start | bytes 442376 | tf_op jit(solution)/shard_map/ppermute | solution.py:290
  22.9 0.0 collective-permute-done.6.refs_1_.rest_1_
  22.9 0.1 collective-permute-start.10
  23.0 0.0 collective-permute-done.7.refs_2_.rest_2_
  23.0 1.5 %collective-permute-start.11 = (f32[72,512]{1,0:T(8,128)S(1)}, f32[72,512]{1,0:T(8,128)S(1)}, u32[]{:S(2)}, u32[]{:S(2)}) collective-permute-start(f32[72,512]{1,0:T(8,128)S(1)} %collective-permute-done.7.refs_2_.rest_2_), channel_id=1, source_target_pairs={{0,32},{1,33},{2,34},{3,35},{4,36},{5,37},{6,38},{7,39},{8,40},{9,... | collective-permute-start | bytes 442376 | tf_op jit(solution)/shard_map/ppermute | solution.py:290
  24.5 0.0 collective-permute-done.8.refs_3_.rest_3_
  24.5 2.3 %collective-permute-start.12 = (f32[72,512]{1,0:T(8,128)S(1)}, f32[72,512]{1,0:T(8,128)S(1)}, u32[]{:S(2)}, u32[]{:S(2)}) collective-permute-start(f32[72,512]{1,0:T(8,128)S(1)} %collective-permute-done.8.refs_3_.rest_3_), channel_id=1, source_target_pairs={{0,32},{1,33},{2,34},{3,35},{4,36},{5,37},{6,38},{7,39},{8,40},{9,... | collective-permute-start | bytes 442376 | tf_op jit(solution)/shard_map/ppermute | solution.py:290
  26.8 0.6 first.1.rest_4_
  27.4 0.0 collective-permute-done.9.refs_4_.rest_0_
  27.4 0.0 collective-permute-done.10.refs_5_.rest_1_
  27.4 0.0 collective-permute-done.11.refs_6_.rest_2_
  27.4 0.4 collective-permute-done.12.refs_7_.rest_3_
  27.8 0.6 first_far.1
  28.4 5.2 %collective-permute-start.13 = (f32[1,1024]{1,0:T(1,128)S(1)}, f32[1,1024]{1,0:T(1,128)S(1)}, u32[]{:S(2)}, u32[]{:S(2)}) collective-permute-start(f32[1,1024]{1,0:T(1,128)S(1)} %first_far.1), channel_id=1, source_target_pairs={{0,64},{1,65},{2,66},{3,67},{4,68},{5,69},{6,70},{7,71},{8,72},{9,... | collective-permute-start | bytes 12296 | tf_op jit(solution)/shard_map/ppermute | solution.py:290
  33.6 0.0 collective-permute-start.14
  33.6 0.0 collective-permute-start.15
  33.6 3.6 %collective-permute-start.16 = (f32[1,1024]{1,0:T(1,128)S(1)}, f32[1,1024]{1,0:T(1,128)S(1)}, u32[]{:S(2)}, u32[]{:S(2)}) collective-permute-start(f32[1,1024]{1,0:T(1,128)S(1)} %first_far.1), channel_id=1, source_target_pairs={{0,67},{1,66},{2,65},{3,64},{4,71},{5,70},{6,69},{7,68},{8,75},{9,... | collective-permute-start | bytes 12296 | tf_op jit(solution)/shard_map/ppermute | solution.py:290
  37.2 0.8 %split.1 = (bf16[8,192,512]{2,1,0:T(8,128)(2,1)S(1)}, f32[8,8,512]{2,1,0:T(8,128)S(1)}) custom-call(s32[6]{0:T(128)S(1)} %stack.27.place, f32[72,512]{1,0:T(8,128)S(1)} %collective-permute-done.5.refs_0_.rest_0_, f32[72,512]{1,0:T(8,128)S(1)} %collective-permute-done.6.refs_1_.rest_1_, f32[72,512]{1,0:T(8,128)S(1)} %collective-permute-done.7.refs_2_.rest_2_, ...), custom_call_target="tpu_custom_call" | custom-call | tf_op jit(solution)/shard_map/split/pallas_call | solution.py:332
  38.0 0.0 collective-permute-done.13.rest_0_
  38.0 0.0 collective-permute-done.14.rest_1_
  38.0 0.1 collective-permute-done.15.rest_2_
  38.1 0.7 collective-permute-done.16.rest_3_
  38.8 0.0 collective-permute-done.4.rows
  38.8 4.8 %second.1 = (f32[1,512]{1,0:T(1,128)S(1)}, f32[16,32,128]{2,1,0:T(8,128)}) custom-call(s32[6]{0:T(128)S(1)} %stack.27.place, f32[72,1024]{1,0:T(8,128)S(1)} %collective-permute-done.4.rows, bf16[8,192,512]{2,1,0:T(8,128)(2,1)S(1)} %get-tuple-element.24.cols, f32[1,1024]{1,0:T(1,128)S(1)} %collective-permute-done.13.rest_0_, ...), custom_call_target="tpu_custom_call" | custom-call | tf_op jit(solution)/shard_map/second/pallas_call | solution.py:335
  43.6 0.0 copy-start.2
  43.6 4.6 %all-to-all-start = ((f32[16,32,128]{2,1,0:T(8,128)}), f32[16,32,128]{2,1,0:T(8,128)S(1)}, u32[]{:S(2)}, u32[]{:S(2)}) async-start(f32[16,32,128]{2,1,0:T(8,128)} %get-tuple-element.26), calls=%async_computation | async-start | bytes 524288 | tf_op jit(solution)/shard_map/all_to_all | solution.py:345
  48.2 0.1 collective-permute-start.17
  48.3 3.0 %collective-permute-done.17.belief1 = f32[1,512]{1,0:T(1,128)S(1)} collective-permute-done((f32[1,512]{1,0:T(1,128)S(1)}, f32[1,512]{1,0:T(1,128)S(1)}, u32[]{:S(2)}, u32[]{:S(2)}) %collective-permute-start.17) | collective-permute-done | bytes 2080 | tf_op jit(solution)/shard_map/ppermute | solution.py:290
  51.3 6.4 %all-to-all-done.came = f32[16,32,128]{2,1,0:T(8,128)S(1)} async-done(((f32[16,32,128]{2,1,0:T(8,128)}), f32[16,32,128]{2,1,0:T(8,128)S(1)}, u32[]{:S(2)}, u32[]{:S(2)}) %all-to-all-start) | async-done | bytes 262176 | tf_op jit(solution)/shard_map/all_to_all | solution.py:345
  57.7 4.1 %third.1 = (f32[1,512]{1,0:T(1,128)S(1)}, f32[1,1024]{1,0:T(1,128)S(1)}) custom-call(s32[6]{0:T(128)S(1)} %stack.27.place, bf16[1024,256]{1,0:T(8,128)(2,1)S(1)} %get-tuple-element.25.rows, bf16[8,192,512]{2,1,0:T(8,128)(2,1)S(1)} %get-tuple-element.24.cols, f32[8,8,512]{2,1,0:T(8,128)S(1)} %get-tuple-element.29.extra, f32[16,32,128]{2,1,0:T(8,128)S(1)} %all-to-all-done.came), custom_call_target="tpu_custom_call" | custom-call | tf_op jit(solution)/shard_map/third/pallas_call | solution.py:347
  61.8 1.9 %collective-permute-start.18 = (f32[1,1024]{1,0:T(1,128)S(1)}, f32[1,1024]{1,0:T(1,128)S(1)}, u32[]{:S(2)}, u32[]{:S(2)}) collective-permute-start(f32[1,1024]{1,0:T(1,128)S(1)} %get-tuple-element.32), channel_id=1, source_target_pairs={{0,32},{1,33},{2,2},{3,3},{4,36},{5,37},{6,6},{7,7},{8,40},{9,41},... | collective-permute-start | bytes 12296 | tf_op jit(solution)/shard_map/ppermute | solution.py:290
  63.8 2.9 %collective-permute-start.19 = (f32[1,1024]{1,0:T(1,128)S(1)}, f32[1,1024]{1,0:T(1,128)S(1)}, u32[]{:S(2)}, u32[]{:S(2)}) collective-permute-start(f32[1,1024]{1,0:T(1,128)S(1)} %get-tuple-element.32), channel_id=1, source_target_pairs={{0,33},{1,32},{2,3},{3,2},{4,37},{5,36},{6,7},{7,6},{8,41},{9,40},... | collective-permute-start | bytes 12296 | tf_op jit(solution)/shard_map/ppermute | solution.py:290
  66.6 0.8 %collective-permute-start.20 = (f32[1,1024]{1,0:T(1,128)S(1)}, f32[1,1024]{1,0:T(1,128)S(1)}, u32[]{:S(2)}, u32[]{:S(2)}) collective-permute-start(f32[1,1024]{1,0:T(1,128)S(1)} %get-tuple-element.32), channel_id=1, source_target_pairs={{0,2},{1,3},{2,32},{3,33},{4,6},{5,7},{6,36},{7,37},{8,10},{9,11},... | collective-permute-start | bytes 12296 | tf_op jit(solution)/shard_map/ppermute | solution.py:290
  67.4 1.1 %collective-permute-start.21 = (f32[1,1024]{1,0:T(1,128)S(1)}, f32[1,1024]{1,0:T(1,128)S(1)}, u32[]{:S(2)}, u32[]{:S(2)}) collective-permute-start(f32[1,1024]{1,0:T(1,128)S(1)} %get-tuple-element.32), channel_id=1, source_target_pairs={{0,3},{1,2},{2,33},{3,32},{4,7},{5,6},{6,37},{7,36},{8,11},{9,10},... | collective-permute-start | bytes 12296 | tf_op jit(solution)/shard_map/ppermute | solution.py:290
  68.6 0.0 collective-permute-done.18.rest_0_
  68.6 0.0 collective-permute-done.19.rest_1_
  68.6 1.1 %collective-permute-done.20.rest_2_ = f32[1,1024]{1,0:T(1,128)S(1)} collective-permute-done((f32[1,1024]{1,0:T(1,128)S(1)}, f32[1,1024]{1,0:T(1,128)S(1)}, u32[]{:S(2)}, u32[]{:S(2)}) %collective-permute-start.20) | collective-permute-done | bytes 4128 | tf_op jit(solution)/shard_map/ppermute | solution.py:290
  69.7 3.2 %collective-permute-done.21.rest_3_ = f32[1,1024]{1,0:T(1,128)S(1)} collective-permute-done((f32[1,1024]{1,0:T(1,128)S(1)}, f32[1,1024]{1,0:T(1,128)S(1)}, u32[]{:S(2)}, u32[]{:S(2)}) %collective-permute-start.21) | collective-permute-done | bytes 4128 | tf_op jit(solution)/shard_map/ppermute | solution.py:290
  72.9 0.0 copy-done.2
  72.9 1.1 %last.1 = f32[1,512]{1,0:T(1,128)} custom-call(s32[6]{0:T(128)S(1)} %stack.27.place, f32[1,512]{1,0:T(1,128)S(1)} %copy-done.2, f32[1,512]{1,0:T(1,128)S(1)} %get-tuple-element.19.base, f32[1,512]{1,0:T(1,128)S(1)} %collective-permute-done.17.belief1, f32[1,512]{1,0:T(1,128)S(1)} %get-tuple-element.31.belief2, ...), custom_call_target="tpu_custom_call" | custom-call | tf_op jit(solution)/shard_map/last/pallas_call | solution.py:359
  (1 shorter events, 0.0 us)
Async XLA Ops:
  0.0 2.3 %collective-permute-start = (f32[1,64,512]{2,1,0:T(8,128)}, f32[1,64,512]{2,1,0:T(8,128)S(1)}, u32[]{:S(2)}, u32[]{:S(2)}) collective-permute-start(f32[1,64,512]{2,1,0:T(8,128)} %own.1), channel_id=1, source_target_pairs={{0,32},{1,33},{2,34},{3,35},{4,36},{5,37},{6,38},{7,39},{8,40},{9,... | collective-permute-start | bytes 393224 | tf_op jit(solution)/shard_map/ppermute | solution.py:290
  0.0 2.3 %collective-permute-start.1 = (f32[1,512]{1,0:T(1,128)}, f32[1,512]{1,0:T(1,128)S(1)}, u32[]{:S(2)}, u32[]{:S(2)}) collective-permute-start(f32[1,512]{1,0:T(1,128)} %pot.1), channel_id=1, source_target_pairs={{0,32},{1,33},{2,34},{3,35},{4,36},{5,37},{6,38},{7,39},{8,40},{9,... | collective-permute-start | bytes 6152 | tf_op jit(solution)/shard_map/ppermute | solution.py:290
  0.5 0.9 %copy-start = (f32[1,64,512]{2,1,0:T(8,128)S(1)}, f32[1,64,512]{2,1,0:T(8,128)}, u32[]{:S(2)}) copy-start(f32[1,64,512]{2,1,0:T(8,128)} %own.1) | copy-start | bytes 393220
  1.4 0.7 copy-start.1
  2.9 9.1 %collective-permute-start.2 = (f32[72,512]{1,0:T(8,128)S(1)}, f32[72,512]{1,0:T(8,128)S(1)}, u32[]{:S(2)}, u32[]{:S(2)}) collective-permute-start(f32[72,512]{1,0:T(8,128)S(1)} %get-tuple-element.21), channel_id=1, source_target_pairs={{0,0},{1,1},{2,32},{3,33},{4,4},{5,5},{6,36},{7,37},{8,8},{9,9},{1... | collective-permute-start | bytes 442376 | tf_op jit(solution)/shard_map/ppermute | solution.py:290
  3.5 9.5 %collective-permute-start.3 = (f32[72,512]{1,0:T(8,128)S(1)}, f32[72,512]{1,0:T(8,128)S(1)}, u32[]{:S(2)}, u32[]{:S(2)}) collective-permute-start(f32[72,512]{1,0:T(8,128)S(1)} %get-tuple-element.21), channel_id=1, source_target_pairs={{0,1},{1,0},{2,33},{3,32},{4,5},{5,4},{6,37},{7,36},{8,9},{9,8},{1... | collective-permute-start | bytes 442376 | tf_op jit(solution)/shard_map/ppermute | solution.py:290
  5.7 9.5 %collective-permute-start.5 = (f32[72,512]{1,0:T(8,128)S(1)}, f32[72,512]{1,0:T(8,128)S(1)}, u32[]{:S(2)}, u32[]{:S(2)}) collective-permute-start(f32[72,512]{1,0:T(8,128)S(1)} %get-tuple-element.23), channel_id=1, source_target_pairs={{0,0},{1,1},{2,2},{3,3},{4,4},{5,5},{6,6},{7,7},{8,8},{9,9},{10,10... | collective-permute-start | bytes 442376 | tf_op jit(solution)/shard_map/ppermute | solution.py:290
  6.4 16.5 %collective-permute-start.6 = (f32[72,512]{1,0:T(8,128)S(1)}, f32[72,512]{1,0:T(8,128)S(1)}, u32[]{:S(2)}, u32[]{:S(2)}) collective-permute-start(f32[72,512]{1,0:T(8,128)S(1)} %get-tuple-element.23), channel_id=1, source_target_pairs={{0,8},{1,9},{2,10},{3,11},{4,12},{5,13},{6,14},{7,15},{8,16},{9,17... | collective-permute-start | bytes 442376 | tf_op jit(solution)/shard_map/ppermute | solution.py:290
  8.4 14.6 %collective-permute-start.7 = (f32[72,512]{1,0:T(8,128)S(1)}, f32[72,512]{1,0:T(8,128)S(1)}, u32[]{:S(2)}, u32[]{:S(2)}) collective-permute-start(f32[72,512]{1,0:T(8,128)S(1)} %get-tuple-element.23), channel_id=1, source_target_pairs={{0,16},{1,17},{2,18},{3,19},{4,20},{5,21},{6,22},{7,23},{8,24},{9,... | collective-permute-start | bytes 442376 | tf_op jit(solution)/shard_map/ppermute | solution.py:290
  12.0 12.5 %collective-permute-start.8 = (f32[72,512]{1,0:T(8,128)S(1)}, f32[72,512]{1,0:T(8,128)S(1)}, u32[]{:S(2)}, u32[]{:S(2)}) collective-permute-start(f32[72,512]{1,0:T(8,128)S(1)} %get-tuple-element.23), channel_id=1, source_target_pairs={{0,24},{1,25},{2,26},{3,27},{4,28},{5,29},{6,30},{7,31},{8,0},{9,1... | collective-permute-start | bytes 442376 | tf_op jit(solution)/shard_map/ppermute | solution.py:290
  13.7 25.1 %collective-permute-start.4 = (f32[72,1024]{1,0:T(8,128)S(1)}, f32[72,1024]{1,0:T(8,128)S(1)}, u32[]{:S(2)}, u32[]{:S(2)}) collective-permute-start(f32[72,1024]{1,0:T(8,128)S(1)} %get-tuple-element.22), channel_id=1, source_target_pairs={{0,64},{1,65},{2,66},{3,67},{4,68},{5,69},{6,70},{7,71},{8,72},{9,... | collective-permute-start | bytes 884744 | tf_op jit(solution)/shard_map/ppermute | solution.py:290
  15.3 12.1 %collective-permute-start.9 = (f32[72,512]{1,0:T(8,128)S(1)}, f32[72,512]{1,0:T(8,128)S(1)}, u32[]{:S(2)}, u32[]{:S(2)}) collective-permute-start(f32[72,512]{1,0:T(8,128)S(1)} %collective-permute-done.5.refs_0_.rest_0_), channel_id=1, source_target_pairs={{0,32},{1,33},{2,34},{3,35},{4,36},{5,37},{6,38},{7,39},{8,40},{9,... | collective-permute-start | bytes 442376 | tf_op jit(solution)/shard_map/ppermute | solution.py:290
  22.9 4.5 %collective-permute-start.10 = (f32[72,512]{1,0:T(8,128)S(1)}, f32[72,512]{1,0:T(8,128)S(1)}, u32[]{:S(2)}, u32[]{:S(2)}) collective-permute-start(f32[72,512]{1,0:T(8,128)S(1)} %collective-permute-done.6.refs_1_.rest_1_), channel_id=1, source_target_pairs={{0,32},{1,33},{2,34},{3,35},{4,36},{5,37},{6,38},{7,39},{8,40},{9,... | collective-permute-start | bytes 442376 | tf_op jit(solution)/shard_map/ppermute | solution.py:290
  23.0 4.4 %collective-permute-start.11 = (f32[72,512]{1,0:T(8,128)S(1)}, f32[72,512]{1,0:T(8,128)S(1)}, u32[]{:S(2)}, u32[]{:S(2)}) collective-permute-start(f32[72,512]{1,0:T(8,128)S(1)} %collective-permute-done.7.refs_2_.rest_2_), channel_id=1, source_target_pairs={{0,32},{1,33},{2,34},{3,35},{4,36},{5,37},{6,38},{7,39},{8,40},{9,... | collective-permute-start | bytes 442376 | tf_op jit(solution)/shard_map/ppermute | solution.py:290
  24.5 3.3 %collective-permute-start.12 = (f32[72,512]{1,0:T(8,128)S(1)}, f32[72,512]{1,0:T(8,128)S(1)}, u32[]{:S(2)}, u32[]{:S(2)}) collective-permute-start(f32[72,512]{1,0:T(8,128)S(1)} %collective-permute-done.8.refs_3_.rest_3_), channel_id=1, source_target_pairs={{0,32},{1,33},{2,34},{3,35},{4,36},{5,37},{6,38},{7,39},{8,40},{9,... | collective-permute-start | bytes 442376 | tf_op jit(solution)/shard_map/ppermute | solution.py:290
  28.4 9.6 %collective-permute-start.13 = (f32[1,1024]{1,0:T(1,128)S(1)}, f32[1,1024]{1,0:T(1,128)S(1)}, u32[]{:S(2)}, u32[]{:S(2)}) collective-permute-start(f32[1,1024]{1,0:T(1,128)S(1)} %first_far.1), channel_id=1, source_target_pairs={{0,64},{1,65},{2,66},{3,67},{4,68},{5,69},{6,70},{7,71},{8,72},{9,... | collective-permute-start | bytes 12296 | tf_op jit(solution)/shard_map/ppermute | solution.py:290
  33.6 4.4 %collective-permute-start.14 = (f32[1,1024]{1,0:T(1,128)S(1)}, f32[1,1024]{1,0:T(1,128)S(1)}, u32[]{:S(2)}, u32[]{:S(2)}) collective-permute-start(f32[1,1024]{1,0:T(1,128)S(1)} %first_far.1), channel_id=1, source_target_pairs={{0,65},{1,64},{2,67},{3,66},{4,69},{5,68},{6,71},{7,70},{8,73},{9,... | collective-permute-start | bytes 12296 | tf_op jit(solution)/shard_map/ppermute | solution.py:290
  33.6 4.5 %collective-permute-start.15 = (f32[1,1024]{1,0:T(1,128)S(1)}, f32[1,1024]{1,0:T(1,128)S(1)}, u32[]{:S(2)}, u32[]{:S(2)}) collective-permute-start(f32[1,1024]{1,0:T(1,128)S(1)} %first_far.1), channel_id=1, source_target_pairs={{0,66},{1,67},{2,64},{3,65},{4,70},{5,71},{6,68},{7,69},{8,74},{9,... | collective-permute-start | bytes 12296 | tf_op jit(solution)/shard_map/ppermute | solution.py:290
  33.6 5.2 %collective-permute-start.16 = (f32[1,1024]{1,0:T(1,128)S(1)}, f32[1,1024]{1,0:T(1,128)S(1)}, u32[]{:S(2)}, u32[]{:S(2)}) collective-permute-start(f32[1,1024]{1,0:T(1,128)S(1)} %first_far.1), channel_id=1, source_target_pairs={{0,67},{1,66},{2,65},{3,64},{4,71},{5,70},{6,69},{7,68},{8,75},{9,... | collective-permute-start | bytes 12296 | tf_op jit(solution)/shard_map/ppermute | solution.py:290
  43.6 29.2 %copy-start.2 = (f32[1,512]{1,0:T(1,128)S(1)}, f32[1,512]{1,0:T(1,128)}, u32[]{:S(2)}) copy-start(f32[1,512]{1,0:T(1,128)} %pot.1) | copy-start | bytes 6148
  43.6 14.1 %all-to-all-start = ((f32[16,32,128]{2,1,0:T(8,128)}), f32[16,32,128]{2,1,0:T(8,128)S(1)}, u32[]{:S(2)}, u32[]{:S(2)}) async-start(f32[16,32,128]{2,1,0:T(8,128)} %get-tuple-element.26), calls=%async_computation | async-start | bytes 524288 | tf_op jit(solution)/shard_map/all_to_all | solution.py:345
  48.2 3.1 %collective-permute-start.17 = (f32[1,512]{1,0:T(1,128)S(1)}, f32[1,512]{1,0:T(1,128)S(1)}, u32[]{:S(2)}, u32[]{:S(2)}) collective-permute-start(f32[1,512]{1,0:T(1,128)S(1)} %get-tuple-element.27), channel_id=1, source_target_pairs={{0,96},{1,97},{2,66},{3,67},{4,100},{5,101},{6,70},{7,71},{8,104},... | collective-permute-start | bytes 6152 | tf_op jit(solution)/shard_map/ppermute | solution.py:290
  61.8 6.7 %collective-permute-start.18 = (f32[1,1024]{1,0:T(1,128)S(1)}, f32[1,1024]{1,0:T(1,128)S(1)}, u32[]{:S(2)}, u32[]{:S(2)}) collective-permute-start(f32[1,1024]{1,0:T(1,128)S(1)} %get-tuple-element.32), channel_id=1, source_target_pairs={{0,32},{1,33},{2,2},{3,3},{4,36},{5,37},{6,6},{7,7},{8,40},{9,41},... | collective-permute-start | bytes 12296 | tf_op jit(solution)/shard_map/ppermute | solution.py:290
  63.8 4.8 %collective-permute-start.19 = (f32[1,1024]{1,0:T(1,128)S(1)}, f32[1,1024]{1,0:T(1,128)S(1)}, u32[]{:S(2)}, u32[]{:S(2)}) collective-permute-start(f32[1,1024]{1,0:T(1,128)S(1)} %get-tuple-element.32), channel_id=1, source_target_pairs={{0,33},{1,32},{2,3},{3,2},{4,37},{5,36},{6,7},{7,6},{8,41},{9,40},... | collective-permute-start | bytes 12296 | tf_op jit(solution)/shard_map/ppermute | solution.py:290
  66.6 3.0 %collective-permute-start.20 = (f32[1,1024]{1,0:T(1,128)S(1)}, f32[1,1024]{1,0:T(1,128)S(1)}, u32[]{:S(2)}, u32[]{:S(2)}) collective-permute-start(f32[1,1024]{1,0:T(1,128)S(1)} %get-tuple-element.32), channel_id=1, source_target_pairs={{0,2},{1,3},{2,32},{3,33},{4,6},{5,7},{6,36},{7,37},{8,10},{9,11},... | collective-permute-start | bytes 12296 | tf_op jit(solution)/shard_map/ppermute | solution.py:290
  67.4 5.4 %collective-permute-start.21 = (f32[1,1024]{1,0:T(1,128)S(1)}, f32[1,1024]{1,0:T(1,128)S(1)}, u32[]{:S(2)}, u32[]{:S(2)}) collective-permute-start(f32[1,1024]{1,0:T(1,128)S(1)} %get-tuple-element.32), channel_id=1, source_target_pairs={{0,3},{1,2},{2,33},{3,32},{4,7},{5,6},{6,37},{7,36},{8,11},{9,10},... | collective-permute-start | bytes 12296 | tf_op jit(solution)/shard_map/ppermute | solution.py:290

commit v4 on v3

--- a/solution.py
+++ b/solution.py
@@ -143,12 +143,24 @@
     base[...] = own_pot[...] - square(own[0]) - offset
 
 
-def pick_kernel(place, own, other, other_pot, source, target):
+def pick_kernel(place, own, other, other_pot, part, target):
     first = place[1] == 0
     dims, n = other.shape[1:]
-    theirs = jnp.concatenate([other[0], jnp.broadcast_to(other_pot[...], (8, n))], axis=0)
-    source[...] = jnp.where(first, own[...], theirs)
-    target[...] = jnp.where(first, theirs, own[...])
+    half = n // 2
+    at = pl.multiple_of(place[1] * half, half)
+    part[0:dims, :] = jnp.where(first, own[0:dims, pl.ds(at, half)], other[0, :, pl.ds(at, half)])
+    part[dims:, :] = jnp.where(
+        first, own[dims:, pl.ds(at, half)], jnp.broadcast_to(other_pot[:, pl.ds(at, half)], (8, half))
+    )
+    target[0:dims, :] = jnp.where(first, other[0], own[0:dims, :])
+    target[dims:, :] = jnp.where(first, jnp.broadcast_to(other_pot[...], (8, n)), own[dims:, :])
+
+
+def join_kernel(place, own, other, out):
+    half = own.shape[1]
+    first = place[5] == 0
+    out[:, 0:half] = jnp.where(first, own[...], other[...])
+    out[:, half:] = jnp.where(first, other[...], own[...])
 
 
 def order_kernel(place, own, other, out, operand):
@@ -190,8 +202,7 @@
     def _():
         for k, c in enumerate(cols):
             depth = lax.rem(place[4] + DEPTHS - k % DEPTHS, DEPTHS)
-            high_y = lax.rem(place[5] + place[1] + k // DEPTHS, 2)
-            at = 2 * depth + high_y
+            at = 2 * depth + lax.rem(place[1] + k // DEPTHS, 2)
             x = c[0:dims, :]
             high, low = halves(x)
             out[at, :, :] = jnp.concatenate([high, low, high], axis=0)
@@ -250,7 +261,10 @@
             return jnp.concatenate(parts, axis=1)
 
         out[...] = over_columns(rows[...], chunk, blocks // 2, 2 * width, (one, two), top, total)
-        belief[...] = final[pl.ds(2 * place[4] + place[5], 1), :]
+        half = width // 2
+        for side in (0, 1):
+            line = final[pl.ds(2 * place[4] + side, 1), :]
+            belief[:, side * half : (side + 1) * half] = jnp.where(place[5] == 0, line[:, 0:half], line[:, half:])
 
 
 def last_kernel(place, pot, base, belief1, belief2, *rest):
@@ -308,15 +322,18 @@
         compiler_params=params(),
         name="pack",
     )(coords, potentials)
-    source, target = call(pick_kernel, "pick", [arr(tall, n)] * 2, 4)(
+    half, target = call(pick_kernel, "pick", [arr(tall, n // 2), arr(tall, n)], 4)(
         place, own, swapped(coords), swapped(potentials)
     )
     sides = [
         sent(target, lambda l, c, z, f, y, h: (l, y, z, f, c, h)),
         sent(target, lambda l, c, z, f, y, h: (l, y, z, f, c, 1 - h)),
     ]
-    near = [
-        sent(source, lambda l, c, z, f, y, h, d=d: (l, c, (z + d) % DEPTHS, f ^ c, y, h)) for d in range(DEPTHS)
+    joined = call(join_kernel, "join", arr(tall, n), 3)(
+        place, half, sent(half, lambda l, c, z, f, y, h: (l, c, z, 1 - f, y, h))
+    )
+    near = [joined] + [
+        sent(joined, lambda l, c, z, f, y, h, d=d: (l, c, (z + d) % DEPTHS, f, y, h)) for d in range(1, DEPTHS)
     ]
     rows, operand = call(order_kernel, "order", [arr(tall, 2 * n), arr(2 * n, 4 * dims, dtype=BF16)], 3)(place, *sides)
     rows1 = sent(rows, lambda l, c, z, f, y, h: (1 - l, c, z, f, y, h))

time: 74.3 us -> 76.5 us (1.030)
  waiting for transfers between devices: 15 us -> 22 us
  starting transfers between devices: 43.9 us -> 37.7 us
    ppermute x22, starting transfers between devices: 39.3 us -> 31.5 us  [sent(): return lax.ppermute(x, ('tm', 'cell'), moves(to))]
    ppermute x22, waiting for transfers between devices: 8.55 us -> 15.6 us  [sent(): return lax.ppermute(x, ('tm', 'cell'), moves(to))]
    all_to_all x1, starting transfers between devices: 4.56 us -> 6.23 us  [body(): lax.all_to_all(mine, ('tm', 'cell'), 0, 0, axis_index_groups=sixteen, til...]
  transfers between devices with their start and end apart: 23 -> 23, of which waited for: 7 -> 10; matrix products, arithmetic and copies ran while one was open for 0% -> 0% of each run, Pallas kernels for 4% -> 4%
where the time goes in v4:
time: 76.5 us; the launch traced here: 75.5 us
  starting transfers between devices  37.7 us (49%)
  waiting for transfers between devices  22 us (29%)
  Pallas kernels  13.9 us (18%)
  local copies, waits for them, and re-layouts  1.67 us (2%)
    ppermute x22, starting transfers between devices, sent(): return lax.ppermute(x, ('tm', 'cell'), moves(to))  31.5 us
    ppermute x22, waiting for transfers between devices, sent(): return lax.ppermute(x, ('tm', 'cell'), moves(to))  15.6 us
    all_to_all x1, waiting for transfers between devices, body(): lax.all_to_all(mine, ('tm', 'cell'), 0, 0, axis_index_groups=sixteen, til...  6.4 us
    all_to_all x1, starting transfers between devices, body(): lax.all_to_all(mine, ('tm', 'cell'), 0, 0, axis_index_groups=sixteen, til...  6.23 us
    pallas_call x1, Pallas kernels, body(): call(functools.partial(second_kernel, offset), 'second', [arr(1, n), arr(...  4.84 us
    pallas_call x1, Pallas kernels, body(): call(functools.partial(third_kernel, offset), 'third', [arr(1, n), arr(1,...  4.14 us
    unnamed x6, local copies, waits for them, and re-layouts  1.59 us
  transfers between devices with their start and end apart: 23, of which 10 were waited for; matrix products, arithmetic and copies ran while one was open for 0% of the time, Pallas kernels for 4%

profile of v4, /device:TPU:2, one launch (start us, length us, event | category | flops | bytes accessed | tf_op | source)
XLA Modules:
  0.0 75.5 jit_solution(17011583541641269094)
XLA Ops:
  0.0 0.0 collective-permute-start
  0.0 0.5 collective-permute-start.1
  0.5 0.0 copy-start
  0.5 0.9 %copy-done = f32[1,64,512]{2,1,0:T(8,128)S(1)} copy-done((f32[1,64,512]{2,1,0:T(8,128)S(1)}, f32[1,64,512]{2,1,0:T(8,128)}, u32[]{:S(2)}) %copy-start) | copy-done | bytes 131096
  1.4 0.0 copy-start.1
  1.4 0.7 copy-done.1
  2.2 0.1 stack.27.place
  2.3 0.0 collective-permute-done.1.other_pot
  2.3 0.0 collective-permute-done.other
  2.3 0.6 pick.1
  2.9 0.7 collective-permute-start.2
  3.5 2.2 %collective-permute-start.3 = (f32[72,512]{1,0:T(8,128)S(1)}, f32[72,512]{1,0:T(8,128)S(1)}, u32[]{:S(2)}, u32[]{:S(2)}) collective-permute-start(f32[72,512]{1,0:T(8,128)S(1)} %get-tuple-element.21), channel_id=1, source_target_pairs={{0,1},{1,0},{2,33},{3,32},{4,5},{5,4},{6,37},{7,36},{8,9},{9,8},{1... | collective-permute-start | bytes 442376 | tf_op jit(solution)/shard_map/ppermute | solution.py:304
  5.7 3.2 %collective-permute-start.5 = (f32[72,256]{1,0:T(8,128)S(1)}, f32[72,256]{1,0:T(8,128)S(1)}, u32[]{:S(2)}, u32[]{:S(2)}) collective-permute-start(f32[72,256]{1,0:T(8,128)S(1)} %get-tuple-element.23.own), channel_id=1, source_target_pairs={{0,4},{1,5},{2,6},{3,7},{4,0},{5,1},{6,2},{7,3},{8,12},{9,13},{10,... | collective-permute-start | bytes 221192 | tf_op jit(solution)/shard_map/ppermute | solution.py:304
  8.9 3.4 %collective-permute-done.5.other = f32[72,256]{1,0:T(8,128)S(1)} collective-permute-done((f32[72,256]{1,0:T(8,128)S(1)}, f32[72,256]{1,0:T(8,128)S(1)}, u32[]{:S(2)}, u32[]{:S(2)}) %collective-permute-start.5) | collective-permute-done | bytes 73760 | tf_op jit(solution)/shard_map/ppermute | solution.py:304
  12.3 0.6 join.1.refs_0_.rest_0_
  12.9 2.0 %collective-permute-start.6 = (f32[72,512]{1,0:T(8,128)S(1)}, f32[72,512]{1,0:T(8,128)S(1)}, u32[]{:S(2)}, u32[]{:S(2)}) collective-permute-start(f32[72,512]{1,0:T(8,128)S(1)} %join.1.refs_0_.rest_0_), channel_id=1, source_target_pairs={{0,8},{1,9},{2,10},{3,11},{4,12},{5,13},{6,14},{7,15},{8,16},{9,17... | collective-permute-start | bytes 442376 | tf_op jit(solution)/shard_map/ppermute | solution.py:304
  14.9 3.6 %collective-permute-start.7 = (f32[72,512]{1,0:T(8,128)S(1)}, f32[72,512]{1,0:T(8,128)S(1)}, u32[]{:S(2)}, u32[]{:S(2)}) collective-permute-start(f32[72,512]{1,0:T(8,128)S(1)} %join.1.refs_0_.rest_0_), channel_id=1, source_target_pairs={{0,16},{1,17},{2,18},{3,19},{4,20},{5,21},{6,22},{7,23},{8,24},{9,... | collective-permute-start | bytes 442376 | tf_op jit(solution)/shard_map/ppermute | solution.py:304
  18.5 1.0 %collective-permute-start.8 = (f32[72,512]{1,0:T(8,128)S(1)}, f32[72,512]{1,0:T(8,128)S(1)}, u32[]{:S(2)}, u32[]{:S(2)}) collective-permute-start(f32[72,512]{1,0:T(8,128)S(1)} %join.1.refs_0_.rest_0_), channel_id=1, source_target_pairs={{0,24},{1,25},{2,26},{3,27},{4,28},{5,29},{6,30},{7,31},{8,0},{9,1... | collective-permute-start | bytes 442376 | tf_op jit(solution)/shard_map/ppermute | solution.py:304
  19.5 0.0 collective-permute-done.2.own
  19.5 0.0 collective-permute-done.3.other
  19.5 0.8 order.1
  20.2 0.8 %collective-permute-start.4 = (f32[72,1024]{1,0:T(8,128)S(1)}, f32[72,1024]{1,0:T(8,128)S(1)}, u32[]{:S(2)}, u32[]{:S(2)}) collective-permute-start(f32[72,1024]{1,0:T(8,128)S(1)} %get-tuple-element.22), channel_id=1, source_target_pairs={{0,64},{1,65},{2,66},{3,67},{4,68},{5,69},{6,70},{7,71},{8,72},{9,... | collective-permute-start | bytes 884744 | tf_op jit(solution)/shard_map/ppermute | solution.py:304
  21.1 1.6 %collective-permute-start.9 = (f32[72,512]{1,0:T(8,128)S(1)}, f32[72,512]{1,0:T(8,128)S(1)}, u32[]{:S(2)}, u32[]{:S(2)}) collective-permute-start(f32[72,512]{1,0:T(8,128)S(1)} %join.1.refs_0_.rest_0_), channel_id=1, source_target_pairs={{0,32},{1,33},{2,34},{3,35},{4,36},{5,37},{6,38},{7,39},{8,40},{9,... | collective-permute-start | bytes 442376 | tf_op jit(solution)/shard_map/ppermute | solution.py:304
  22.6 0.0 collective-permute-done.6.refs_1_.rest_1_
  22.6 0.0 collective-permute-start.10
  22.6 2.2 %collective-permute-done.7.refs_2_.rest_2_ = f32[72,512]{1,0:T(8,128)S(1)} collective-permute-done((f32[72,512]{1,0:T(8,128)S(1)}, f32[72,512]{1,0:T(8,128)S(1)}, u32[]{:S(2)}, u32[]{:S(2)}) %collective-permute-start.7) | collective-permute-done | bytes 147488 | tf_op jit(solution)/shard_map/ppermute | solution.py:304
  24.8 1.3 %collective-permute-start.11 = (f32[72,512]{1,0:T(8,128)S(1)}, f32[72,512]{1,0:T(8,128)S(1)}, u32[]{:S(2)}, u32[]{:S(2)}) collective-permute-start(f32[72,512]{1,0:T(8,128)S(1)} %collective-permute-done.7.refs_2_.rest_2_), channel_id=1, source_target_pairs={{0,32},{1,33},{2,34},{3,35},{4,36},{5,37},{6,38},{7,39},{8,40},{9,... | collective-permute-start | bytes 442376 | tf_op jit(solution)/shard_map/ppermute | solution.py:304
  26.1 0.0 collective-permute-done.8.refs_3_.rest_3_
  26.1 0.0 collective-permute-start.12
  26.1 0.6 first.1.rest_4_
  26.7 0.0 collective-permute-done.9.refs_4_.rest_0_
  26.7 0.0 collective-permute-done.10.refs_5_.rest_1_
  26.7 0.4 collective-permute-done.11.refs_6_.rest_2_
  27.1 0.4 collective-permute-done.12.refs_7_.rest_3_
  27.5 0.6 first_far.1
  28.1 4.2 %collective-permute-start.13 = (f32[1,1024]{1,0:T(1,128)S(1)}, f32[1,1024]{1,0:T(1,128)S(1)}, u32[]{:S(2)}, u32[]{:S(2)}) collective-permute-start(f32[1,1024]{1,0:T(1,128)S(1)} %first_far.1), channel_id=1, source_target_pairs={{0,64},{1,65},{2,66},{3,67},{4,68},{5,69},{6,70},{7,71},{8,72},{9,... | collective-permute-start | bytes 12296 | tf_op jit(solution)/shard_map/ppermute | solution.py:304
  32.3 0.0 collective-permute-start.14
  32.3 3.3 %collective-permute-start.15 = (f32[1,1024]{1,0:T(1,128)S(1)}, f32[1,1024]{1,0:T(1,128)S(1)}, u32[]{:S(2)}, u32[]{:S(2)}) collective-permute-start(f32[1,1024]{1,0:T(1,128)S(1)} %first_far.1), channel_id=1, source_target_pairs={{0,66},{1,67},{2,64},{3,65},{4,70},{5,71},{6,68},{7,69},{8,74},{9,... | collective-permute-start | bytes 12296 | tf_op jit(solution)/shard_map/ppermute | solution.py:304
  35.6 0.3 collective-permute-start.16
  35.9 0.8 %split.1 = (bf16[8,192,512]{2,1,0:T(8,128)(2,1)S(1)}, f32[8,8,512]{2,1,0:T(8,128)S(1)}) custom-call(s32[6]{0:T(128)S(1)} %stack.27.place, f32[72,512]{1,0:T(8,128)S(1)} %join.1.refs_0_.rest_0_, f32[72,512]{1,0:T(8,128)S(1)} %collective-permute-done.6.refs_1_.rest_1_, f32[72,512]{1,0:T(8,128)S(1)} %collective-permute-done.7.refs_2_.rest_2_, ...), custom_call_target="tpu_custom_call" | custom-call | tf_op jit(solution)/shard_map/split/pallas_call | solution.py:349
  36.7 0.0 collective-permute-done.13.rest_0_
  36.7 0.0 collective-permute-done.14.rest_1_
  36.7 0.5 collective-permute-done.15.rest_2_
  37.2 2.9 %collective-permute-done.16.rest_3_ = f32[1,1024]{1,0:T(1,128)S(1)} collective-permute-done((f32[1,1024]{1,0:T(1,128)S(1)}, f32[1,1024]{1,0:T(1,128)S(1)}, u32[]{:S(2)}, u32[]{:S(2)}) %collective-permute-start.16) | collective-permute-done | bytes 4128 | tf_op jit(solution)/shard_map/ppermute | solution.py:304
  40.1 0.0 collective-permute-done.4.rows
  40.1 4.8 %second.1 = (f32[1,512]{1,0:T(1,128)S(1)}, f32[16,32,128]{2,1,0:T(8,128)}) custom-call(s32[6]{0:T(128)S(1)} %stack.27.place, f32[72,1024]{1,0:T(8,128)S(1)} %collective-permute-done.4.rows, bf16[8,192,512]{2,1,0:T(8,128)(2,1)S(1)} %get-tuple-element.24.cols, f32[1,1024]{1,0:T(1,128)S(1)} %collective-permute-done.13.rest_0_, ...), custom_call_target="tpu_custom_call" | custom-call | tf_op jit(solution)/shard_map/second/pallas_call | solution.py:352
  44.9 0.0 copy-start.2
  44.9 6.2 %all-to-all-start = ((f32[16,32,128]{2,1,0:T(8,128)}), f32[16,32,128]{2,1,0:T(8,128)S(1)}, u32[]{:S(2)}, u32[]{:S(2)}) async-start(f32[16,32,128]{2,1,0:T(8,128)} %get-tuple-element.26), calls=%async_computation | async-start | bytes 524288 | tf_op jit(solution)/shard_map/all_to_all | solution.py:362
  51.2 0.1 collective-permute-start.17
  51.3 3.0 %collective-permute-done.17.belief1 = f32[1,512]{1,0:T(1,128)S(1)} collective-permute-done((f32[1,512]{1,0:T(1,128)S(1)}, f32[1,512]{1,0:T(1,128)S(1)}, u32[]{:S(2)}, u32[]{:S(2)}) %collective-permute-start.17) | collective-permute-done | bytes 2080 | tf_op jit(solution)/shard_map/ppermute | solution.py:304
  54.3 6.4 %all-to-all-done.came = f32[16,32,128]{2,1,0:T(8,128)S(1)} async-done(((f32[16,32,128]{2,1,0:T(8,128)}), f32[16,32,128]{2,1,0:T(8,128)S(1)}, u32[]{:S(2)}, u32[]{:S(2)}) %all-to-all-start) | async-done | bytes 262176 | tf_op jit(solution)/shard_map/all_to_all | solution.py:362
  60.7 4.1 %third.1 = (f32[1,512]{1,0:T(1,128)S(1)}, f32[1,1024]{1,0:T(1,128)S(1)}) custom-call(s32[6]{0:T(128)S(1)} %stack.27.place, bf16[1024,256]{1,0:T(8,128)(2,1)S(1)} %get-tuple-element.25.rows, bf16[8,192,512]{2,1,0:T(8,128)(2,1)S(1)} %get-tuple-element.24.cols, f32[8,8,512]{2,1,0:T(8,128)S(1)} %get-tuple-element.29.extra, f32[16,32,128]{2,1,0:T(8,128)S(1)} %all-to-all-done.came), custom_call_target="tpu_custom_call" | custom-call | tf_op jit(solution)/shard_map/third/pallas_call | solution.py:364
  64.8 1.9 %collective-permute-start.18 = (f32[1,1024]{1,0:T(1,128)S(1)}, f32[1,1024]{1,0:T(1,128)S(1)}, u32[]{:S(2)}, u32[]{:S(2)}) collective-permute-start(f32[1,1024]{1,0:T(1,128)S(1)} %get-tuple-element.32), channel_id=1, source_target_pairs={{0,32},{1,33},{2,2},{3,3},{4,36},{5,37},{6,6},{7,7},{8,40},{9,41},... | collective-permute-start | bytes 12296 | tf_op jit(solution)/shard_map/ppermute | solution.py:304
  66.7 2.2 %collective-permute-start.19 = (f32[1,1024]{1,0:T(1,128)S(1)}, f32[1,1024]{1,0:T(1,128)S(1)}, u32[]{:S(2)}, u32[]{:S(2)}) collective-permute-start(f32[1,1024]{1,0:T(1,128)S(1)} %get-tuple-element.32), channel_id=1, source_target_pairs={{0,33},{1,32},{2,3},{3,2},{4,37},{5,36},{6,7},{7,6},{8,41},{9,40},... | collective-permute-start | bytes 12296 | tf_op jit(solution)/shard_map/ppermute | solution.py:304
  69.0 0.0 collective-permute-start.20
  69.0 2.6 %collective-permute-start.21 = (f32[1,1024]{1,0:T(1,128)S(1)}, f32[1,1024]{1,0:T(1,128)S(1)}, u32[]{:S(2)}, u32[]{:S(2)}) collective-permute-start(f32[1,1024]{1,0:T(1,128)S(1)} %get-tuple-element.32), channel_id=1, source_target_pairs={{0,3},{1,2},{2,33},{3,32},{4,7},{5,6},{6,37},{7,36},{8,11},{9,10},... | collective-permute-start | bytes 12296 | tf_op jit(solution)/shard_map/ppermute | solution.py:304
  71.5 0.0 collective-permute-done.18.rest_0_
  71.5 0.0 collective-permute-done.19.rest_1_
  71.5 0.5 collective-permute-done.20.rest_2_
  72.0 2.4 %collective-permute-done.21.rest_3_ = f32[1,1024]{1,0:T(1,128)S(1)} collective-permute-done((f32[1,1024]{1,0:T(1,128)S(1)}, f32[1,1024]{1,0:T(1,128)S(1)}, u32[]{:S(2)}, u32[]{:S(2)}) %collective-permute-start.21) | collective-permute-done | bytes 4128 | tf_op jit(solution)/shard_map/ppermute | solution.py:304
  74.4 0.0 copy-done.2
  74.4 1.1 %last.1 = f32[1,512]{1,0:T(1,128)} custom-call(s32[6]{0:T(128)S(1)} %stack.27.place, f32[1,512]{1,0:T(1,128)S(1)} %copy-done.2, f32[1,512]{1,0:T(1,128)S(1)} %get-tuple-element.19.base, f32[1,512]{1,0:T(1,128)S(1)} %collective-permute-done.17.belief1, f32[1,512]{1,0:T(1,128)S(1)} %get-tuple-element.31.belief2, ...), custom_call_target="tpu_custom_call" | custom-call | tf_op jit(solution)/shard_map/last/pallas_call | solution.py:376
  (1 shorter events, 0.0 us)
Async XLA Ops:
  0.0 2.3 %collective-permute-start = (f32[1,64,512]{2,1,0:T(8,128)}, f32[1,64,512]{2,1,0:T(8,128)S(1)}, u32[]{:S(2)}, u32[]{:S(2)}) collective-permute-start(f32[1,64,512]{2,1,0:T(8,128)} %own.1), channel_id=1, source_target_pairs={{0,32},{1,33},{2,34},{3,35},{4,36},{5,37},{6,38},{7,39},{8,40},{9,... | collective-permute-start | bytes 393224 | tf_op jit(solution)/shard_map/ppermute | solution.py:304
  0.0 2.3 %collective-permute-start.1 = (f32[1,512]{1,0:T(1,128)}, f32[1,512]{1,0:T(1,128)S(1)}, u32[]{:S(2)}, u32[]{:S(2)}) collective-permute-start(f32[1,512]{1,0:T(1,128)} %pot.1), channel_id=1, source_target_pairs={{0,32},{1,33},{2,34},{3,35},{4,36},{5,37},{6,38},{7,39},{8,40},{9,... | collective-permute-start | bytes 6152 | tf_op jit(solution)/shard_map/ppermute | solution.py:304
  0.5 0.9 %copy-start = (f32[1,64,512]{2,1,0:T(8,128)S(1)}, f32[1,64,512]{2,1,0:T(8,128)}, u32[]{:S(2)}) copy-start(f32[1,64,512]{2,1,0:T(8,128)} %own.1) | copy-start | bytes 393220
  1.4 0.7 copy-start.1
  2.9 16.6 %collective-permute-start.2 = (f32[72,512]{1,0:T(8,128)S(1)}, f32[72,512]{1,0:T(8,128)S(1)}, u32[]{:S(2)}, u32[]{:S(2)}) collective-permute-start(f32[72,512]{1,0:T(8,128)S(1)} %get-tuple-element.21), channel_id=1, source_target_pairs={{0,0},{1,1},{2,32},{3,33},{4,4},{5,5},{6,36},{7,37},{8,8},{9,9},{1... | collective-permute-start | bytes 442376 | tf_op jit(solution)/shard_map/ppermute | solution.py:304
  3.5 15.9 %collective-permute-start.3 = (f32[72,512]{1,0:T(8,128)S(1)}, f32[72,512]{1,0:T(8,128)S(1)}, u32[]{:S(2)}, u32[]{:S(2)}) collective-permute-start(f32[72,512]{1,0:T(8,128)S(1)} %get-tuple-element.21), channel_id=1, source_target_pairs={{0,1},{1,0},{2,33},{3,32},{4,5},{5,4},{6,37},{7,36},{8,9},{9,8},{1... | collective-permute-start | bytes 442376 | tf_op jit(solution)/shard_map/ppermute | solution.py:304
  5.7 6.6 %collective-permute-start.5 = (f32[72,256]{1,0:T(8,128)S(1)}, f32[72,256]{1,0:T(8,128)S(1)}, u32[]{:S(2)}, u32[]{:S(2)}) collective-permute-start(f32[72,256]{1,0:T(8,128)S(1)} %get-tuple-element.23.own), channel_id=1, source_target_pairs={{0,4},{1,5},{2,6},{3,7},{4,0},{5,1},{6,2},{7,3},{8,12},{9,13},{10,... | collective-permute-start | bytes 221192 | tf_op jit(solution)/shard_map/ppermute | solution.py:304
  12.9 9.7 %collective-permute-start.6 = (f32[72,512]{1,0:T(8,128)S(1)}, f32[72,512]{1,0:T(8,128)S(1)}, u32[]{:S(2)}, u32[]{:S(2)}) collective-permute-start(f32[72,512]{1,0:T(8,128)S(1)} %join.1.refs_0_.rest_0_), channel_id=1, source_target_pairs={{0,8},{1,9},{2,10},{3,11},{4,12},{5,13},{6,14},{7,15},{8,16},{9,17... | collective-permute-start | bytes 442376 | tf_op jit(solution)/shard_map/ppermute | solution.py:304
  14.9 9.9 %collective-permute-start.7 = (f32[72,512]{1,0:T(8,128)S(1)}, f32[72,512]{1,0:T(8,128)S(1)}, u32[]{:S(2)}, u32[]{:S(2)}) collective-permute-start(f32[72,512]{1,0:T(8,128)S(1)} %join.1.refs_0_.rest_0_), channel_id=1, source_target_pairs={{0,16},{1,17},{2,18},{3,19},{4,20},{5,21},{6,22},{7,23},{8,24},{9,... | collective-permute-start | bytes 442376 | tf_op jit(solution)/shard_map/ppermute | solution.py:304
  18.5 7.7 %collective-permute-start.8 = (f32[72,512]{1,0:T(8,128)S(1)}, f32[72,512]{1,0:T(8,128)S(1)}, u32[]{:S(2)}, u32[]{:S(2)}) collective-permute-start(f32[72,512]{1,0:T(8,128)S(1)} %join.1.refs_0_.rest_0_), channel_id=1, source_target_pairs={{0,24},{1,25},{2,26},{3,27},{4,28},{5,29},{6,30},{7,31},{8,0},{9,1... | collective-permute-start | bytes 442376 | tf_op jit(solution)/shard_map/ppermute | solution.py:304
  20.2 19.9 %collective-permute-start.4 = (f32[72,1024]{1,0:T(8,128)S(1)}, f32[72,1024]{1,0:T(8,128)S(1)}, u32[]{:S(2)}, u32[]{:S(2)}) collective-permute-start(f32[72,1024]{1,0:T(8,128)S(1)} %get-tuple-element.22), channel_id=1, source_target_pairs={{0,64},{1,65},{2,66},{3,67},{4,68},{5,69},{6,70},{7,71},{8,72},{9,... | collective-permute-start | bytes 884744 | tf_op jit(solution)/shard_map/ppermute | solution.py:304
  21.1 5.6 %collective-permute-start.9 = (f32[72,512]{1,0:T(8,128)S(1)}, f32[72,512]{1,0:T(8,128)S(1)}, u32[]{:S(2)}, u32[]{:S(2)}) collective-permute-start(f32[72,512]{1,0:T(8,128)S(1)} %join.1.refs_0_.rest_0_), channel_id=1, source_target_pairs={{0,32},{1,33},{2,34},{3,35},{4,36},{5,37},{6,38},{7,39},{8,40},{9,... | collective-permute-start | bytes 442376 | tf_op jit(solution)/shard_map/ppermute | solution.py:304
  22.6 4.1 %collective-permute-start.10 = (f32[72,512]{1,0:T(8,128)S(1)}, f32[72,512]{1,0:T(8,128)S(1)}, u32[]{:S(2)}, u32[]{:S(2)}) collective-permute-start(f32[72,512]{1,0:T(8,128)S(1)} %collective-permute-done.6.refs_1_.rest_1_), channel_id=1, source_target_pairs={{0,32},{1,33},{2,34},{3,35},{4,36},{5,37},{6,38},{7,39},{8,40},{9,... | collective-permute-start | bytes 442376 | tf_op jit(solution)/shard_map/ppermute | solution.py:304
  24.8 2.3 %collective-permute-start.11 = (f32[72,512]{1,0:T(8,128)S(1)}, f32[72,512]{1,0:T(8,128)S(1)}, u32[]{:S(2)}, u32[]{:S(2)}) collective-permute-start(f32[72,512]{1,0:T(8,128)S(1)} %collective-permute-done.7.refs_2_.rest_2_), channel_id=1, source_target_pairs={{0,32},{1,33},{2,34},{3,35},{4,36},{5,37},{6,38},{7,39},{8,40},{9,... | collective-permute-start | bytes 442376 | tf_op jit(solution)/shard_map/ppermute | solution.py:304
  26.1 1.4 %collective-permute-start.12 = (f32[72,512]{1,0:T(8,128)S(1)}, f32[72,512]{1,0:T(8,128)S(1)}, u32[]{:S(2)}, u32[]{:S(2)}) collective-permute-start(f32[72,512]{1,0:T(8,128)S(1)} %collective-permute-done.8.refs_3_.rest_3_), channel_id=1, source_target_pairs={{0,32},{1,33},{2,34},{3,35},{4,36},{5,37},{6,38},{7,39},{8,40},{9,... | collective-permute-start | bytes 442376 | tf_op jit(solution)/shard_map/ppermute | solution.py:304
  28.1 8.6 %collective-permute-start.13 = (f32[1,1024]{1,0:T(1,128)S(1)}, f32[1,1024]{1,0:T(1,128)S(1)}, u32[]{:S(2)}, u32[]{:S(2)}) collective-permute-start(f32[1,1024]{1,0:T(1,128)S(1)} %first_far.1), channel_id=1, source_target_pairs={{0,64},{1,65},{2,66},{3,67},{4,68},{5,69},{6,70},{7,71},{8,72},{9,... | collective-permute-start | bytes 12296 | tf_op jit(solution)/shard_map/ppermute | solution.py:304
  32.3 4.4 %collective-permute-start.14 = (f32[1,1024]{1,0:T(1,128)S(1)}, f32[1,1024]{1,0:T(1,128)S(1)}, u32[]{:S(2)}, u32[]{:S(2)}) collective-permute-start(f32[1,1024]{1,0:T(1,128)S(1)} %first_far.1), channel_id=1, source_target_pairs={{0,65},{1,64},{2,67},{3,66},{4,69},{5,68},{6,71},{7,70},{8,73},{9,... | collective-permute-start | bytes 12296 | tf_op jit(solution)/shard_map/ppermute | solution.py:304
  32.3 4.9 %collective-permute-start.15 = (f32[1,1024]{1,0:T(1,128)S(1)}, f32[1,1024]{1,0:T(1,128)S(1)}, u32[]{:S(2)}, u32[]{:S(2)}) collective-permute-start(f32[1,1024]{1,0:T(1,128)S(1)} %first_far.1), channel_id=1, source_target_pairs={{0,66},{1,67},{2,64},{3,65},{4,70},{5,71},{6,68},{7,69},{8,74},{9,... | collective-permute-start | bytes 12296 | tf_op jit(solution)/shard_map/ppermute | solution.py:304
  35.6 4.5 %collective-permute-start.16 = (f32[1,1024]{1,0:T(1,128)S(1)}, f32[1,1024]{1,0:T(1,128)S(1)}, u32[]{:S(2)}, u32[]{:S(2)}) collective-permute-start(f32[1,1024]{1,0:T(1,128)S(1)} %first_far.1), channel_id=1, source_target_pairs={{0,67},{1,66},{2,65},{3,64},{4,71},{5,70},{6,69},{7,68},{8,75},{9,... | collective-permute-start | bytes 12296 | tf_op jit(solution)/shard_map/ppermute | solution.py:304
  44.9 29.5 %copy-start.2 = (f32[1,512]{1,0:T(1,128)S(1)}, f32[1,512]{1,0:T(1,128)}, u32[]{:S(2)}) copy-start(f32[1,512]{1,0:T(1,128)} %pot.1) | copy-start | bytes 6148
  44.9 15.7 %all-to-all-start = ((f32[16,32,128]{2,1,0:T(8,128)}), f32[16,32,128]{2,1,0:T(8,128)S(1)}, u32[]{:S(2)}, u32[]{:S(2)}) async-start(f32[16,32,128]{2,1,0:T(8,128)} %get-tuple-element.26), calls=%async_computation | async-start | bytes 524288 | tf_op jit(solution)/shard_map/all_to_all | solution.py:362
  51.2 3.1 %collective-permute-start.17 = (f32[1,512]{1,0:T(1,128)S(1)}, f32[1,512]{1,0:T(1,128)S(1)}, u32[]{:S(2)}, u32[]{:S(2)}) collective-permute-start(f32[1,512]{1,0:T(1,128)S(1)} %get-tuple-element.27), channel_id=1, source_target_pairs={{0,96},{1,97},{2,66},{3,67},{4,100},{5,101},{6,70},{7,71},{8,104},... | collective-permute-start | bytes 6152 | tf_op jit(solution)/shard_map/ppermute | solution.py:304
  64.8 6.7 %collective-permute-start.18 = (f32[1,1024]{1,0:T(1,128)S(1)}, f32[1,1024]{1,0:T(1,128)S(1)}, u32[]{:S(2)}, u32[]{:S(2)}) collective-permute-start(f32[1,1024]{1,0:T(1,128)S(1)} %get-tuple-element.32), channel_id=1, source_target_pairs={{0,32},{1,33},{2,2},{3,3},{4,36},{5,37},{6,6},{7,7},{8,40},{9,41},... | collective-permute-start | bytes 12296 | tf_op jit(solution)/shard_map/ppermute | solution.py:304
  66.7 4.8 %collective-permute-start.19 = (f32[1,1024]{1,0:T(1,128)S(1)}, f32[1,1024]{1,0:T(1,128)S(1)}, u32[]{:S(2)}, u32[]{:S(2)}) collective-permute-start(f32[1,1024]{1,0:T(1,128)S(1)} %get-tuple-element.32), channel_id=1, source_target_pairs={{0,33},{1,32},{2,3},{3,2},{4,37},{5,36},{6,7},{7,6},{8,41},{9,40},... | collective-permute-start | bytes 12296 | tf_op jit(solution)/shard_map/ppermute | solution.py:304
  69.0 3.0 %collective-permute-start.20 = (f32[1,1024]{1,0:T(1,128)S(1)}, f32[1,1024]{1,0:T(1,128)S(1)}, u32[]{:S(2)}, u32[]{:S(2)}) collective-permute-start(f32[1,1024]{1,0:T(1,128)S(1)} %get-tuple-element.32), channel_id=1, source_target_pairs={{0,2},{1,3},{2,32},{3,33},{4,6},{5,7},{6,36},{7,37},{8,10},{9,11},... | collective-permute-start | bytes 12296 | tf_op jit(solution)/shard_map/ppermute | solution.py:304
  69.0 5.4 %collective-permute-start.21 = (f32[1,1024]{1,0:T(1,128)S(1)}, f32[1,1024]{1,0:T(1,128)S(1)}, u32[]{:S(2)}, u32[]{:S(2)}) collective-permute-start(f32[1,1024]{1,0:T(1,128)S(1)} %get-tuple-element.32), channel_id=1, source_target_pairs={{0,3},{1,2},{2,33},{3,32},{4,7},{5,6},{6,37},{7,36},{8,11},{9,10},... | collective-permute-start | bytes 12296 | tf_op jit(solution)/shard_map/ppermute | solution.py:304

commit v5 on v4

--- a/solution.py
+++ b/solution.py
@@ -156,11 +156,8 @@
     target[dims:, :] = jnp.where(first, jnp.broadcast_to(other_pot[...], (8, n)), own[dims:, :])
 
 
-def join_kernel(place, own, other, out):
-    half = own.shape[1]
-    first = place[5] == 0
-    out[:, 0:half] = jnp.where(first, own[...], other[...])
-    out[:, half:] = jnp.where(first, other[...], own[...])
+def spread_kernel(part, out):
+    out[...] = jnp.broadcast_to(part[...][None], out.shape)
 
 
 def order_kernel(place, own, other, out, operand):
@@ -172,21 +169,21 @@
     operand[...] = jnp.transpose(row_side(out[0:dims, :], jnp.zeros((1, 2 * n), F32)))
 
 
-def first_kernel(place, rows, *rest):
-    *ins, out, one, two, top, total = rest
-    cols, so_far = ins[:DEPTHS], ins[DEPTHS:]
-    dims = cols[0].shape[0] - 8
+def first_kernel(place, rows, cols, *rest):
+    *so_far, out, one, two, top, total = rest
+    blocks, tall, width = cols.shape
+    dims = tall - 8
 
     @pl.when(place[0] == 0)
     def _():
         def chunk(k):
             parts = []
-            for c in cols[2 * k : 2 * k + 2]:
-                x = c[0:dims, :]
-                parts.append(col_side(x, (c[dims : dims + 1, :] - square(x)) * LOG2E))
+            for i in range(4 * k, 4 * k + 4):
+                x = cols[i, 0:dims, :]
+                parts.append(col_side(x, (cols[i, dims : dims + 1, :] - square(x)) * LOG2E))
             return jnp.concatenate(parts, axis=1)
 
-        line = over_columns(rows[...], chunk, DEPTHS // 2, 2 * cols[0].shape[1], (one, two), top, total)
+        line = over_columns(rows[...], chunk, blocks // 4, 4 * width, (one, two), top, total)
         out[...] = lse2([line] + [s[...] for s in so_far])
 
     @pl.when(place[0] != 0)
@@ -194,20 +191,20 @@
         out[...] = jnp.zeros(out.shape, F32)
 
 
-def split_kernel(place, *refs):
-    *cols, out, extra = refs
-    dims = cols[0].shape[0] - 8
+def split_kernel(place, near, far, out, extra):
+    blocks, tall, _ = near.shape
+    dims = tall - 8
 
     @pl.when(place[0] != 0)
     def _():
-        for k, c in enumerate(cols):
-            depth = lax.rem(place[4] + DEPTHS - k % DEPTHS, DEPTHS)
-            at = 2 * depth + lax.rem(place[1] + k // DEPTHS, 2)
-            x = c[0:dims, :]
-            high, low = halves(x)
-            out[at, :, :] = jnp.concatenate([high, low, high], axis=0)
-            extra[at, 0:1, :] = square(x)
-            extra[at, 1:2, :] = c[dims : dims + 1, :]
+        for cols, side in ((near, place[1]), (far, 1 - place[1])):
+            for i in range(blocks):
+                at = side * blocks + i
+                x = cols[i, 0:dims, :]
+                high, low = halves(x)
+                out[at, :, :] = jnp.concatenate([high, low, high], axis=0)
+                extra[at, 0:1, :] = square(x)
+                extra[at, 1:2, :] = cols[i, dims : dims + 1, :]
 
 
 def second_kernel(offset, place, rows, cols, *rest):
@@ -231,13 +228,13 @@
         no_bias = bias_rows(0, jnp.zeros((1, width), F32), width)
 
         def chunk(k):
-            return jnp.concatenate([cols[k], no_bias], axis=0)
-
-        lines = over_rows(rows_t, chunk, blocks, width, (one, two))
+            return jnp.concatenate([jnp.concatenate([cols[i], no_bias], axis=0) for i in (2 * k, 2 * k + 1)], axis=1)
+
+        lines = over_rows(rows_t, chunk, blocks // 2, 2 * width, (one, two))
         out[...] = jnp.broadcast_to(jnp.concatenate(lines, axis=0)[None], out.shape)
 
 
-def third_kernel(offset, place, rows, cols, extra, came, belief, out, one, two, top, total, seen, final):
+def third_kernel(offset, place, rows, cols, extra, came, before, belief, out, one, two, top, total, seen, final):
     blocks, _, width = cols.shape
     some = width // LANES
 
@@ -252,7 +249,7 @@
 
         def chunk(k):
             parts = []
-            for i in (2 * k, 2 * k + 1):
+            for i in range(4 * k, 4 * k + 4):
                 line = jnp.concatenate([seen[some * i + q : some * i + q + 1, :] for q in range(some)], axis=1)
                 x2 = extra[i, 0:1, :]
                 b = line - x2 + extra[i, 1:2, :]
@@ -260,20 +257,23 @@
                 parts.append(jnp.concatenate([cols[i], bias_rows(0, (b - x2) * LOG2E, width)], axis=0))
             return jnp.concatenate(parts, axis=1)
 
-        out[...] = over_columns(rows[...], chunk, blocks // 2, 2 * width, (one, two), top, total)
-        half = width // 2
-        for side in (0, 1):
-            line = final[pl.ds(2 * place[4] + side, 1), :]
-            belief[:, side * half : (side + 1) * half] = jnp.where(place[5] == 0, line[:, 0:half], line[:, half:])
-
-
-def last_kernel(place, pot, base, belief1, belief2, *rest):
+        wide = rows.shape[0]
+        out[:, 0:wide] = over_columns(rows[...], chunk, blocks // 4, 4 * width, (one, two), top, total)
+        out[:, wide:] = before[...]
+        own = 2 * place[4] + place[5]
+        belief[:, 0:width] = final[pl.ds(own, 1), :]
+        belief[:, width:] = final[pl.ds(own + blocks // 2, 1), :]
+
+
+def last_kernel(place, pot, base, belief2, *rest):
     *came, out = rest
     here = 2 * place[0] + place[1]
     n = pot.shape[1]
-    line = lse2([c[...] for c in came]) * LN2
+    wide = 2 * n
+    line = lse2([c[:, 0:wide] for c in came]) * LN2
+    belief1 = came[0][:, wide:]
     end = jnp.where(place[2] == 0, line[:, 0:n], line[:, n:]) + base[...]
-    out[...] = jnp.where(here == 0, pot[...], jnp.where(here == 1, belief1[...], jnp.where(here == 2, belief2[...], end)))
+    out[...] = jnp.where(here == 0, pot[...], jnp.where(here == 1, belief1, jnp.where(here == 2, belief2[...], end)))
 
 
 def device(low, core, depth, far, near, high):
@@ -329,30 +329,30 @@
         sent(target, lambda l, c, z, f, y, h: (l, y, z, f, c, h)),
         sent(target, lambda l, c, z, f, y, h: (l, y, z, f, c, 1 - h)),
     ]
-    joined = call(join_kernel, "join", arr(tall, n), 3)(
-        place, half, sent(half, lambda l, c, z, f, y, h: (l, c, z, 1 - f, y, h))
-    )
-    near = [joined] + [
-        sent(joined, lambda l, c, z, f, y, h, d=d: (l, c, (z + d) % DEPTHS, f, y, h)) for d in range(1, DEPTHS)
-    ]
+    copies = pl.pallas_call(
+        spread_kernel, out_shape=arr(PLACES, tall, n // 2), compiler_params=params(), name="spread"
+    )(half)
     rows, operand = call(order_kernel, "order", [arr(tall, 2 * n), arr(2 * n, 4 * dims, dtype=BF16)], 3)(place, *sides)
+    copies, rows, operand = lax.optimization_barrier((copies, rows, operand))
+    corners = [[p * 4 + k for p in range(PLACES)] for k in range(4)]
+    near = lax.all_to_all(copies, "cell", 0, 0, axis_index_groups=corners, tiled=True)
+    near, rows = lax.optimization_barrier((near, rows))
     rows1 = sent(rows, lambda l, c, z, f, y, h: (1 - l, c, z, f, y, h))
-    far = [swapped(x) for x in near]
+    far = swapped(near)
 
     bufs = [pltpu.VMEM((2 * n, 2 * n), F32)] * 2
     pair = [pltpu.VMEM((2 * n, LANES), F32)] * 2
-    part = call(first_kernel, "first", arr(1, 2 * n), 6, bufs + pair)(place, operand, *near)
-    part = call(first_kernel, "first_far", arr(1, 2 * n), 7, bufs + pair)(place, operand, *far, part)
+    part = call(first_kernel, "first", arr(1, 2 * n), 3, bufs + pair)(place, operand, near)
+    part = call(first_kernel, "first_far", arr(1, 2 * n), 4, bufs + pair)(place, operand, far, part)
     parts = [
         sent(part, lambda l, c, z, f, y, h, j=j, k=k: (1 - l, c, z, f, y ^ j, h ^ k)) for j in (0, 1) for k in (0, 1)
     ]
     cols, extra = call(
-        split_kernel, "split", [arr(PLACES, 3 * dims, n, dtype=BF16), arr(PLACES, 8, n)], 1 + PLACES
-    )(place, *near, *far)
+        split_kernel, "split", [arr(2 * PLACES, 3 * dims, n // 2, dtype=BF16), arr(2 * PLACES, 8, n // 2)], 3
+    )(place, near, far)
     belief1, mine = call(
         functools.partial(second_kernel, offset), "second", [arr(1, n), arr(2 * PLACES, lines, LANES)], 7, bufs
     )(place, rows1, cols, *parts)
-    belief1 = sent(belief1, lambda l, c, z, f, y, h: (1 - l, c ^ y ^ 1, z, f, y, h))
     sixteen = [
         [device(l, c, z, f, y, h) for c in (0, 1) for z in range(DEPTHS) for f in (0, 1)]
         for l in (0, 1)
@@ -360,20 +360,22 @@
         for h in (0, 1)
     ]
     seen = lax.all_to_all(mine, ("tm", "cell"), 0, 0, axis_index_groups=sixteen, tiled=True)
-    seen, belief1 = lax.optimization_barrier((seen, belief1))
     belief2, part = call(
         functools.partial(third_kernel, offset),
         "third",
-        [arr(1, n), arr(1, 2 * n)],
-        5,
-        bufs + pair + [pltpu.VMEM((lines, LANES), F32), pltpu.VMEM((PLACES, n), F32)],
-    )(place, operand, cols, extra, seen)
-    parts = [
+        [arr(1, n), arr(1, 3 * n)],
+        6,
+        bufs + pair + [pltpu.VMEM((lines, LANES), F32), pltpu.VMEM((2 * PLACES, n // 2), F32)],
+    )(place, operand, cols, extra, seen, belief1)
+
+    def ending(l, c, z, f, y, h):
+        return (l if c == y else 1 - l, l, z, f, c, h)
+
+    parts = [sent(part, ending)] + [
         sent(part, lambda l, c, z, f, y, h, j=j, k=k: (l, c ^ y ^ j ^ 1, z, f, y ^ j, h ^ k))
-        for j in (0, 1)
-        for k in (0, 1)
+        for j, k in ((0, 1), (1, 0), (1, 1))
     ]
-    return call(last_kernel, "last", arr(1, n), 9)(place, potentials, base, belief1, belief2, *parts)
+    return call(last_kernel, "last", arr(1, n), 8)(place, potentials, base, belief2, *parts)
 
 
 def solution(mesh):

time: 76.5 us -> 80.9 us (1.058)
  blocking collectives: 0 us -> 33.9 us
  starting transfers between devices: 37.7 us -> 18.9 us
  waiting for transfers between devices: 22 us -> 13.1 us
  Pallas kernels: 13.9 us -> 12.9 us
    all_to_all x0 -> x2, blocking collectives: none -> 33.9 us  [the longest x1 21.6 us: body(): lax.all_to_all(copies, 'cell', 0, 0, axis_index_groups=corners, tiled=True)]
    ppermute x22 -> x14, starting transfers between devices: 31.5 us -> 18.9 us  [sent(): return lax.ppermute(x, ('tm', 'cell'), moves(to))]
    all_to_all x1 -> x0, waiting for transfers between devices: 6.4 us -> none  [body(): lax.all_to_all(mine, ('tm', 'cell'), 0, 0, axis_index_groups=sixteen, til...]
    all_to_all x1 -> x0, starting transfers between devices: 6.23 us -> none  [body(): lax.all_to_all(mine, ('tm', 'cell'), 0, 0, axis_index_groups=sixteen, til...]
    ppermute x22 -> x14, waiting for transfers between devices: 15.6 us -> 13.1 us  [sent(): return lax.ppermute(x, ('tm', 'cell'), moves(to))]
    pallas_call x1, Pallas kernels: 4.84 us -> 3.98 us  [body(): call(functools.partial(second_kernel, offset), 'second', [arr(1, n), arr(...]
  transfers between devices with their start and end apart: 23 -> 14, of which waited for: 10 -> 6; matrix products, arithmetic and copies ran while one was open for 0% -> 0% of each run, Pallas kernels for 4% -> 2%
where the time goes in v5:
time: 80.9 us; the launch traced here: 80.7 us
  blocking collectives  33.9 us (42%)
  starting transfers between devices  18.9 us (23%)
  waiting for transfers between devices  13.1 us (16%)
  Pallas kernels  12.9 us (16%)
  local copies, waits for them, and re-layouts  1.68 us (2%)
    all_to_all x1, blocking collectives, body(): lax.all_to_all(copies, 'cell', 0, 0, axis_index_groups=corners, tiled=True)  21.6 us
    ppermute x14, starting transfers between devices, sent(): return lax.ppermute(x, ('tm', 'cell'), moves(to))  18.9 us
    ppermute x14, waiting for transfers between devices, sent(): return lax.ppermute(x, ('tm', 'cell'), moves(to))  13.1 us
    all_to_all x1, blocking collectives, body(): lax.all_to_all(mine, ('tm', 'cell'), 0, 0, axis_index_groups=sixteen, til...  12.3 us
    pallas_call x1, Pallas kernels, body(): call(functools.partial(third_kernel, offset), 'third', [arr(1, n), arr(1,...  4.46 us
    pallas_call x1, Pallas kernels, body(): call(functools.partial(second_kernel, offset), 'second', [arr(1, n), arr(...  3.98 us
  transfers between devices with their start and end apart: 14, of which 6 were waited for; matrix products, arithmetic and copies ran while one was open for 0% of the time, Pallas kernels for 2%

profile of v5, /device:TPU:2, one launch (start us, length us, event | category | flops | bytes accessed | tf_op | source)
XLA Modules:
  0.0 80.7 jit_solution(15690431790187808751)
XLA Ops:
  0.0 0.0 collective-permute-start
  0.0 0.5 collective-permute-start.1
  0.5 0.0 copy-start
  0.5 0.9 %copy-done = f32[1,64,512]{2,1,0:T(8,128)S(1)} copy-done((f32[1,64,512]{2,1,0:T(8,128)S(1)}, f32[1,64,512]{2,1,0:T(8,128)}, u32[]{:S(2)}) %copy-start) | copy-done | bytes 131096
  1.4 0.0 copy-start.1
  1.4 0.7 copy-done.1
  2.2 0.1 stack.27.place
  2.3 0.0 collective-permute-done.1.other_pot
  2.3 0.0 collective-permute-done.other
  2.3 0.6 pick.1
  2.9 2.2 %collective-permute-start.3 = (f32[72,512]{1,0:T(8,128)S(1)}, f32[72,512]{1,0:T(8,128)S(1)}, u32[]{:S(2)}, u32[]{:S(2)}) collective-permute-start(f32[72,512]{1,0:T(8,128)S(1)} %get-tuple-element.25), channel_id=1, source_target_pairs={{0,1},{1,0},{2,33},{3,32},{4,5},{5,4},{6,37},{7,36},{8,9},{9,8},{1... | collective-permute-start | bytes 442376 | tf_op jit(solution)/shard_map/ppermute | solution.py:304
  5.1 0.7 collective-permute-start.2
  5.8 5.0 %collective-permute-done.3.other = f32[72,512]{1,0:T(8,128)S(1)} collective-permute-done((f32[72,512]{1,0:T(8,128)S(1)}, f32[72,512]{1,0:T(8,128)S(1)}, u32[]{:S(2)}, u32[]{:S(2)}) %collective-permute-start.3) | collective-permute-done | bytes 147488 | tf_op jit(solution)/shard_map/ppermute | solution.py:304
  10.8 0.0 collective-permute-done.2.own
  10.8 0.7 order.1
  11.6 21.6 %all_to_all.10.near.cols = f32[8,72,256]{2,1,0:T(8,128)S(1)} all-to-all(f32[8,72,256]{2,1,0:T(8,128)S(1)} %spread.1), channel_id=1, replica_groups={{0,4,8,12,16,20,24,28},{1,5,9,13,17,21,25,29},{2,6,10,14,18,22,26,30},{..., dimensions={0} | all-to-all | bytes 1179648 | tf_op jit(solution)/shard_map/all_to_all | solution.py:338
  33.2 0.1 collective-permute-start.4
  33.3 0.4 collective-permute-start.5
  33.7 0.6 first.1.rest_0_
  34.3 0.9 %collective-permute-done.4.far.cols = f32[8,72,256]{2,1,0:T(8,128)S(1)} collective-permute-done((f32[8,72,256]{2,1,0:T(8,128)S(1)}, f32[8,72,256]{2,1,0:T(8,128)S(1)}, u32[]{:S(2)}, u32[]{:S(2)}) %collective-permute-start.4) | collective-permute-done | bytes 589856 | tf_op jit(solution)/shard_map/ppermute | solution.py:304
  35.2 0.6 first_far.1
  35.7 3.5 %collective-permute-start.9 = (f32[1,1024]{1,0:T(1,128)S(1)}, f32[1,1024]{1,0:T(1,128)S(1)}, u32[]{:S(2)}, u32[]{:S(2)}) collective-permute-start(f32[1,1024]{1,0:T(1,128)S(1)} %first_far.1), channel_id=1, source_target_pairs={{0,67},{1,66},{2,65},{3,64},{4,71},{5,70},{6,69},{7,68},{8,75},{9,... | collective-permute-start | bytes 12296 | tf_op jit(solution)/shard_map/ppermute | solution.py:304
  39.2 0.9 %collective-permute-start.8 = (f32[1,1024]{1,0:T(1,128)S(1)}, f32[1,1024]{1,0:T(1,128)S(1)}, u32[]{:S(2)}, u32[]{:S(2)}) collective-permute-start(f32[1,1024]{1,0:T(1,128)S(1)} %first_far.1), channel_id=1, source_target_pairs={{0,66},{1,67},{2,64},{3,65},{4,70},{5,71},{6,68},{7,69},{8,74},{9,... | collective-permute-start | bytes 12296 | tf_op jit(solution)/shard_map/ppermute | solution.py:304
  40.1 4.1 %collective-permute-start.7 = (f32[1,1024]{1,0:T(1,128)S(1)}, f32[1,1024]{1,0:T(1,128)S(1)}, u32[]{:S(2)}, u32[]{:S(2)}) collective-permute-start(f32[1,1024]{1,0:T(1,128)S(1)} %first_far.1), channel_id=1, source_target_pairs={{0,65},{1,64},{2,67},{3,66},{4,69},{5,68},{6,71},{7,70},{8,73},{9,... | collective-permute-start | bytes 12296 | tf_op jit(solution)/shard_map/ppermute | solution.py:304
  44.2 0.1 collective-permute-start.6
  44.3 0.8 split.1
  45.1 0.0 collective-permute-done.5.rows
  45.1 0.0 collective-permute-done.9.rest_3_
  45.1 0.0 collective-permute-done.8.rest_2_
  45.1 0.7 collective-permute-done.7.rest_1_
  45.8 2.0 %collective-permute-done.6.rest_0_ = f32[1,1024]{1,0:T(1,128)S(1)} collective-permute-done((f32[1,1024]{1,0:T(1,128)S(1)}, f32[1,1024]{1,0:T(1,128)S(1)}, u32[]{:S(2)}, u32[]{:S(2)}) %collective-permute-start.6) | collective-permute-done | bytes 4128 | tf_op jit(solution)/shard_map/ppermute | solution.py:304
  47.8 4.0 %second.1 = (f32[1,512]{1,0:T(1,128)S(1)}, f32[16,32,128]{2,1,0:T(8,128)S(1)}) custom-call(s32[6]{0:T(128)S(1)} %stack.27.place, f32[72,1024]{1,0:T(8,128)S(1)} %collective-permute-done.5.rows, bf16[16,192,256]{2,1,0:T(8,128)(2,1)S(1)} %get-tuple-element.32.cols, f32[1,1024]{1,0:T(1,128)S(1)} %collective-permute-done.6.rest_0_, ...), custom_call_target="tpu_custom_call" | custom-call | tf_op jit(solution)/shard_map/second/pallas_call | solution.py:353
  51.8 0.0 copy-start.2
  51.8 12.3 %all_to_all.11.came = f32[16,32,128]{2,1,0:T(8,128)S(1)} all-to-all(f32[16,32,128]{2,1,0:T(8,128)S(1)} %get-tuple-element.35), channel_id=1, replica_groups={{0,4,8,12,16,20,24,28,32,36,40,44,48,52,56,60},{1,5,9,13,17,21,25,29,33..., dimensions={0} | all-to-all | bytes 524288 | tf_op jit(solution)/shard_map/all_to_all | solution.py:362
  64.1 4.5 %third.1 = (f32[1,512]{1,0:T(1,128)S(1)}, f32[1,1536]{1,0:T(1,128)S(1)}) custom-call(s32[6]{0:T(128)S(1)} %stack.27.place, bf16[1024,256]{1,0:T(8,128)(2,1)S(1)} %get-tuple-element.28.rows, bf16[16,192,256]{2,1,0:T(8,128)(2,1)S(1)} %get-tuple-element.32.cols, f32[16,8,256]{2,1,0:T(8,128)S(1)} %get-tuple-element.33.extra, ...), custom_call_target="tpu_custom_call" | custom-call | tf_op jit(solution)/shard_map/third/pallas_call | solution.py:363
  68.6 0.7 collective-permute-start.13
  69.3 1.6 %collective-permute-start.12 = (f32[1,1536]{1,0:T(1,128)S(1)}, f32[1,1536]{1,0:T(1,128)S(1)}, u32[]{:S(2)}, u32[]{:S(2)}) collective-permute-start(f32[1,1536]{1,0:T(1,128)S(1)} %get-tuple-element.38), channel_id=1, source_target_pairs={{0,2},{1,3},{2,32},{3,33},{4,6},{5,7},{6,36},{7,37},{8,10},{9,11},... | collective-permute-start | bytes 18440 | tf_op jit(solution)/shard_map/ppermute | solution.py:304
  70.9 2.2 %collective-permute-start.11 = (f32[1,1536]{1,0:T(1,128)S(1)}, f32[1,1536]{1,0:T(1,128)S(1)}, u32[]{:S(2)}, u32[]{:S(2)}) collective-permute-start(f32[1,1536]{1,0:T(1,128)S(1)} %get-tuple-element.38), channel_id=1, source_target_pairs={{0,33},{1,32},{2,3},{3,2},{4,37},{5,36},{6,7},{7,6},{8,41},{9,40},... | collective-permute-start | bytes 18440 | tf_op jit(solution)/shard_map/ppermute | solution.py:304
  73.1 1.9 %collective-permute-start.10 = (f32[1,1536]{1,0:T(1,128)S(1)}, f32[1,1536]{1,0:T(1,128)S(1)}, u32[]{:S(2)}, u32[]{:S(2)}) collective-permute-start(f32[1,1536]{1,0:T(1,128)S(1)} %get-tuple-element.38), channel_id=1, source_target_pairs={{0,0},{1,1},{2,64},{3,65},{4,4},{5,5},{6,68},{7,69},{8,8},{9,9},{1... | collective-permute-start | bytes 18440 | tf_op jit(solution)/shard_map/ppermute | solution.py:304
  75.0 0.0 collective-permute-done.13.rest_3_
  75.0 0.0 collective-permute-done.12.rest_2_
  75.0 0.4 collective-permute-done.11.rest_1_
  75.4 4.1 %collective-permute-done.10.rest_0_ = f32[1,1536]{1,0:T(1,128)S(1)} collective-permute-done((f32[1,1536]{1,0:T(1,128)S(1)}, f32[1,1536]{1,0:T(1,128)S(1)}, u32[]{:S(2)}, u32[]{:S(2)}) %collective-permute-start.10) | collective-permute-done | bytes 6176 | tf_op jit(solution)/shard_map/ppermute | solution.py:304
  79.5 0.0 copy-done.2
  79.5 1.1 %last.1 = f32[1,512]{1,0:T(1,128)} custom-call(s32[6]{0:T(128)S(1)} %stack.27.place, f32[1,512]{1,0:T(1,128)S(1)} %copy-done.2, f32[1,512]{1,0:T(1,128)S(1)} %get-tuple-element.22.base, f32[1,512]{1,0:T(1,128)S(1)} %get-tuple-element.37.belief2, f32[1,1536]{1,0:T(1,128)S(1)} %collective-permute-done.10.rest_0_, ...), custom_call_target="tpu_custom_call" | custom-call | tf_op jit(solution)/shard_map/last/pallas_call | solution.py:378
  (2 shorter events, 0.1 us)
Async XLA Ops:
  0.0 2.3 %collective-permute-start = (f32[1,64,512]{2,1,0:T(8,128)}, f32[1,64,512]{2,1,0:T(8,128)S(1)}, u32[]{:S(2)}, u32[]{:S(2)}) collective-permute-start(f32[1,64,512]{2,1,0:T(8,128)} %own.1), channel_id=1, source_target_pairs={{0,32},{1,33},{2,34},{3,35},{4,36},{5,37},{6,38},{7,39},{8,40},{9,... | collective-permute-start | bytes 393224 | tf_op jit(solution)/shard_map/ppermute | solution.py:304
  0.0 2.3 %collective-permute-start.1 = (f32[1,512]{1,0:T(1,128)}, f32[1,512]{1,0:T(1,128)S(1)}, u32[]{:S(2)}, u32[]{:S(2)}) collective-permute-start(f32[1,512]{1,0:T(1,128)} %pot.1), channel_id=1, source_target_pairs={{0,32},{1,33},{2,34},{3,35},{4,36},{5,37},{6,38},{7,39},{8,40},{9,... | collective-permute-start | bytes 6152 | tf_op jit(solution)/shard_map/ppermute | solution.py:304
  0.5 0.9 %copy-start = (f32[1,64,512]{2,1,0:T(8,128)S(1)}, f32[1,64,512]{2,1,0:T(8,128)}, u32[]{:S(2)}) copy-start(f32[1,64,512]{2,1,0:T(8,128)} %own.1) | copy-start | bytes 393220
  1.4 0.7 copy-start.1
  2.9 8.0 %collective-permute-start.3 = (f32[72,512]{1,0:T(8,128)S(1)}, f32[72,512]{1,0:T(8,128)S(1)}, u32[]{:S(2)}, u32[]{:S(2)}) collective-permute-start(f32[72,512]{1,0:T(8,128)S(1)} %get-tuple-element.25), channel_id=1, source_target_pairs={{0,1},{1,0},{2,33},{3,32},{4,5},{5,4},{6,37},{7,36},{8,9},{9,8},{1... | collective-permute-start | bytes 442376 | tf_op jit(solution)/shard_map/ppermute | solution.py:304
  5.1 5.7 %collective-permute-start.2 = (f32[72,512]{1,0:T(8,128)S(1)}, f32[72,512]{1,0:T(8,128)S(1)}, u32[]{:S(2)}, u32[]{:S(2)}) collective-permute-start(f32[72,512]{1,0:T(8,128)S(1)} %get-tuple-element.25), channel_id=1, source_target_pairs={{0,0},{1,1},{2,32},{3,33},{4,4},{5,5},{6,36},{7,37},{8,8},{9,9},{1... | collective-permute-start | bytes 442376 | tf_op jit(solution)/shard_map/ppermute | solution.py:304
  33.2 2.0 %collective-permute-start.4 = (f32[8,72,256]{2,1,0:T(8,128)S(1)}, f32[8,72,256]{2,1,0:T(8,128)S(1)}, u32[]{:S(2)}, u32[]{:S(2)}) collective-permute-start(f32[8,72,256]{2,1,0:T(8,128)S(1)} %all_to_all.10.near.cols), channel_id=1, source_target_pairs={{0,32},{1,33},{2,34},{3,35},{4,36},{5,37},{6,38},{7,39},{8,40},{9,... | collective-permute-start | bytes 1769480 | tf_op jit(solution)/shard_map/ppermute | solution.py:304
  33.3 11.8 %collective-permute-start.5 = (f32[72,1024]{1,0:T(8,128)S(1)}, f32[72,1024]{1,0:T(8,128)S(1)}, u32[]{:S(2)}, u32[]{:S(2)}) collective-permute-start(f32[72,1024]{1,0:T(8,128)S(1)} %get-tuple-element.34), channel_id=1, source_target_pairs={{0,64},{1,65},{2,66},{3,67},{4,68},{5,69},{6,70},{7,71},{8,72},{9,... | collective-permute-start | bytes 884744 | tf_op jit(solution)/shard_map/ppermute | solution.py:304
  35.7 9.4 %collective-permute-start.9 = (f32[1,1024]{1,0:T(1,128)S(1)}, f32[1,1024]{1,0:T(1,128)S(1)}, u32[]{:S(2)}, u32[]{:S(2)}) collective-permute-start(f32[1,1024]{1,0:T(1,128)S(1)} %first_far.1), channel_id=1, source_target_pairs={{0,67},{1,66},{2,65},{3,64},{4,71},{5,70},{6,69},{7,68},{8,75},{9,... | collective-permute-start | bytes 12296 | tf_op jit(solution)/shard_map/ppermute | solution.py:304
  39.2 5.9 %collective-permute-start.8 = (f32[1,1024]{1,0:T(1,128)S(1)}, f32[1,1024]{1,0:T(1,128)S(1)}, u32[]{:S(2)}, u32[]{:S(2)}) collective-permute-start(f32[1,1024]{1,0:T(1,128)S(1)} %first_far.1), channel_id=1, source_target_pairs={{0,66},{1,67},{2,64},{3,65},{4,70},{5,71},{6,68},{7,69},{8,74},{9,... | collective-permute-start | bytes 12296 | tf_op jit(solution)/shard_map/ppermute | solution.py:304
  40.1 5.7 %collective-permute-start.7 = (f32[1,1024]{1,0:T(1,128)S(1)}, f32[1,1024]{1,0:T(1,128)S(1)}, u32[]{:S(2)}, u32[]{:S(2)}) collective-permute-start(f32[1,1024]{1,0:T(1,128)S(1)} %first_far.1), channel_id=1, source_target_pairs={{0,65},{1,64},{2,67},{3,66},{4,69},{5,68},{6,71},{7,70},{8,73},{9,... | collective-permute-start | bytes 12296 | tf_op jit(solution)/shard_map/ppermute | solution.py:304
  44.2 3.6 %collective-permute-start.6 = (f32[1,1024]{1,0:T(1,128)S(1)}, f32[1,1024]{1,0:T(1,128)S(1)}, u32[]{:S(2)}, u32[]{:S(2)}) collective-permute-start(f32[1,1024]{1,0:T(1,128)S(1)} %first_far.1), channel_id=1, source_target_pairs={{0,64},{1,65},{2,66},{3,67},{4,68},{5,69},{6,70},{7,71},{8,72},{9,... | collective-permute-start | bytes 12296 | tf_op jit(solution)/shard_map/ppermute | solution.py:304
  51.8 27.7 %copy-start.2 = (f32[1,512]{1,0:T(1,128)S(1)}, f32[1,512]{1,0:T(1,128)}, u32[]{:S(2)}) copy-start(f32[1,512]{1,0:T(1,128)} %pot.1) | copy-start | bytes 6148
  68.6 6.4 %collective-permute-start.13 = (f32[1,1536]{1,0:T(1,128)S(1)}, f32[1,1536]{1,0:T(1,128)S(1)}, u32[]{:S(2)}, u32[]{:S(2)}) collective-permute-start(f32[1,1536]{1,0:T(1,128)S(1)} %get-tuple-element.38), channel_id=1, source_target_pairs={{0,3},{1,2},{2,33},{3,32},{4,7},{5,6},{6,37},{7,36},{8,11},{9,10},... | collective-permute-start | bytes 18440 | tf_op jit(solution)/shard_map/ppermute | solution.py:304
  69.3 5.8 %collective-permute-start.12 = (f32[1,1536]{1,0:T(1,128)S(1)}, f32[1,1536]{1,0:T(1,128)S(1)}, u32[]{:S(2)}, u32[]{:S(2)}) collective-permute-start(f32[1,1536]{1,0:T(1,128)S(1)} %get-tuple-element.38), channel_id=1, source_target_pairs={{0,2},{1,3},{2,32},{3,33},{4,6},{5,7},{6,36},{7,37},{8,10},{9,11},... | collective-permute-start | bytes 18440 | tf_op jit(solution)/shard_map/ppermute | solution.py:304
  70.9 4.6 %collective-permute-start.11 = (f32[1,1536]{1,0:T(1,128)S(1)}, f32[1,1536]{1,0:T(1,128)S(1)}, u32[]{:S(2)}, u32[]{:S(2)}) collective-permute-start(f32[1,1536]{1,0:T(1,128)S(1)} %get-tuple-element.38), channel_id=1, source_target_pairs={{0,33},{1,32},{2,3},{3,2},{4,37},{5,36},{6,7},{7,6},{8,41},{9,40},... | collective-permute-start | bytes 18440 | tf_op jit(solution)/shard_map/ppermute | solution.py:304
  73.1 6.4 %collective-permute-start.10 = (f32[1,1536]{1,0:T(1,128)S(1)}, f32[1,1536]{1,0:T(1,128)S(1)}, u32[]{:S(2)}, u32[]{:S(2)}) collective-permute-start(f32[1,1536]{1,0:T(1,128)S(1)} %get-tuple-element.38), channel_id=1, source_target_pairs={{0,0},{1,1},{2,64},{3,65},{4,4},{5,5},{6,68},{7,69},{8,8},{9,9},{1... | collective-permute-start | bytes 18440 | tf_op jit(solution)/shard_map/ppermute | solution.py:304

commit v6 on v5

--- a/solution.py
+++ b/solution.py
@@ -234,7 +234,7 @@
         out[...] = jnp.broadcast_to(jnp.concatenate(lines, axis=0)[None], out.shape)
 
 
-def third_kernel(offset, place, rows, cols, extra, came, before, belief, out, one, two, top, total, seen, final):
+def third_kernel(offset, place, rows, cols, extra, came, belief, out, one, two, top, total, seen, final):
     blocks, _, width = cols.shape
     some = width // LANES
 
@@ -257,23 +257,19 @@
                 parts.append(jnp.concatenate([cols[i], bias_rows(0, (b - x2) * LOG2E, width)], axis=0))
             return jnp.concatenate(parts, axis=1)
 
-        wide = rows.shape[0]
-        out[:, 0:wide] = over_columns(rows[...], chunk, blocks // 4, 4 * width, (one, two), top, total)
-        out[:, wide:] = before[...]
+        out[...] = over_columns(rows[...], chunk, blocks // 4, 4 * width, (one, two), top, total)
         own = 2 * place[4] + place[5]
         belief[:, 0:width] = final[pl.ds(own, 1), :]
         belief[:, width:] = final[pl.ds(own + blocks // 2, 1), :]
 
 
-def last_kernel(place, pot, base, belief2, *rest):
+def last_kernel(place, pot, base, belief1, belief2, *rest):
     *came, out = rest
     here = 2 * place[0] + place[1]
     n = pot.shape[1]
-    wide = 2 * n
-    line = lse2([c[:, 0:wide] for c in came]) * LN2
-    belief1 = came[0][:, wide:]
+    line = lse2([c[...] for c in came]) * LN2
     end = jnp.where(place[2] == 0, line[:, 0:n], line[:, n:]) + base[...]
-    out[...] = jnp.where(here == 0, pot[...], jnp.where(here == 1, belief1, jnp.where(here == 2, belief2[...], end)))
+    out[...] = jnp.where(here == 0, pot[...], jnp.where(here == 1, belief1[...], jnp.where(here == 2, belief2[...], end)))
 
 
 def device(low, core, depth, far, near, high):
@@ -333,7 +329,6 @@
         spread_kernel, out_shape=arr(PLACES, tall, n // 2), compiler_params=params(), name="spread"
     )(half)
     rows, operand = call(order_kernel, "order", [arr(tall, 2 * n), arr(2 * n, 4 * dims, dtype=BF16)], 3)(place, *sides)
-    copies, rows, operand = lax.optimization_barrier((copies, rows, operand))
     corners = [[p * 4 + k for p in range(PLACES)] for k in range(4)]
     near = lax.all_to_all(copies, "cell", 0, 0, axis_index_groups=corners, tiled=True)
     near, rows = lax.optimization_barrier((near, rows))
@@ -360,22 +355,22 @@
         for h in (0, 1)
     ]
     seen = lax.all_to_all(mine, ("tm", "cell"), 0, 0, axis_index_groups=sixteen, tiled=True)
+    seen, belief1 = lax.optimization_barrier((seen, belief1))
+    belief1 = sent(belief1, lambda l, c, z, f, y, h: (1 - l, c ^ y ^ 1, z, f, y, h))
     belief2, part = call(
         functools.partial(third_kernel, offset),
         "third",
-        [arr(1, n), arr(1, 3 * n)],
-        6,
+        [arr(1, n), arr(1, 2 * n)],
+        5,
         bufs + pair + [pltpu.VMEM((lines, LANES), F32), pltpu.VMEM((2 * PLACES, n // 2), F32)],
-    )(place, operand, cols, extra, seen, belief1)
-
-    def ending(l, c, z, f, y, h):
-        return (l if c == y else 1 - l, l, z, f, c, h)
-
-    parts = [sent(part, ending)] + [
+    )(place, operand, cols, extra, seen)
+    part, belief1 = lax.optimization_barrier((part, belief1))
+    parts = [
         sent(part, lambda l, c, z, f, y, h, j=j, k=k: (l, c ^ y ^ j ^ 1, z, f, y ^ j, h ^ k))
-        for j, k in ((0, 1), (1, 0), (1, 1))
+        for j in (0, 1)
+        for k in (0, 1)
     ]
-    return call(last_kernel, "last", arr(1, n), 8)(place, potentials, base, belief2, *parts)
+    return call(last_kernel, "last", arr(1, n), 9)(place, potentials, base, belief1, belief2, *parts)
 
 
 def solution(mesh):

time: 80.9 us -> 72.7 us (0.90)
  blocking collectives: 33.9 us -> 13.2 us
  starting transfers between devices: 18.9 us -> 26.4 us
  waiting for transfers between devices: 13.1 us -> 16.7 us
    all_to_all x1 -> x0, blocking collectives: 21.6 us -> none  [body(): lax.all_to_all(copies, 'cell', 0, 0, axis_index_groups=corners, tiled=True)]
    all_to_all x0 -> x1, starting transfers between devices: none -> 7.94 us  [body(): lax.all_to_all(copies, 'cell', 0, 0, axis_index_groups=corners, tiled=True)]
    all_to_all x0 -> x1, waiting for transfers between devices: none -> 6.79 us  [body(): lax.all_to_all(copies, 'cell', 0, 0, axis_index_groups=corners, tiled=True)]
    ppermute x14 -> x15, waiting for transfers between devices: 13.1 us -> 9.9 us  [sent(): return lax.ppermute(x, ('tm', 'cell'), moves(to))]
    all_to_all x1, blocking collectives: 12.3 us -> 13.2 us  [body(): lax.all_to_all(mine, ('tm', 'cell'), 0, 0, axis_index_groups=sixteen, til...]
    pallas_call x1, Pallas kernels: 0.04 us -> 0.88 us  [body(): pl.pallas_call(spread_kernel, out_shape=arr(PLACES, tall, n // 2), compil...]
    ppermute x14 -> x15, starting transfers between devices: 18.9 us -> 18.4 us  [sent(): return lax.ppermute(x, ('tm', 'cell'), moves(to))]
  transfers between devices with their start and end apart: 14 -> 16, of which waited for: 6 -> 7; matrix products, arithmetic and copies ran while one was open for 0% -> 0% of each run, Pallas kernels for 2% -> 10%
where the time goes in v6:
time: 72.7 us; the launch traced here: 71.8 us
  starting transfers between devices  26.4 us (36%)
  waiting for transfers between devices  16.7 us (23%)
  Pallas kernels  13.6 us (19%)
  blocking collectives  13.2 us (18%)
  local copies, waits for them, and re-layouts  1.68 us (2%)
    ppermute x15, starting transfers between devices, sent(): return lax.ppermute(x, ('tm', 'cell'), moves(to))  18.4 us
    all_to_all x1, blocking collectives, body(): lax.all_to_all(mine, ('tm', 'cell'), 0, 0, axis_index_groups=sixteen, til...  13.2 us
    ppermute x15, waiting for transfers between devices, sent(): return lax.ppermute(x, ('tm', 'cell'), moves(to))  9.9 us
    all_to_all x1, starting transfers between devices, body(): lax.all_to_all(copies, 'cell', 0, 0, axis_index_groups=corners, tiled=True)  7.94 us
    all_to_all x1, waiting for transfers between devices, body(): lax.all_to_all(copies, 'cell', 0, 0, axis_index_groups=corners, tiled=True)  6.79 us
    pallas_call x1, Pallas kernels, body(): call(functools.partial(third_kernel, offset), 'third', [arr(1, n), arr(1,...  4.37 us
    pallas_call x1, Pallas kernels, body(): call(functools.partial(second_kernel, offset), 'second', [arr(1, n), arr(...  3.98 us
    unnamed x6, local copies, waits for them, and re-layouts  1.59 us
  transfers between devices with their start and end apart: 16, of which 7 were waited for; matrix products, arithmetic and copies ran while one was open for 0% of the time, Pallas kernels for 10%

profile of v6, /device:TPU:2, one launch (start us, length us, event | category | flops | bytes accessed | tf_op | source)
XLA Modules:
  0.0 71.8 jit_solution(3375447362016500744)
XLA Ops:
  0.0 0.0 collective-permute-start
  0.0 0.5 collective-permute-start.1
  0.5 0.0 copy-start
  0.5 0.9 %copy-done = f32[1,64,512]{2,1,0:T(8,128)S(1)} copy-done((f32[1,64,512]{2,1,0:T(8,128)S(1)}, f32[1,64,512]{2,1,0:T(8,128)}, u32[]{:S(2)}) %copy-start) | copy-done | bytes 131096
  1.4 0.0 copy-start.1
  1.4 0.7 copy-done.1
  2.2 0.1 stack.27.place
  2.3 0.0 collective-permute-done.1.other_pot
  2.3 0.0 collective-permute-done.other
  2.3 0.6 pick.1
  2.9 0.9 %spread.1 = f32[8,72,256]{2,1,0:T(8,128)} custom-call(f32[72,256]{1,0:T(8,128)S(1)} %get-tuple-element.27.part), custom_call_target="tpu_custom_call" | custom-call | tf_op jit(solution)/shard_map/spread/pallas_call | solution.py:328
  3.7 7.9 %all-to-all-start = ((f32[8,72,256]{2,1,0:T(8,128)}), f32[8,72,256]{2,1,0:T(8,128)S(1)}, u32[]{:S(2)}, u32[]{:S(2)}) async-start(f32[8,72,256]{2,1,0:T(8,128)} %spread.1), calls=%async_computation | async-start | bytes 1179648 | tf_op jit(solution)/shard_map/all_to_all | solution.py:333
  11.7 2.1 %collective-permute-start.3 = (f32[72,512]{1,0:T(8,128)S(1)}, f32[72,512]{1,0:T(8,128)S(1)}, u32[]{:S(2)}, u32[]{:S(2)}) collective-permute-start(f32[72,512]{1,0:T(8,128)S(1)} %get-tuple-element.25), channel_id=1, source_target_pairs={{0,1},{1,0},{2,33},{3,32},{4,5},{5,4},{6,37},{7,36},{8,9},{9,8},{1... | collective-permute-start | bytes 442376 | tf_op jit(solution)/shard_map/ppermute | solution.py:300
  13.8 0.7 collective-permute-start.2
  14.5 5.0 %collective-permute-done.3.other = f32[72,512]{1,0:T(8,128)S(1)} collective-permute-done((f32[72,512]{1,0:T(8,128)S(1)}, f32[72,512]{1,0:T(8,128)S(1)}, u32[]{:S(2)}, u32[]{:S(2)}) %collective-permute-start.3) | collective-permute-done | bytes 147488 | tf_op jit(solution)/shard_map/ppermute | solution.py:300
  19.4 0.0 collective-permute-done.2.own
  19.4 0.8 %order.1 = (f32[72,1024]{1,0:T(8,128)S(1)}, bf16[1024,256]{1,0:T(8,128)(2,1)S(1)}) custom-call(s32[6]{0:T(128)S(1)} %stack.27.place, f32[72,512]{1,0:T(8,128)S(1)} %collective-permute-done.2.own, f32[72,512]{1,0:T(8,128)S(1)} %collective-permute-done.3.other), custom_call_target="tpu_custom_call" | custom-call | tf_op jit(solution)/shard_map/order/pallas_call | solution.py:331
  20.2 6.8 %all-to-all-done.near.cols = f32[8,72,256]{2,1,0:T(8,128)S(1)} async-done(((f32[8,72,256]{2,1,0:T(8,128)}), f32[8,72,256]{2,1,0:T(8,128)S(1)}, u32[]{:S(2)}, u32[]{:S(2)}) %all-to-all-start) | async-done | bytes 589856 | tf_op jit(solution)/shard_map/all_to_all | solution.py:333
  27.0 0.0 collective-permute-start.4
  27.0 0.4 collective-permute-start.5
  27.4 0.6 first.1.rest_0_
  27.9 1.1 %collective-permute-done.4.far.cols = f32[8,72,256]{2,1,0:T(8,128)S(1)} collective-permute-done((f32[8,72,256]{2,1,0:T(8,128)S(1)}, f32[8,72,256]{2,1,0:T(8,128)S(1)}, u32[]{:S(2)}, u32[]{:S(2)}) %collective-permute-start.4) | collective-permute-done | bytes 589856 | tf_op jit(solution)/shard_map/ppermute | solution.py:300
  29.0 0.6 first_far.1
  29.6 4.3 %collective-permute-start.9 = (f32[1,1024]{1,0:T(1,128)S(1)}, f32[1,1024]{1,0:T(1,128)S(1)}, u32[]{:S(2)}, u32[]{:S(2)}) collective-permute-start(f32[1,1024]{1,0:T(1,128)S(1)} %first_far.1), channel_id=1, source_target_pairs={{0,67},{1,66},{2,65},{3,64},{4,71},{5,70},{6,69},{7,68},{8,75},{9,... | collective-permute-start | bytes 12296 | tf_op jit(solution)/shard_map/ppermute | solution.py:300
  33.8 0.0 collective-permute-start.8
  33.8 4.0 %collective-permute-start.7 = (f32[1,1024]{1,0:T(1,128)S(1)}, f32[1,1024]{1,0:T(1,128)S(1)}, u32[]{:S(2)}, u32[]{:S(2)}) collective-permute-start(f32[1,1024]{1,0:T(1,128)S(1)} %first_far.1), channel_id=1, source_target_pairs={{0,65},{1,64},{2,67},{3,66},{4,69},{5,68},{6,71},{7,70},{8,73},{9,... | collective-permute-start | bytes 12296 | tf_op jit(solution)/shard_map/ppermute | solution.py:300
  37.8 0.1 collective-permute-start.6
  37.9 0.8 %split.1 = (bf16[16,192,256]{2,1,0:T(8,128)(2,1)S(1)}, f32[16,8,256]{2,1,0:T(8,128)S(1)}) custom-call(s32[6]{0:T(128)S(1)} %stack.27.place, f32[8,72,256]{2,1,0:T(8,128)S(1)} %all-to-all-done.near.cols, f32[8,72,256]{2,1,0:T(8,128)S(1)} %collective-permute-done.4.far.cols), custom_call_target="tpu_custom_call" | custom-call | tf_op jit(solution)/shard_map/split/pallas_call | solution.py:345
  38.7 0.0 collective-permute-done.5.rows
  38.7 0.0 collective-permute-done.9.rest_3_
  38.7 0.0 collective-permute-done.8.rest_2_
  38.7 0.7 collective-permute-done.7.rest_1_
  39.4 2.0 %collective-permute-done.6.rest_0_ = f32[1,1024]{1,0:T(1,128)S(1)} collective-permute-done((f32[1,1024]{1,0:T(1,128)S(1)}, f32[1,1024]{1,0:T(1,128)S(1)}, u32[]{:S(2)}, u32[]{:S(2)}) %collective-permute-start.6) | collective-permute-done | bytes 4128 | tf_op jit(solution)/shard_map/ppermute | solution.py:300
  41.5 4.0 %second.1 = (f32[1,512]{1,0:T(1,128)S(1)}, f32[16,32,128]{2,1,0:T(8,128)S(1)}) custom-call(s32[6]{0:T(128)S(1)} %stack.27.place, f32[72,1024]{1,0:T(8,128)S(1)} %collective-permute-done.5.rows, bf16[16,192,256]{2,1,0:T(8,128)(2,1)S(1)} %get-tuple-element.30.cols, f32[1,1024]{1,0:T(1,128)S(1)} %collective-permute-done.6.rest_0_, ...), custom_call_target="tpu_custom_call" | custom-call | tf_op jit(solution)/shard_map/second/pallas_call | solution.py:348
  45.4 0.0 copy-start.2
  45.5 13.2 %all_to_all.10.came = f32[16,32,128]{2,1,0:T(8,128)S(1)} all-to-all(f32[16,32,128]{2,1,0:T(8,128)S(1)} %get-tuple-element.33), channel_id=1, replica_groups={{0,4,8,12,16,20,24,28,32,36,40,44,48,52,56,60},{1,5,9,13,17,21,25,29,33..., dimensions={0} | all-to-all | bytes 524288 | tf_op jit(solution)/shard_map/all_to_all | solution.py:357
  58.7 0.0 collective-permute-start.10
  58.7 4.4 %third.1 = (f32[1,512]{1,0:T(1,128)S(1)}, f32[1,1024]{1,0:T(1,128)S(1)}) custom-call(s32[6]{0:T(128)S(1)} %stack.27.place, bf16[1024,256]{1,0:T(8,128)(2,1)S(1)} %get-tuple-element.26.rows, bf16[16,192,256]{2,1,0:T(8,128)(2,1)S(1)} %get-tuple-element.30.cols, f32[16,8,256]{2,1,0:T(8,128)S(1)} %get-tuple-element.31.extra, f32[16,32,128]{2,1,0:T(8,128)S(1)} %all_to_all.10.came), custom_call_target="tpu_custom_call" | custom-call | tf_op jit(solution)/shard_map/third/pallas_call | solution.py:360
  63.0 0.0 collective-permute-done.10.belief1
  63.1 2.0 %collective-permute-start.14 = (f32[1,1024]{1,0:T(1,128)S(1)}, f32[1,1024]{1,0:T(1,128)S(1)}, u32[]{:S(2)}, u32[]{:S(2)}) collective-permute-start(f32[1,1024]{1,0:T(1,128)S(1)} %get-tuple-element.40), channel_id=1, source_target_pairs={{0,3},{1,2},{2,33},{3,32},{4,7},{5,6},{6,37},{7,36},{8,11},{9,10},... | collective-permute-start | bytes 12296 | tf_op jit(solution)/shard_map/ppermute | solution.py:300
  65.1 0.2 collective-permute-start.13
  65.3 2.2 %collective-permute-start.12 = (f32[1,1024]{1,0:T(1,128)S(1)}, f32[1,1024]{1,0:T(1,128)S(1)}, u32[]{:S(2)}, u32[]{:S(2)}) collective-permute-start(f32[1,1024]{1,0:T(1,128)S(1)} %get-tuple-element.40), channel_id=1, source_target_pairs={{0,33},{1,32},{2,3},{3,2},{4,37},{5,36},{6,7},{7,6},{8,41},{9,40},... | collective-permute-start | bytes 12296 | tf_op jit(solution)/shard_map/ppermute | solution.py:300
  67.6 1.9 %collective-permute-start.11 = (f32[1,1024]{1,0:T(1,128)S(1)}, f32[1,1024]{1,0:T(1,128)S(1)}, u32[]{:S(2)}, u32[]{:S(2)}) collective-permute-start(f32[1,1024]{1,0:T(1,128)S(1)} %get-tuple-element.40), channel_id=1, source_target_pairs={{0,32},{1,33},{2,2},{3,3},{4,36},{5,37},{6,6},{7,7},{8,40},{9,41},... | collective-permute-start | bytes 12296 | tf_op jit(solution)/shard_map/ppermute | solution.py:300
  69.5 0.0 collective-permute-done.14.rest_3_
  69.5 0.0 collective-permute-done.13.rest_2_
  69.5 0.4 collective-permute-done.12.rest_1_
  69.9 0.7 %collective-permute-done.11.rest_0_ = f32[1,1024]{1,0:T(1,128)S(1)} collective-permute-done((f32[1,1024]{1,0:T(1,128)S(1)}, f32[1,1024]{1,0:T(1,128)S(1)}, u32[]{:S(2)}, u32[]{:S(2)}) %collective-permute-start.11) | collective-permute-done | bytes 4128 | tf_op jit(solution)/shard_map/ppermute | solution.py:300
  70.6 0.0 copy-done.2
  70.6 1.1 %last.1 = f32[1,512]{1,0:T(1,128)} custom-call(s32[6]{0:T(128)S(1)} %stack.27.place, f32[1,512]{1,0:T(1,128)S(1)} %copy-done.2, f32[1,512]{1,0:T(1,128)S(1)} %get-tuple-element.23.base, f32[1,512]{1,0:T(1,128)S(1)} %collective-permute-done.10.belief1, f32[1,512]{1,0:T(1,128)S(1)} %get-tuple-element.39.belief2, ...), custom_call_target="tpu_custom_call" | custom-call | tf_op jit(solution)/shard_map/last/pallas_call | solution.py:373
  (1 shorter events, 0.0 us)
Async XLA Ops:
  0.0 2.3 %collective-permute-start = (f32[1,64,512]{2,1,0:T(8,128)}, f32[1,64,512]{2,1,0:T(8,128)S(1)}, u32[]{:S(2)}, u32[]{:S(2)}) collective-permute-start(f32[1,64,512]{2,1,0:T(8,128)} %own.1), channel_id=1, source_target_pairs={{0,32},{1,33},{2,34},{3,35},{4,36},{5,37},{6,38},{7,39},{8,40},{9,... | collective-permute-start | bytes 393224 | tf_op jit(solution)/shard_map/ppermute | solution.py:300
  0.0 2.3 %collective-permute-start.1 = (f32[1,512]{1,0:T(1,128)}, f32[1,512]{1,0:T(1,128)S(1)}, u32[]{:S(2)}, u32[]{:S(2)}) collective-permute-start(f32[1,512]{1,0:T(1,128)} %pot.1), channel_id=1, source_target_pairs={{0,32},{1,33},{2,34},{3,35},{4,36},{5,37},{6,38},{7,39},{8,40},{9,... | collective-permute-start | bytes 6152 | tf_op jit(solution)/shard_map/ppermute | solution.py:300
  0.5 0.9 %copy-start = (f32[1,64,512]{2,1,0:T(8,128)S(1)}, f32[1,64,512]{2,1,0:T(8,128)}, u32[]{:S(2)}) copy-start(f32[1,64,512]{2,1,0:T(8,128)} %own.1) | copy-start | bytes 393220
  1.4 0.7 copy-start.1
  3.7 23.3 %all-to-all-start = ((f32[8,72,256]{2,1,0:T(8,128)}), f32[8,72,256]{2,1,0:T(8,128)S(1)}, u32[]{:S(2)}, u32[]{:S(2)}) async-start(f32[8,72,256]{2,1,0:T(8,128)} %spread.1), calls=%async_computation | async-start | bytes 1179648 | tf_op jit(solution)/shard_map/all_to_all | solution.py:333
  11.7 7.8 %collective-permute-start.3 = (f32[72,512]{1,0:T(8,128)S(1)}, f32[72,512]{1,0:T(8,128)S(1)}, u32[]{:S(2)}, u32[]{:S(2)}) collective-permute-start(f32[72,512]{1,0:T(8,128)S(1)} %get-tuple-element.25), channel_id=1, source_target_pairs={{0,1},{1,0},{2,33},{3,32},{4,5},{5,4},{6,37},{7,36},{8,9},{9,8},{1... | collective-permute-start | bytes 442376 | tf_op jit(solution)/shard_map/ppermute | solution.py:300
  13.8 5.6 %collective-permute-start.2 = (f32[72,512]{1,0:T(8,128)S(1)}, f32[72,512]{1,0:T(8,128)S(1)}, u32[]{:S(2)}, u32[]{:S(2)}) collective-permute-start(f32[72,512]{1,0:T(8,128)S(1)} %get-tuple-element.25), channel_id=1, source_target_pairs={{0,0},{1,1},{2,32},{3,33},{4,4},{5,5},{6,36},{7,37},{8,8},{9,9},{1... | collective-permute-start | bytes 442376 | tf_op jit(solution)/shard_map/ppermute | solution.py:300
  27.0 2.0 %collective-permute-start.4 = (f32[8,72,256]{2,1,0:T(8,128)S(1)}, f32[8,72,256]{2,1,0:T(8,128)S(1)}, u32[]{:S(2)}, u32[]{:S(2)}) collective-permute-start(f32[8,72,256]{2,1,0:T(8,128)S(1)} %all-to-all-done.near.cols), channel_id=1, source_target_pairs={{0,32},{1,33},{2,34},{3,35},{4,36},{5,37},{6,38},{7,39},{8,40},{9,... | collective-permute-start | bytes 1769480 | tf_op jit(solution)/shard_map/ppermute | solution.py:300
  27.0 11.7 %collective-permute-start.5 = (f32[72,1024]{1,0:T(8,128)S(1)}, f32[72,1024]{1,0:T(8,128)S(1)}, u32[]{:S(2)}, u32[]{:S(2)}) collective-permute-start(f32[72,1024]{1,0:T(8,128)S(1)} %get-tuple-element.32), channel_id=1, source_target_pairs={{0,64},{1,65},{2,66},{3,67},{4,68},{5,69},{6,70},{7,71},{8,72},{9,... | collective-permute-start | bytes 884744 | tf_op jit(solution)/shard_map/ppermute | solution.py:300
  29.6 9.1 %collective-permute-start.9 = (f32[1,1024]{1,0:T(1,128)S(1)}, f32[1,1024]{1,0:T(1,128)S(1)}, u32[]{:S(2)}, u32[]{:S(2)}) collective-permute-start(f32[1,1024]{1,0:T(1,128)S(1)} %first_far.1), channel_id=1, source_target_pairs={{0,67},{1,66},{2,65},{3,64},{4,71},{5,70},{6,69},{7,68},{8,75},{9,... | collective-permute-start | bytes 12296 | tf_op jit(solution)/shard_map/ppermute | solution.py:300
  33.8 4.9 %collective-permute-start.8 = (f32[1,1024]{1,0:T(1,128)S(1)}, f32[1,1024]{1,0:T(1,128)S(1)}, u32[]{:S(2)}, u32[]{:S(2)}) collective-permute-start(f32[1,1024]{1,0:T(1,128)S(1)} %first_far.1), channel_id=1, source_target_pairs={{0,66},{1,67},{2,64},{3,65},{4,70},{5,71},{6,68},{7,69},{8,74},{9,... | collective-permute-start | bytes 12296 | tf_op jit(solution)/shard_map/ppermute | solution.py:300
  33.8 5.6 %collective-permute-start.7 = (f32[1,1024]{1,0:T(1,128)S(1)}, f32[1,1024]{1,0:T(1,128)S(1)}, u32[]{:S(2)}, u32[]{:S(2)}) collective-permute-start(f32[1,1024]{1,0:T(1,128)S(1)} %first_far.1), channel_id=1, source_target_pairs={{0,65},{1,64},{2,67},{3,66},{4,69},{5,68},{6,71},{7,70},{8,73},{9,... | collective-permute-start | bytes 12296 | tf_op jit(solution)/shard_map/ppermute | solution.py:300
  37.8 3.6 %collective-permute-start.6 = (f32[1,1024]{1,0:T(1,128)S(1)}, f32[1,1024]{1,0:T(1,128)S(1)}, u32[]{:S(2)}, u32[]{:S(2)}) collective-permute-start(f32[1,1024]{1,0:T(1,128)S(1)} %first_far.1), channel_id=1, source_target_pairs={{0,64},{1,65},{2,66},{3,67},{4,68},{5,69},{6,70},{7,71},{8,72},{9,... | collective-permute-start | bytes 12296 | tf_op jit(solution)/shard_map/ppermute | solution.py:300
  45.4 25.2 %copy-start.2 = (f32[1,512]{1,0:T(1,128)S(1)}, f32[1,512]{1,0:T(1,128)}, u32[]{:S(2)}) copy-start(f32[1,512]{1,0:T(1,128)} %pot.1) | copy-start | bytes 6148
  58.7 4.4 %collective-permute-start.10 = (f32[1,512]{1,0:T(1,128)S(1)}, f32[1,512]{1,0:T(1,128)S(1)}, u32[]{:S(2)}, u32[]{:S(2)}) collective-permute-start(f32[1,512]{1,0:T(1,128)S(1)} %get-tuple-element.37), channel_id=1, source_target_pairs={{0,96},{1,97},{2,66},{3,67},{4,100},{5,101},{6,70},{7,71},{8,104},... | collective-permute-start | bytes 6152 | tf_op jit(solution)/shard_map/ppermute | solution.py:300
  63.1 6.4 %collective-permute-start.14 = (f32[1,1024]{1,0:T(1,128)S(1)}, f32[1,1024]{1,0:T(1,128)S(1)}, u32[]{:S(2)}, u32[]{:S(2)}) collective-permute-start(f32[1,1024]{1,0:T(1,128)S(1)} %get-tuple-element.40), channel_id=1, source_target_pairs={{0,3},{1,2},{2,33},{3,32},{4,7},{5,6},{6,37},{7,36},{8,11},{9,10},... | collective-permute-start | bytes 12296 | tf_op jit(solution)/shard_map/ppermute | solution.py:300
  65.1 4.4 %collective-permute-start.13 = (f32[1,1024]{1,0:T(1,128)S(1)}, f32[1,1024]{1,0:T(1,128)S(1)}, u32[]{:S(2)}, u32[]{:S(2)}) collective-permute-start(f32[1,1024]{1,0:T(1,128)S(1)} %get-tuple-element.40), channel_id=1, source_target_pairs={{0,2},{1,3},{2,32},{3,33},{4,6},{5,7},{6,36},{7,37},{8,10},{9,11},... | collective-permute-start | bytes 12296 | tf_op jit(solution)/shard_map/ppermute | solution.py:300
  65.3 4.5 %collective-permute-start.12 = (f32[1,1024]{1,0:T(1,128)S(1)}, f32[1,1024]{1,0:T(1,128)S(1)}, u32[]{:S(2)}, u32[]{:S(2)}) collective-permute-start(f32[1,1024]{1,0:T(1,128)S(1)} %get-tuple-element.40), channel_id=1, source_target_pairs={{0,33},{1,32},{2,3},{3,2},{4,37},{5,36},{6,7},{7,6},{8,41},{9,40},... | collective-permute-start | bytes 12296 | tf_op jit(solution)/shard_map/ppermute | solution.py:300
  67.6 3.0 %collective-permute-start.11 = (f32[1,1024]{1,0:T(1,128)S(1)}, f32[1,1024]{1,0:T(1,128)S(1)}, u32[]{:S(2)}, u32[]{:S(2)}) collective-permute-start(f32[1,1024]{1,0:T(1,128)S(1)} %get-tuple-element.40), channel_id=1, source_target_pairs={{0,32},{1,33},{2,2},{3,3},{4,36},{5,37},{6,6},{7,7},{8,40},{9,41},... | collective-permute-start | bytes 12296 | tf_op jit(solution)/shard_map/ppermute | solution.py:300

commit v7 on v6

--- a/solution.py
+++ b/solution.py
@@ -96,7 +96,7 @@
     step = 32
 
     def start(k):
-        bufs[k % 2][...] = times(rows_t, col_chunk(k))
+        bufs[k % 2][:, 0:width] = times(rows_t, col_chunk(k))
 
     def finish(k):
         buf = bufs[k % 2]
@@ -178,12 +178,12 @@
     def _():
         def chunk(k):
             parts = []
-            for i in range(4 * k, 4 * k + 4):
+            for i in range(2 * k, 2 * k + 2):
                 x = cols[i, 0:dims, :]
                 parts.append(col_side(x, (cols[i, dims : dims + 1, :] - square(x)) * LOG2E))
             return jnp.concatenate(parts, axis=1)
 
-        line = over_columns(rows[...], chunk, blocks // 4, 4 * width, (one, two), top, total)
+        line = over_columns(rows[...], chunk, blocks // 2, 2 * width, (one, two), top, total)
         out[...] = lse2([line] + [s[...] for s in so_far])
 
     @pl.when(place[0] != 0)

time: 72.7 us -> 72.4 us (level)
  no operation moved by 1% of the time
where the time goes in v7:
time: 72.4 us; the launch traced here: 71.4 us
  starting transfers between devices  26.1 us (36%)
  waiting for transfers between devices  16.7 us (23%)
  Pallas kernels  13.6 us (19%)
  blocking collectives  13.2 us (18%)
  local copies, waits for them, and re-layouts  1.68 us (2%)
    ppermute x15, starting transfers between devices, sent(): return lax.ppermute(x, ('tm', 'cell'), moves(to))  18.1 us
    all_to_all x1, blocking collectives, body(): lax.all_to_all(mine, ('tm', 'cell'), 0, 0, axis_index_groups=sixteen, til...  13.2 us
    ppermute x15, waiting for transfers between devices, sent(): return lax.ppermute(x, ('tm', 'cell'), moves(to))  9.89 us
    all_to_all x1, starting transfers between devices, body(): lax.all_to_all(copies, 'cell', 0, 0, axis_index_groups=corners, tiled=True)  7.94 us
    all_to_all x1, waiting for transfers between devices, body(): lax.all_to_all(copies, 'cell', 0, 0, axis_index_groups=corners, tiled=True)  6.79 us
    pallas_call x1, Pallas kernels, body(): call(functools.partial(third_kernel, offset), 'third', [arr(1, n), arr(1,...  4.37 us
    pallas_call x1, Pallas kernels, body(): call(functools.partial(second_kernel, offset), 'second', [arr(1, n), arr(...  3.99 us
    unnamed x6, local copies, waits for them, and re-layouts  1.59 us
  transfers between devices with their start and end apart: 16, of which 7 were waited for; matrix products, arithmetic and copies ran while one was open for 0% of the time, Pallas kernels for 10%

profile of v7, /device:TPU:2, one launch (start us, length us, event | category | flops | bytes accessed | tf_op | source)
XLA Modules:
  0.0 71.4 jit_solution(13963648965118226379)
XLA Ops:
  0.0 0.0 collective-permute-start
  0.0 0.5 collective-permute-start.1
  0.5 0.0 copy-start
  0.5 0.9 %copy-done = f32[1,64,512]{2,1,0:T(8,128)S(1)} copy-done((f32[1,64,512]{2,1,0:T(8,128)S(1)}, f32[1,64,512]{2,1,0:T(8,128)}, u32[]{:S(2)}) %copy-start) | copy-done | bytes 131096
  1.4 0.0 copy-start.1
  1.4 0.7 copy-done.1
  2.2 0.1 stack.27.place
  2.3 0.0 collective-permute-done.1.other_pot
  2.3 0.0 collective-permute-done.other
  2.3 0.6 pick.1
  2.9 0.9 %spread.1 = f32[8,72,256]{2,1,0:T(8,128)} custom-call(f32[72,256]{1,0:T(8,128)S(1)} %get-tuple-element.27.part), custom_call_target="tpu_custom_call" | custom-call | tf_op jit(solution)/shard_map/spread/pallas_call | solution.py:328
  3.7 7.9 %all-to-all-start = ((f32[8,72,256]{2,1,0:T(8,128)}), f32[8,72,256]{2,1,0:T(8,128)S(1)}, u32[]{:S(2)}, u32[]{:S(2)}) async-start(f32[8,72,256]{2,1,0:T(8,128)} %spread.1), calls=%async_computation | async-start | bytes 1179648 | tf_op jit(solution)/shard_map/all_to_all | solution.py:333
  11.7 2.1 %collective-permute-start.3 = (f32[72,512]{1,0:T(8,128)S(1)}, f32[72,512]{1,0:T(8,128)S(1)}, u32[]{:S(2)}, u32[]{:S(2)}) collective-permute-start(f32[72,512]{1,0:T(8,128)S(1)} %get-tuple-element.25), channel_id=1, source_target_pairs={{0,1},{1,0},{2,33},{3,32},{4,5},{5,4},{6,37},{7,36},{8,9},{9,8},{1... | collective-permute-start | bytes 442376 | tf_op jit(solution)/shard_map/ppermute | solution.py:300
  13.8 0.7 collective-permute-start.2
  14.5 5.0 %collective-permute-done.3.other = f32[72,512]{1,0:T(8,128)S(1)} collective-permute-done((f32[72,512]{1,0:T(8,128)S(1)}, f32[72,512]{1,0:T(8,128)S(1)}, u32[]{:S(2)}, u32[]{:S(2)}) %collective-permute-start.3) | collective-permute-done | bytes 147488 | tf_op jit(solution)/shard_map/ppermute | solution.py:300
  19.4 0.0 collective-permute-done.2.own
  19.4 0.8 %order.1 = (f32[72,1024]{1,0:T(8,128)S(1)}, bf16[1024,256]{1,0:T(8,128)(2,1)S(1)}) custom-call(s32[6]{0:T(128)S(1)} %stack.27.place, f32[72,512]{1,0:T(8,128)S(1)} %collective-permute-done.2.own, f32[72,512]{1,0:T(8,128)S(1)} %collective-permute-done.3.other), custom_call_target="tpu_custom_call" | custom-call | tf_op jit(solution)/shard_map/order/pallas_call | solution.py:331
  20.2 6.8 %all-to-all-done.near.cols = f32[8,72,256]{2,1,0:T(8,128)S(1)} async-done(((f32[8,72,256]{2,1,0:T(8,128)}), f32[8,72,256]{2,1,0:T(8,128)S(1)}, u32[]{:S(2)}, u32[]{:S(2)}) %all-to-all-start) | async-done | bytes 589856 | tf_op jit(solution)/shard_map/all_to_all | solution.py:333
  27.0 0.0 collective-permute-start.4
  27.0 0.4 collective-permute-start.5
  27.4 0.6 first.1.rest_0_
  27.9 1.1 %collective-permute-done.4.far.cols = f32[8,72,256]{2,1,0:T(8,128)S(1)} collective-permute-done((f32[8,72,256]{2,1,0:T(8,128)S(1)}, f32[8,72,256]{2,1,0:T(8,128)S(1)}, u32[]{:S(2)}, u32[]{:S(2)}) %collective-permute-start.4) | collective-permute-done | bytes 589856 | tf_op jit(solution)/shard_map/ppermute | solution.py:300
  29.0 0.6 first_far.1
  29.6 3.9 %collective-permute-start.9 = (f32[1,1024]{1,0:T(1,128)S(1)}, f32[1,1024]{1,0:T(1,128)S(1)}, u32[]{:S(2)}, u32[]{:S(2)}) collective-permute-start(f32[1,1024]{1,0:T(1,128)S(1)} %first_far.1), channel_id=1, source_target_pairs={{0,67},{1,66},{2,65},{3,64},{4,71},{5,70},{6,69},{7,68},{8,75},{9,... | collective-permute-start | bytes 12296 | tf_op jit(solution)/shard_map/ppermute | solution.py:300
  33.5 0.3 collective-permute-start.8
  33.8 3.7 %collective-permute-start.7 = (f32[1,1024]{1,0:T(1,128)S(1)}, f32[1,1024]{1,0:T(1,128)S(1)}, u32[]{:S(2)}, u32[]{:S(2)}) collective-permute-start(f32[1,1024]{1,0:T(1,128)S(1)} %first_far.1), channel_id=1, source_target_pairs={{0,65},{1,64},{2,67},{3,66},{4,69},{5,68},{6,71},{7,70},{8,73},{9,... | collective-permute-start | bytes 12296 | tf_op jit(solution)/shard_map/ppermute | solution.py:300
  37.5 0.1 collective-permute-start.6
  37.6 0.8 %split.1 = (bf16[16,192,256]{2,1,0:T(8,128)(2,1)S(1)}, f32[16,8,256]{2,1,0:T(8,128)S(1)}) custom-call(s32[6]{0:T(128)S(1)} %stack.27.place, f32[8,72,256]{2,1,0:T(8,128)S(1)} %all-to-all-done.near.cols, f32[8,72,256]{2,1,0:T(8,128)S(1)} %collective-permute-done.4.far.cols), custom_call_target="tpu_custom_call" | custom-call | tf_op jit(solution)/shard_map/split/pallas_call | solution.py:345
  38.4 0.0 collective-permute-done.5.rows
  38.4 0.0 collective-permute-done.9.rest_3_
  38.4 0.0 collective-permute-done.8.rest_2_
  38.4 0.7 collective-permute-done.7.rest_1_
  39.1 2.0 %collective-permute-done.6.rest_0_ = f32[1,1024]{1,0:T(1,128)S(1)} collective-permute-done((f32[1,1024]{1,0:T(1,128)S(1)}, f32[1,1024]{1,0:T(1,128)S(1)}, u32[]{:S(2)}, u32[]{:S(2)}) %collective-permute-start.6) | collective-permute-done | bytes 4128 | tf_op jit(solution)/shard_map/ppermute | solution.py:300
  41.1 4.0 %second.1 = (f32[1,512]{1,0:T(1,128)S(1)}, f32[16,32,128]{2,1,0:T(8,128)S(1)}) custom-call(s32[6]{0:T(128)S(1)} %stack.27.place, f32[72,1024]{1,0:T(8,128)S(1)} %collective-permute-done.5.rows, bf16[16,192,256]{2,1,0:T(8,128)(2,1)S(1)} %get-tuple-element.30.cols, f32[1,1024]{1,0:T(1,128)S(1)} %collective-permute-done.6.rest_0_, ...), custom_call_target="tpu_custom_call" | custom-call | tf_op jit(solution)/shard_map/second/pallas_call | solution.py:348
  45.1 0.0 copy-start.2
  45.1 13.2 %all_to_all.10.came = f32[16,32,128]{2,1,0:T(8,128)S(1)} all-to-all(f32[16,32,128]{2,1,0:T(8,128)S(1)} %get-tuple-element.33), channel_id=1, replica_groups={{0,4,8,12,16,20,24,28,32,36,40,44,48,52,56,60},{1,5,9,13,17,21,25,29,33..., dimensions={0} | all-to-all | bytes 524288 | tf_op jit(solution)/shard_map/all_to_all | solution.py:357
  58.3 0.0 collective-permute-start.10
  58.4 4.4 %third.1 = (f32[1,512]{1,0:T(1,128)S(1)}, f32[1,1024]{1,0:T(1,128)S(1)}) custom-call(s32[6]{0:T(128)S(1)} %stack.27.place, bf16[1024,256]{1,0:T(8,128)(2,1)S(1)} %get-tuple-element.26.rows, bf16[16,192,256]{2,1,0:T(8,128)(2,1)S(1)} %get-tuple-element.30.cols, f32[16,8,256]{2,1,0:T(8,128)S(1)} %get-tuple-element.31.extra, f32[16,32,128]{2,1,0:T(8,128)S(1)} %all_to_all.10.came), custom_call_target="tpu_custom_call" | custom-call | tf_op jit(solution)/shard_map/third/pallas_call | solution.py:360
  62.7 0.0 collective-permute-done.10.belief1
  62.7 2.0 %collective-permute-start.14 = (f32[1,1024]{1,0:T(1,128)S(1)}, f32[1,1024]{1,0:T(1,128)S(1)}, u32[]{:S(2)}, u32[]{:S(2)}) collective-permute-start(f32[1,1024]{1,0:T(1,128)S(1)} %get-tuple-element.40), channel_id=1, source_target_pairs={{0,3},{1,2},{2,33},{3,32},{4,7},{5,6},{6,37},{7,36},{8,11},{9,10},... | collective-permute-start | bytes 12296 | tf_op jit(solution)/shard_map/ppermute | solution.py:300
  64.8 0.2 collective-permute-start.13
  65.0 2.2 %collective-permute-start.12 = (f32[1,1024]{1,0:T(1,128)S(1)}, f32[1,1024]{1,0:T(1,128)S(1)}, u32[]{:S(2)}, u32[]{:S(2)}) collective-permute-start(f32[1,1024]{1,0:T(1,128)S(1)} %get-tuple-element.40), channel_id=1, source_target_pairs={{0,33},{1,32},{2,3},{3,2},{4,37},{5,36},{6,7},{7,6},{8,41},{9,40},... | collective-permute-start | bytes 12296 | tf_op jit(solution)/shard_map/ppermute | solution.py:300
  67.2 1.9 %collective-permute-start.11 = (f32[1,1024]{1,0:T(1,128)S(1)}, f32[1,1024]{1,0:T(1,128)S(1)}, u32[]{:S(2)}, u32[]{:S(2)}) collective-permute-start(f32[1,1024]{1,0:T(1,128)S(1)} %get-tuple-element.40), channel_id=1, source_target_pairs={{0,32},{1,33},{2,2},{3,3},{4,36},{5,37},{6,6},{7,7},{8,40},{9,41},... | collective-permute-start | bytes 12296 | tf_op jit(solution)/shard_map/ppermute | solution.py:300
  69.2 0.0 collective-permute-done.14.rest_3_
  69.2 0.0 collective-permute-done.13.rest_2_
  69.2 0.4 collective-permute-done.12.rest_1_
  69.5 0.7 %collective-permute-done.11.rest_0_ = f32[1,1024]{1,0:T(1,128)S(1)} collective-permute-done((f32[1,1024]{1,0:T(1,128)S(1)}, f32[1,1024]{1,0:T(1,128)S(1)}, u32[]{:S(2)}, u32[]{:S(2)}) %collective-permute-start.11) | collective-permute-done | bytes 4128 | tf_op jit(solution)/shard_map/ppermute | solution.py:300
  70.3 0.0 copy-done.2
  70.3 1.1 %last.1 = f32[1,512]{1,0:T(1,128)} custom-call(s32[6]{0:T(128)S(1)} %stack.27.place, f32[1,512]{1,0:T(1,128)S(1)} %copy-done.2, f32[1,512]{1,0:T(1,128)S(1)} %get-tuple-element.23.base, f32[1,512]{1,0:T(1,128)S(1)} %collective-permute-done.10.belief1, f32[1,512]{1,0:T(1,128)S(1)} %get-tuple-element.39.belief2, ...), custom_call_target="tpu_custom_call" | custom-call | tf_op jit(solution)/shard_map/last/pallas_call | solution.py:373
  (1 shorter events, 0.0 us)
Async XLA Ops:
  0.0 2.3 %collective-permute-start = (f32[1,64,512]{2,1,0:T(8,128)}, f32[1,64,512]{2,1,0:T(8,128)S(1)}, u32[]{:S(2)}, u32[]{:S(2)}) collective-permute-start(f32[1,64,512]{2,1,0:T(8,128)} %own.1), channel_id=1, source_target_pairs={{0,32},{1,33},{2,34},{3,35},{4,36},{5,37},{6,38},{7,39},{8,40},{9,... | collective-permute-start | bytes 393224 | tf_op jit(solution)/shard_map/ppermute | solution.py:300
  0.0 2.3 %collective-permute-start.1 = (f32[1,512]{1,0:T(1,128)}, f32[1,512]{1,0:T(1,128)S(1)}, u32[]{:S(2)}, u32[]{:S(2)}) collective-permute-start(f32[1,512]{1,0:T(1,128)} %pot.1), channel_id=1, source_target_pairs={{0,32},{1,33},{2,34},{3,35},{4,36},{5,37},{6,38},{7,39},{8,40},{9,... | collective-permute-start | bytes 6152 | tf_op jit(solution)/shard_map/ppermute | solution.py:300
  0.5 0.9 %copy-start = (f32[1,64,512]{2,1,0:T(8,128)S(1)}, f32[1,64,512]{2,1,0:T(8,128)}, u32[]{:S(2)}) copy-start(f32[1,64,512]{2,1,0:T(8,128)} %own.1) | copy-start | bytes 393220
  1.4 0.7 copy-start.1
  3.7 23.3 %all-to-all-start = ((f32[8,72,256]{2,1,0:T(8,128)}), f32[8,72,256]{2,1,0:T(8,128)S(1)}, u32[]{:S(2)}, u32[]{:S(2)}) async-start(f32[8,72,256]{2,1,0:T(8,128)} %spread.1), calls=%async_computation | async-start | bytes 1179648 | tf_op jit(solution)/shard_map/all_to_all | solution.py:333
  11.7 7.8 %collective-permute-start.3 = (f32[72,512]{1,0:T(8,128)S(1)}, f32[72,512]{1,0:T(8,128)S(1)}, u32[]{:S(2)}, u32[]{:S(2)}) collective-permute-start(f32[72,512]{1,0:T(8,128)S(1)} %get-tuple-element.25), channel_id=1, source_target_pairs={{0,1},{1,0},{2,33},{3,32},{4,5},{5,4},{6,37},{7,36},{8,9},{9,8},{1... | collective-permute-start | bytes 442376 | tf_op jit(solution)/shard_map/ppermute | solution.py:300
  13.8 5.6 %collective-permute-start.2 = (f32[72,512]{1,0:T(8,128)S(1)}, f32[72,512]{1,0:T(8,128)S(1)}, u32[]{:S(2)}, u32[]{:S(2)}) collective-permute-start(f32[72,512]{1,0:T(8,128)S(1)} %get-tuple-element.25), channel_id=1, source_target_pairs={{0,0},{1,1},{2,32},{3,33},{4,4},{5,5},{6,36},{7,37},{8,8},{9,9},{1... | collective-permute-start | bytes 442376 | tf_op jit(solution)/shard_map/ppermute | solution.py:300
  27.0 2.0 %collective-permute-start.4 = (f32[8,72,256]{2,1,0:T(8,128)S(1)}, f32[8,72,256]{2,1,0:T(8,128)S(1)}, u32[]{:S(2)}, u32[]{:S(2)}) collective-permute-start(f32[8,72,256]{2,1,0:T(8,128)S(1)} %all-to-all-done.near.cols), channel_id=1, source_target_pairs={{0,32},{1,33},{2,34},{3,35},{4,36},{5,37},{6,38},{7,39},{8,40},{9,... | collective-permute-start | bytes 1769480 | tf_op jit(solution)/shard_map/ppermute | solution.py:300
  27.0 11.4 %collective-permute-start.5 = (f32[72,1024]{1,0:T(8,128)S(1)}, f32[72,1024]{1,0:T(8,128)S(1)}, u32[]{:S(2)}, u32[]{:S(2)}) collective-permute-start(f32[72,1024]{1,0:T(8,128)S(1)} %get-tuple-element.32), channel_id=1, source_target_pairs={{0,64},{1,65},{2,66},{3,67},{4,68},{5,69},{6,70},{7,71},{8,72},{9,... | collective-permute-start | bytes 884744 | tf_op jit(solution)/shard_map/ppermute | solution.py:300
  29.6 8.8 %collective-permute-start.9 = (f32[1,1024]{1,0:T(1,128)S(1)}, f32[1,1024]{1,0:T(1,128)S(1)}, u32[]{:S(2)}, u32[]{:S(2)}) collective-permute-start(f32[1,1024]{1,0:T(1,128)S(1)} %first_far.1), channel_id=1, source_target_pairs={{0,67},{1,66},{2,65},{3,64},{4,71},{5,70},{6,69},{7,68},{8,75},{9,... | collective-permute-start | bytes 12296 | tf_op jit(solution)/shard_map/ppermute | solution.py:300
  33.5 4.9 %collective-permute-start.8 = (f32[1,1024]{1,0:T(1,128)S(1)}, f32[1,1024]{1,0:T(1,128)S(1)}, u32[]{:S(2)}, u32[]{:S(2)}) collective-permute-start(f32[1,1024]{1,0:T(1,128)S(1)} %first_far.1), channel_id=1, source_target_pairs={{0,66},{1,67},{2,64},{3,65},{4,70},{5,71},{6,68},{7,69},{8,74},{9,... | collective-permute-start | bytes 12296 | tf_op jit(solution)/shard_map/ppermute | solution.py:300
  33.8 5.3 %collective-permute-start.7 = (f32[1,1024]{1,0:T(1,128)S(1)}, f32[1,1024]{1,0:T(1,128)S(1)}, u32[]{:S(2)}, u32[]{:S(2)}) collective-permute-start(f32[1,1024]{1,0:T(1,128)S(1)} %first_far.1), channel_id=1, source_target_pairs={{0,65},{1,64},{2,67},{3,66},{4,69},{5,68},{6,71},{7,70},{8,73},{9,... | collective-permute-start | bytes 12296 | tf_op jit(solution)/shard_map/ppermute | solution.py:300
  37.5 3.6 %collective-permute-start.6 = (f32[1,1024]{1,0:T(1,128)S(1)}, f32[1,1024]{1,0:T(1,128)S(1)}, u32[]{:S(2)}, u32[]{:S(2)}) collective-permute-start(f32[1,1024]{1,0:T(1,128)S(1)} %first_far.1), channel_id=1, source_target_pairs={{0,64},{1,65},{2,66},{3,67},{4,68},{5,69},{6,70},{7,71},{8,72},{9,... | collective-permute-start | bytes 12296 | tf_op jit(solution)/shard_map/ppermute | solution.py:300
  45.1 25.2 %copy-start.2 = (f32[1,512]{1,0:T(1,128)S(1)}, f32[1,512]{1,0:T(1,128)}, u32[]{:S(2)}) copy-start(f32[1,512]{1,0:T(1,128)} %pot.1) | copy-start | bytes 6148
  58.3 4.4 %collective-permute-start.10 = (f32[1,512]{1,0:T(1,128)S(1)}, f32[1,512]{1,0:T(1,128)S(1)}, u32[]{:S(2)}, u32[]{:S(2)}) collective-permute-start(f32[1,512]{1,0:T(1,128)S(1)} %get-tuple-element.37), channel_id=1, source_target_pairs={{0,96},{1,97},{2,66},{3,67},{4,100},{5,101},{6,70},{7,71},{8,104},... | collective-permute-start | bytes 6152 | tf_op jit(solution)/shard_map/ppermute | solution.py:300
  62.7 6.4 %collective-permute-start.14 = (f32[1,1024]{1,0:T(1,128)S(1)}, f32[1,1024]{1,0:T(1,128)S(1)}, u32[]{:S(2)}, u32[]{:S(2)}) collective-permute-start(f32[1,1024]{1,0:T(1,128)S(1)} %get-tuple-element.40), channel_id=1, source_target_pairs={{0,3},{1,2},{2,33},{3,32},{4,7},{5,6},{6,37},{7,36},{8,11},{9,10},... | collective-permute-start | bytes 12296 | tf_op jit(solution)/shard_map/ppermute | solution.py:300
  64.8 4.4 %collective-permute-start.13 = (f32[1,1024]{1,0:T(1,128)S(1)}, f32[1,1024]{1,0:T(1,128)S(1)}, u32[]{:S(2)}, u32[]{:S(2)}) collective-permute-start(f32[1,1024]{1,0:T(1,128)S(1)} %get-tuple-element.40), channel_id=1, source_target_pairs={{0,2},{1,3},{2,32},{3,33},{4,6},{5,7},{6,36},{7,37},{8,10},{9,11},... | collective-permute-start | bytes 12296 | tf_op jit(solution)/shard_map/ppermute | solution.py:300
  65.0 4.5 %collective-permute-start.12 = (f32[1,1024]{1,0:T(1,128)S(1)}, f32[1,1024]{1,0:T(1,128)S(1)}, u32[]{:S(2)}, u32[]{:S(2)}) collective-permute-start(f32[1,1024]{1,0:T(1,128)S(1)} %get-tuple-element.40), channel_id=1, source_target_pairs={{0,33},{1,32},{2,3},{3,2},{4,37},{5,36},{6,7},{7,6},{8,41},{9,40},... | collective-permute-start | bytes 12296 | tf_op jit(solution)/shard_map/ppermute | solution.py:300
  67.2 3.0 %collective-permute-start.11 = (f32[1,1024]{1,0:T(1,128)S(1)}, f32[1,1024]{1,0:T(1,128)S(1)}, u32[]{:S(2)}, u32[]{:S(2)}) collective-permute-start(f32[1,1024]{1,0:T(1,128)S(1)} %get-tuple-element.40), channel_id=1, source_target_pairs={{0,32},{1,33},{2,2},{3,3},{4,36},{5,37},{6,6},{7,7},{8,40},{9,41},... | collective-permute-start | bytes 12296 | tf_op jit(solution)/shard_map/ppermute | solution.py:300
